TPU v7x, 256 devices: a whole 4x4x8 slice. The times are simulated.
256 devices in a mesh: group: 32 (over x, y, core), tp: 8 (over z).
Axes of the slice: x: 4, y: 4, z: 8, core: 2. Of those that a mesh axis runs over, the one named last changes fastest.
Arguments:
- keys_cache: bfloat16 [4096, 8, 128, 128], P('group', 'tp'), may hold values from -6 to 6
- values_cache: bfloat16 [4096, 8, 128, 128], P('group', 'tp'), may hold values from -6 to 6
- lengths: int32 [4096], P('group'), may hold values from 16 to 128, as said below
- guard_flags: int32 [4096], P('group'), may hold values from 0 to 1
- migrations: int32 [832, 3], P('group'), may hold values from 0 to 127, as said below
- queries: bfloat16 [4096, 4, 4096], P('group', None, 'tp'), may hold values from -6 to 6
- new_keys: bfloat16 [4096, 4, 1024], P('group', None, 'tp'), may hold values from -6 to 6
- new_values: bfloat16 [4096, 4, 1024], P('group', None, 'tp'), may hold values from -6 to 6
- out_weight: bfloat16 [4096, 4096], P('tp'), may hold values from -0.375 to 0.375
Outputs:
- attended: bfloat16 [4096, 4, 4096], P('group', None, 'tp')
Inputs may be any that keep to these rules, and one draw needn't show every extreme that they name: `lengths`: some slot has exactly 128 positions. `migrations`: each group's list holds 26 moves. A move takes a row with guard flag 0 of its own group to a slot with guard flag 1 of another group. No two moves share a source row or a destination slot. Every group receives exactly 26 rows, and a group sends either 0 or exactly 2 rows to each other group.
All inputs are finite; a program needn't handle non-finite values.
Results may differ from a plain program's by a relative error of at most 0.0057.
Values may be sent and summed in bfloat16 or wider, within the bound.
No kernel may reach another device: no remote copies, remote signals or barrier semaphores. Data moves between devices by JAX's collectives and lax.ppermute only.
A program may use at most 128 MiB of HBM per device.

v0:
```python
import jax
import jax.numpy as jnp
from jax import lax
from jax.sharding import PartitionSpec as P

CAP = 2


def attend(queried, cached_keys, cached_values, fresh_keys, fresh_values, length):
    batch_size = queried.shape[0]
    step_count = queried.shape[1]
    kv_local = cached_keys.shape[1]
    head_width = cached_keys.shape[3]
    shaped_query = queried.reshape(batch_size, step_count, kv_local, -1, head_width)
    fresh_key_rows = fresh_keys.reshape(batch_size, step_count, kv_local, head_width)
    fresh_value_rows = fresh_values.reshape(batch_size, step_count, kv_local, head_width)
    score_scale = head_width ** (-0.5)
    cache_scores = (
        jnp.einsum(
            "btkqd,bkld->btkql", shaped_query, cached_keys, preferred_element_type=jnp.float32
        )
        * score_scale
    )
    fresh_scores = (
        jnp.einsum(
            "btkqd,bskd->btkqs", shaped_query, fresh_key_rows, preferred_element_type=jnp.float32
        )
        * score_scale
    )
    positions = jnp.arange(cached_keys.shape[2], dtype=jnp.int32)
    cache_scores = jnp.where(
        positions[None, None, None, None, :] < length[:, None, None, None, None],
        cache_scores,
        -jnp.inf,
    )
    step_ids = jnp.arange(step_count, dtype=jnp.int32)
    visible = step_ids[None, :] <= step_ids[:, None]
    fresh_scores = jnp.where(visible[None, :, None, None, :], fresh_scores, -jnp.inf)
    highest = jnp.maximum(jnp.max(cache_scores, axis=-1), jnp.max(fresh_scores, axis=-1))[..., None]
    cache_exp = jnp.exp(cache_scores - highest)
    fresh_exp = jnp.exp(fresh_scores - highest)
    denominator = jnp.sum(cache_exp, axis=-1, keepdims=True) + jnp.sum(
        fresh_exp, axis=-1, keepdims=True
    )
    cache_weight = (cache_exp / denominator).astype(jnp.bfloat16)
    fresh_weight = (fresh_exp / denominator).astype(jnp.bfloat16)
    mixture = jnp.einsum(
        "btkql,bkld->btkqd", cache_weight, cached_values, preferred_element_type=jnp.float32
    )
    mixture = mixture + jnp.einsum(
        "btkqs,bskd->btkqd", fresh_weight, fresh_value_rows, preferred_element_type=jnp.float32
    )
    return mixture.astype(jnp.bfloat16).reshape(batch_size, step_count, -1)


def on_device(
    keys_cache,
    values_cache,
    lengths,
    guard_flags,
    migrations,
    queries,
    new_keys,
    new_values,
    out_weight,
):
    slot_count = keys_cache.shape[0]
    move_count = migrations.shape[0]
    groups = lax.axis_size("group")
    own_group = lax.axis_index("group")
    every_move, every_length = (
        lax.all_gather(migrations, "group", axis=0, tiled=True),
        lax.all_gather(lengths, "group", axis=0, tiled=True),
    )
    group_ids = jnp.arange(groups, dtype=jnp.int32)
    toward = (migrations[:, 1][:, None] == group_ids[None, :]).astype(jnp.int32)
    before = jnp.cumsum(toward, axis=0) - toward
    order_in = jnp.sum(before * toward, axis=1)
    place_hit = toward[:, :, None] * (
        order_in[:, None, None] == jnp.arange(CAP, dtype=jnp.int32)[None, None, :]
    ).astype(jnp.int32)
    outgoing = jnp.sum(place_hit * migrations[:, 0][:, None, None], axis=0).reshape(-1)
    arriving = (every_move[:, 1] == own_group).astype(jnp.int32).reshape(groups, move_count)
    arrive_rank = jnp.cumsum(arriving, axis=1) - arriving
    entry_index = (group_ids[:, None] * CAP + arrive_rank).reshape(-1)
    arriving = arriving.reshape(-1)
    sender_ids = jnp.repeat(group_ids, move_count)
    source_length = every_length[sender_ids * slot_count + every_move[:, 0]]
    slot_ids = jnp.arange(slot_count, dtype=jnp.int32)
    landing = arriving[None, :] * (every_move[:, 2][None, :] == slot_ids[:, None]).astype(jnp.int32)
    received = jnp.sum(landing, axis=1) > 0
    inbound = jnp.sum(landing * entry_index[None, :], axis=1)
    arrived_length = jnp.sum(landing * source_length[None, :], axis=1)
    departed = jnp.any(migrations[:, 0][None, :] == slot_ids[:, None], axis=1)
    live_slot = (guard_flags == 0) & jnp.logical_not(departed) | received
    arrived_keys, arrived_values = (
        lax.all_to_all(keys_cache[outgoing], "group", split_axis=0, concat_axis=0, tiled=True),
        lax.all_to_all(values_cache[outgoing], "group", split_axis=0, concat_axis=0, tiled=True),
    )
    merged_keys = jnp.where(received[:, None, None, None], arrived_keys[inbound], keys_cache)
    merged_values = jnp.where(received[:, None, None, None], arrived_values[inbound], values_cache)
    new_length = jnp.where(received, arrived_length, lengths)
    head_output = attend(queries, merged_keys, merged_values, new_keys, new_values, new_length)
    partial_terms = jnp.einsum(
        "rsf,fo->rso", head_output, out_weight, preferred_element_type=jnp.float32
    )
    partial_terms = jnp.where(live_slot[:, None, None], partial_terms, 0.0)
    return lax.psum_scatter(partial_terms, "tp", scatter_dimension=2, tiled=True).astype(
        jnp.bfloat16
    )


def solution(mesh):
    return jax.shard_map(
        on_device,
        mesh=mesh,
        in_specs=(
            P("group", "tp", None, None),
            P("group", "tp", None, None),
            P("group"),
            P("group"),
            P("group", None),
            P("group", None, "tp"),
            P("group", None, "tp"),
            P("group", None, "tp"),
            P("tp", None),
        ),
        out_specs=P("group", None, "tp"),
        check_vma=False,
    )
```

profile of v0, /device:TPU:1, one launch (start us, length us, event | category | flops | bytes accessed | tf_op | source)
XLA Modules:
  0.0 251.8 jit_solution(3995286207997204688)
XLA Ops:
  6.5 0.8 slice_bitcast_fusion
  8.1 4.4 %gather_fusion.3 = bf16[64,128,128]{2,1,0:T(8,128)(2,1)} fusion(bf16[128,128,128]{2,1,0:T(8,128)(2,1)} %bitcast.138, s32[1024]{0:T(1024)S(1)} %pad_clamp_fusion.2), kind=kCustom, calls=%fused_computation.3 | custom fusion | bytes 4194560 | tf_op jit(solution)/shard_map/gather | solution.py:97
  12.4 8.7 %all-to-all-start.1 = ((bf16[64,1,128,128]{3,2,1,0:T(8,128)(2,1)}), bf16[64,1,128,128]{3,2,1,0:T(8,128)(2,1)S(1)}, u32[]{:S(2)}, u32[]{:S(2)}) async-start(bf16[64,1,128,128]{3,2,1,0:T(8,128)(2,1)} %bitcast.137), calls=%async_computation.1 | async-start | bytes 4194304 | tf_op jit(solution)/shard_map/all_to_all | solution.py:97
  21.2 43.6 %all-gather = s32[32,26,3]{1,2,0:T(4,128)S(1)} all-gather(s32[1,26,3]{1,2,0:T(4,128)S(1)} %bitcast.140), channel_id=1, replica_groups=mesh['group'=32,'tp'=8] {'group'}, dimensions={0}, use_global_device_ids=true | all-gather | bytes 10296 | tf_op jit(solution)/shard_map/all_gather | solution.py:72
  65.6 4.3 %gather_fusion = bf16[64,128,128]{2,1,0:T(8,128)(2,1)} fusion(bf16[128,128,128]{2,1,0:T(8,128)(2,1)} %bitcast.139, s32[1024]{0:T(1024)S(1)} %pad_clamp_fusion.2), kind=kCustom, calls=%fused_computation | custom fusion | bytes 4194560 | tf_op jit(solution)/shard_map/gather | solution.py:98
  70.0 19.9 %all-gather.1 = s32[32,1,128]{2,1,0:T(1,128)S(1)} all-gather(s32[1,1,128]{2,1,0:T(1,128)S(1)} %bitcast.141), channel_id=1, replica_groups=mesh['group'=32,'tp'=8] {'group'}, dimensions={0}, use_global_device_ids=true | all-gather | bytes 16896 | tf_op jit(solution)/shard_map/all_gather | solution.py:73
  89.9 4.9 %gather_fusion.2 = s32[832]{0:T(1024)S(1)} fusion(s32[4096]{0:T(1024)S(1)} %bitcast.134, s32[1024]{0:T(1024)S(1)} %pad_clamp_fusion), kind=kCustom, calls=%fused_computation.2 | custom fusion | bytes 9984 | tf_op jit(solution)/shard_map/gather | solution.py:88
  94.8 0.7 fusion.34
  96.1 5.8 %all-to-all-start = ((bf16[64,1,128,128]{3,2,1,0:T(8,128)(2,1)}), bf16[64,1,128,128]{3,2,1,0:T(8,128)(2,1)}, u32[]{:S(2)}, u32[]{:S(2)}) async-start(bf16[64,1,128,128]{3,2,1,0:T(8,128)(2,1)} %bitcast.136), calls=%async_computation | async-start | bytes 4194304 | tf_op jit(solution)/shard_map/all_to_all | solution.py:98
  101.9 0.6 iota_compare_fusion.5
  102.5 1.0 reshape.261
  104.2 5.9 %fusion.46 = (f32[128,4,4]{2,1,0:T(4,128)S(1)}, f32[128,4,1,4,4]{3,4,1,0,2:T(4,128)S(1)}) fusion(bf16[128,4,4,128]{3,2,1,0:T(4,128)(2,1)} %reshape.261, bf16[128,4,128]{2,1,0:T(4,128)(2,1)} %param.15, pred[4,4]{1,0:T(4,128)(4,1)} %iota_compare_fusion.5), kind=kOutput, calls=%fused_computation.79 | convolution fusion | flops 2119680 | bytes 696336 | tf_op jit(solution)/shard_map/btkqd,bskd->btkqs/dot_general | solution.py:25
  110.1 3.1 %gather_fusion.4 = bf16[128,128,128]{2,1,0:T(8,128)(2,1)} fusion(bf16[64,128,128]{2,1,0:T(8,128)(2,1)S(1)} %bitcast.135, s32[1024]{0:T(1024)} %pad_clamp_fusion.1), kind=kCustom, calls=%fused_computation.4 | custom fusion | bytes 8389120 | tf_op jit(solution)/shard_map/gather | solution.py:100
  113.2 6.0 %fusion.45 = (f32[128,4,4]{2,1,0:T(4,128)S(1)}, f32[128,4,1,4,128]{4,3,1,0,2:T(4,128)S(1)}) fusion(bf16[128,4,4,128]{3,2,1,0:T(4,128)(2,1)} %reshape.261, bf16[128,1,128,128]{3,2,1,0:T(8,128)(2,1)} %param.9, bf16[128,128,128]{2,1,0:T(8,128)(2,1)} %gather_fusion.4, pred[128]{0:T(512)(128)(4,1)} %get-tuple-element.13, pred[128,128]{1,0:T(8,128)(4,1)S(1)} %iota_compare_fusion.1), kind=kOutput, calls=%fused_computation.78 | convolution fusion | flops 69990400 | bytes 9986176 | tf_op jit(solution)/shard_map/btkqd,bkld->btkql/dot_general | solution.py:19
  119.3 1.0 fusion.27
  120.3 1.5 fusion.26
  121.8 8.4 %all-to-all-done = bf16[64,1,128,128]{3,2,1,0:T(8,128)(2,1)} async-done(((bf16[64,1,128,128]{3,2,1,0:T(8,128)(2,1)}), bf16[64,1,128,128]{3,2,1,0:T(8,128)(2,1)}, u32[]{:S(2)}, u32[]{:S(2)}) %all-to-all-start) | async-done | bytes 2097184 | tf_op jit(solution)/shard_map/all_to_all | solution.py:98
  130.2 4.7 %gather_fusion.1 = bf16[128,128,128]{2,1,0:T(8,128)(2,1)} fusion(bf16[64,128,128]{2,1,0:T(8,128)(2,1)} %bitcast.6, s32[1024]{0:T(1024)} %pad_clamp_fusion.1), kind=kCustom, calls=%fused_computation.1 | custom fusion | bytes 8389120 | tf_op jit(solution)/shard_map/gather | solution.py:101
  135.0 4.4 %fusion.2 = f32[128,128,4,4]{1,3,2,0:T(4,128)S(1)} fusion(bf16[128,1,128,128]{3,2,1,0:T(8,128)(2,1)} %param.10, bf16[128,128,128]{2,1,0:T(8,128)(2,1)} %gather_fusion.1, pred[128]{0:T(512)(128)(4,1)S(1)} %copy-done.6, f32[128,4,1,4,128]{4,3,1,0,2:T(4,128)S(1)} %get-tuple-element.16, f32[128,4,4]{2,1,0:T(4,128)S(1)} %add.70, f32[128,4,4]{2,1,0:T(4,128)S(1)} %max.9), kind=kOutput, calls=%fused_computation.8 | convolution fusion | flops 69992448 | bytes 10502272 | tf_op jit(solution)/shard_map/btkql,bkld->btkqd/dot_general | solution.py:47
  139.4 0.8 fusion.18
  140.5 7.8 %convolution_select_fusion = f32[128,4,4096]{2,0,1:T(8,128)} fusion(bf16[512,4096]{1,0:T(8,128)(2,1)} %param.17, pred[128]{0:T(512)(128)(4,1)S(1)} %copy-done.2, bf16[128,4,512]{2,1,0:T(4,128)(2,1)S(1)} %reshape.264), kind=kOutput, calls=%fused_computation.5 | convolution fusion | flops 2149580800 | bytes 13107328 | tf_op jit(solution)/shard_map/rsf,fo->rso/dot_general | solution.py:104
  148.3 94.2 %reduce-scatter.2.cloned.1.call-done = f32[128,4,512]{2,0,1:T(8,128)} async-done(((f32[128,4,4096]{2,0,1:T(8,128)}), f32[128,4,512]{2,0,1:T(8,128)}) %reduce-scatter.2.cloned.1.call-update) | async-done | bytes 1048592 | tf_op jit(solution)/shard_map/reduce_scatter | solution.py:108
  242.5 1.3 convert_element_type.64
  243.7 1.2 copy.29
  (48 shorter events, 3.3 us)
Async XLA Ops:
  6.5 132.9 %copy-start = (bf16[128,4,128]{2,1,0:T(4,128)(2,1)S(1)}, bf16[128,4,128]{2,1,0:T(4,128)(2,1)}, u32[]{:S(2)}) copy-start(bf16[128,4,128]{2,1,0:T(4,128)(2,1)} %param.16) | copy-start | bytes 393220
  8.0 13.1 %copy-start.3 = (s32[26,3]{0,1:T(4,128)S(1)}, s32[26,3]{0,1:T(4,128)}, u32[]{:S(2)}) copy-start(s32[26,3]{0,1:T(4,128)} %param.13) | copy-start | bytes 940
  12.4 57.5 %copy-start.4 = (s32[128]{0:T(128)S(1)}, s32[128]{0:T(128)}, u32[]{:S(2)}) copy-start(s32[128]{0:T(128)} %param.11) | copy-start | bytes 1540
  12.4 83.6 %all-to-all-start.1 = ((bf16[64,1,128,128]{3,2,1,0:T(8,128)(2,1)}), bf16[64,1,128,128]{3,2,1,0:T(8,128)(2,1)S(1)}, u32[]{:S(2)}, u32[]{:S(2)}) async-start(bf16[64,1,128,128]{3,2,1,0:T(8,128)(2,1)} %bitcast.137), calls=%async_computation.1 | async-start | bytes 4194304 | tf_op jit(solution)/shard_map/all_to_all | solution.py:97
  89.8 12.6 %copy-start.1 = (bf16[128,4,512]{2,1,0:T(4,128)(2,1)S(1)}, bf16[128,4,512]{2,1,0:T(4,128)(2,1)}, u32[]{:S(2)}) copy-start(bf16[128,4,512]{2,1,0:T(4,128)(2,1)} %param.14) | copy-start | bytes 1572868
  89.9 13.7 %copy-start.5 = (s32[128]{0:T(128)S(1)}, s32[128]{0:T(128)}, u32[]{:S(2)}) copy-start(s32[128]{0:T(128)} %param.12) | copy-start | bytes 1540
  96.1 34.1 %all-to-all-start = ((bf16[64,1,128,128]{3,2,1,0:T(8,128)(2,1)}), bf16[64,1,128,128]{3,2,1,0:T(8,128)(2,1)}, u32[]{:S(2)}, u32[]{:S(2)}) async-start(bf16[64,1,128,128]{3,2,1,0:T(8,128)(2,1)} %bitcast.136), calls=%async_computation | async-start | bytes 4194304 | tf_op jit(solution)/shard_map/all_to_all | solution.py:98
  101.8 140.6 %reduce-scatter.2.cloned.1.call-start = ((), (), s32[]{:S(2)}) async-start(), calls=%async_computation.3 | async-start | bytes 9437184 | tf_op jit(solution)/shard_map/reduce_scatter | solution.py:108
  130.2 4.8 %copy-start.6 = (pred[128]{0:T(512)(128)(4,1)S(1)}, pred[128]{0:T(512)(128)(4,1)}, u32[]{:S(2)}) copy-start(pred[128]{0:T(512)(128)(4,1)} %get-tuple-element.13) | copy-start | bytes 388
  139.4 1.1 copy-start.2
Sparse Core Ops, SparseCore 0:
  148.4 93.9 reduce-scatter.1
where the time goes:
time: 252 us
  waiting for transfers between devices  103 us (41%)
  blocking collectives  63.5 us (25%)
  local copies, waits for them, and re-layouts  25.4 us (10%)
  matrix products  24.9 us (10%)
  starting transfers between devices  14.5 us (6%)
  between operations  13.7 us (5%)
  other arithmetic  7.3 us (3%)
    reduce_scatter x1, waiting for transfers between devices, on_device(): lax.psum_scatter(partial_terms, 'tp', scatter_dimension=2, tiled=True)  94.2 us
    all_gather x1, blocking collectives, on_device(): lax.all_gather(migrations, 'group', axis=0, tiled=True)  43.6 us
    all_gather x1, blocking collectives, on_device(): lax.all_gather(lengths, 'group', axis=0, tiled=True)  19.9 us
    all_to_all x1, starting transfers between devices, on_device(): lax.all_to_all(keys_cache[outgoing], 'group', split_axis=0, concat_axis=0...  8.72 us
    all_to_all x1, waiting for transfers between devices, on_device(): lax.all_to_all(values_cache[outgoing], 'group', split_axis=0, concat_axis...  8.37 us
    dot_general x1, matrix products, on_device(): jnp.einsum('rsf,fo->rso', head_output, out_weight, preferred_element_type...  7.78 us
    dot_general x1, matrix products, attend(): jnp.einsum('btkqd,bkld->btkql', shaped_query, cached_keys, preferred_elem...  6.01 us
    dot_general x1, matrix products, attend(): jnp.einsum('btkqd,bskd->btkqs', shaped_query, fresh_key_rows, preferred_e...  5.86 us
  transfers between devices with their start and end apart: 3, of which 2 were waited for; matrix products, arithmetic and copies ran while one was open for 12% of the time, Pallas kernels for 0%

commit v1 on v0

v1 whole, which is shorter than its diff:
```python
import functools

import jax
import jax.numpy as jnp
from jax import lax
from jax.experimental import pallas as pl
from jax.experimental.pallas import tpu as pltpu
from jax.sharding import PartitionSpec as P

CAP = 2
F32, BF16, I32 = jnp.float32, jnp.bfloat16, jnp.int32
FRESH = 16
VMEM = pl.BlockSpec(memory_space=pltpu.VMEM)
SMEM = pl.BlockSpec(memory_space=pltpu.SMEM)
ANY = pl.BlockSpec(memory_space=pl.ANY)


def call(kernel, out_shape, in_specs, scratch=(), flops=0, nbytes=0, exps=0, limit=32):
    single = isinstance(out_shape, jax.ShapeDtypeStruct)
    return pl.pallas_call(
        kernel,
        out_shape=out_shape,
        in_specs=in_specs,
        out_specs=VMEM if single else [VMEM] * len(out_shape),
        scratch_shapes=list(scratch),
        cost_estimate=pl.CostEstimate(
            flops=flops, bytes_accessed=nbytes, transcendentals=exps
        ),
        compiler_params=pltpu.CompilerParams(vmem_limit_bytes=limit << 20),
    )


def table_kernel(moves_ref, table_ref):
    groups, lanes = table_ref.shape
    moves = moves_ref.shape[1]
    target = moves_ref[1:2, :]
    slot = (moves_ref[2:3, :] + 1).astype(F32)
    hit = lax.broadcasted_iota(I32, (groups, moves), 0) == target
    earlier = lax.broadcasted_iota(I32, (moves, moves), 0) < lax.broadcasted_iota(
        I32, (moves, moves), 1
    )
    before = jnp.dot(
        hit.astype(F32), earlier.astype(F32), preferred_element_type=F32
    ).astype(I32)
    lane = lax.broadcasted_iota(I32, (groups, lanes), 1)
    table = jnp.zeros((groups, lanes), I32)
    for c in range(CAP):
        entry = jnp.sum(
            jnp.where(hit & (before == c), slot, 0.0), axis=1, keepdims=True
        ).astype(I32)
        table = jnp.where(lane == c, entry, table)
    table_ref[...] = table


def payload_kernel(table_ref, query_ref, key_ref, value_ref, out_ref):
    wide, narrow = query_ref.shape[2], key_ref.shape[2]
    for e in range(out_ref.shape[0]):
        slot = jnp.maximum(table_ref[e // CAP, e % CAP] - 1, 0)
        out_ref[e, :, 0:wide] = query_ref[slot]
        out_ref[e, :, wide : wide + narrow] = key_ref[slot]
        out_ref[e, :, wide + narrow : wide + 2 * narrow] = value_ref[slot]


def fetch(keys_ref, values_ref, kbuf, vbuf, ksem, vsem, row_of, rows, batch):
    cache = keys_ref.shape[2]

    def start(i, carry):
        row = row_of(i)
        pltpu.make_async_copy(
            keys_ref.at[row, 0], kbuf.at[i, pl.ds(0, cache)], ksem.at[i // batch]
        ).start()
        pltpu.make_async_copy(
            values_ref.at[row, 0], vbuf.at[i, pl.ds(0, cache)], vsem.at[i // batch]
        ).start()
        return carry

    lax.fori_loop(0, rows, start, 0)


def await_batch(cache_ref, buf, sem, b, batch):
    cache = cache_ref.shape[2]
    pltpu.make_async_copy(
        cache_ref.at[pl.ds(0, batch), 0],
        buf.at[pl.ds(b * batch, batch), pl.ds(0, cache)],
        sem.at[b],
    ).wait()


def attend(
    rows, batch, keys_ref, values_ref, kbuf, vbuf, ksem, vsem, score, weight, query_of, fresh_of, length_of, put
):
    cache, head = keys_ref.shape[2], keys_ref.shape[3]
    positions = cache + FRESH

    def stack(value):
        heads = value.shape[1] // head
        value = value.astype(F32)
        parts = [value[:, h * head : (h + 1) * head] for h in range(heads)]
        return jnp.concatenate(parts, axis=0)

    def fresh_rows(value):
        value = value.astype(F32)
        pad = jnp.zeros((FRESH - value.shape[0], head), F32)
        return jnp.concatenate([value, pad], axis=0).astype(BF16)

    steps = query_of(0).shape[0]
    lines = query_of(0).shape[1] // head * steps

    def scores(b, carry):
        for u in range(batch):
            i = b * batch + u
            fresh_key, fresh_value = fresh_of(i)
            kbuf[i, cache:positions, :] = fresh_rows(fresh_key)
            vbuf[i, cache:positions, :] = fresh_rows(fresh_value)
        await_batch(keys_ref, kbuf, ksem, b, batch)
        lane = lax.broadcasted_iota(I32, (lines, positions), 1)
        step = lax.rem(lax.broadcasted_iota(I32, (lines, positions), 0), steps)
        visible = (lane >= cache) & (lane - cache <= step)
        for u in range(batch):
            i = b * batch + u
            products = lax.dot_general(
                stack(query_of(i)).astype(BF16),
                kbuf[i],
                (((1,), (1,)), ((), ())),
                preferred_element_type=F32,
            )
            score[pl.ds(pl.multiple_of(i * lines, lines), lines), :] = jnp.where(
                (lane < length_of(i)) | visible, products * head**-0.5, -jnp.inf
            )
        return carry

    lax.fori_loop(0, rows // batch, scores, 0)

    def soften(b, carry):
        chunk = pl.ds(pl.multiple_of(b * batch * lines, lines), batch * lines)
        s = score[chunk, :]
        e = jnp.exp(s - jnp.max(s, axis=1, keepdims=True))
        weight[chunk, :] = (e * (1.0 / jnp.sum(e, axis=1, keepdims=True))).astype(BF16)
        return carry

    lax.fori_loop(0, rows // batch, soften, 0)

    def mix(b, carry):
        await_batch(values_ref, vbuf, vsem, b, batch)
        mixed = []
        for u in range(batch):
            i = b * batch + u
            mixed.append(
                jnp.dot(
                    weight[pl.ds(pl.multiple_of(i * lines, lines), lines), :],
                    vbuf[i],
                    preferred_element_type=F32,
                )
            )
        put(b, mixed)
        return carry

    lax.fori_loop(0, rows // batch, mix, 0)


def list_staying(moves_ref, flags_ref, gone, listed):
    slots, moves = flags_ref.shape[0], moves_ref.shape[1]

    def copy(i, carry):
        gone[i] = flags_ref[i]
        listed[i] = 0
        return carry

    lax.fori_loop(0, slots, copy, 0, unroll=8)

    def leave(m, carry):
        gone[moves_ref[0, m]] = 1
        return carry

    lax.fori_loop(0, moves, leave, 0, unroll=2)

    def enter(i, count):
        listed[count] = i
        return count + jnp.where(gone[i] == 0, 1, 0)

    return lax.fori_loop(0, slots, enter, 0, unroll=8)


def staying_kernel(
    place_ref, moves_ref, flags_ref, lengths_ref, query_ref, key_ref, value_ref, keys_ref, values_ref, weight_ref,
    up_ref, down_ref, own_ref, terms_ref,
    gone, listed, kbuf, vbuf, score, weight, heads, wbuf, ksem, vsem, wsem,
):
    rows, batch = kbuf.shape[0], kbuf.shape[0] // ksem.shape[0]
    steps, head = query_ref.shape[1], keys_ref.shape[3]
    ring, columns = 8, up_ref.shape[1]
    load = pltpu.make_async_copy(weight_ref, wbuf, wsem)
    list_staying(moves_ref, flags_ref, gone, listed)
    fetch(keys_ref, values_ref, kbuf, vbuf, ksem, vsem, lambda i: listed[i], rows, batch)
    load.start()

    def put(b, mixed):
        quads = len(mixed) // 4
        for j in range(quads):
            four = mixed[4 * j : 4 * j + 4]
            for h in range(query_ref.shape[2] // head):
                tile = jnp.concatenate([o[h * steps : (h + 1) * steps] for o in four], axis=0)
                at = pl.ds(pl.multiple_of((b * quads + j) * 16, 16), 16)
                heads[at, h * head : (h + 1) * head] = tile.astype(BF16)

    attend(
        rows, batch, keys_ref, values_ref, kbuf, vbuf, ksem, vsem, score, weight,
        lambda i: query_ref[listed[i]],
        lambda i: (key_ref[listed[i]], value_ref[listed[i]]),
        lambda i: lengths_ref[listed[i]],
        put,
    )
    load.wait()

    def block(k):
        at = lax.rem(place_ref[0] + k, ring) * columns
        return jnp.dot(
            heads[...],
            wbuf[:, pl.ds(pl.multiple_of(at, columns), columns)],
            preferred_element_type=F32,
        )

    far = block(ring // 2)
    cut = up_ref.shape[0]
    up_ref[...] = far[:cut].astype(BF16)
    down_ref[...] = far[cut:].astype(BF16)
    own_ref[...] = block(0)

    def rest(j, carry):
        terms_ref[j] = block(jnp.where(j < 3, j + 1, j + 2))
        return carry

    lax.fori_loop(0, 6, rest, 0)


def leaving_kernel(
    moves_ref, lengths_ref, asked_ref, keys_ref, values_ref,
    out_ref,
    count, entry, kbuf, vbuf, score, weight, ksem, vsem,
):
    rows, batch = kbuf.shape[0], kbuf.shape[0] // ksem.shape[0]
    steps, head = asked_ref.shape[1], keys_ref.shape[3]
    wide = out_ref.shape[2]
    fetch(keys_ref, values_ref, kbuf, vbuf, ksem, vsem, lambda i: moves_ref[0, i], rows, batch)
    for g in range(count.shape[0]):
        count[g] = 0

    def enter(m, carry):
        target = moves_ref[1, m]
        entry[m] = target * CAP + count[target]
        count[target] = count[target] + 1
        return carry

    lax.fori_loop(0, rows, enter, 0, unroll=2)
    out_ref[...] = jnp.zeros(out_ref.shape, BF16)

    def put(b, mixed):
        for u, o in enumerate(mixed):
            at = entry[b * batch + u]
            for h in range(wide // head):
                out_ref[at, :, h * head : (h + 1) * head] = o[h * steps : (h + 1) * steps].astype(BF16)

    attend(
        rows, batch, keys_ref, values_ref, kbuf, vbuf, ksem, vsem, score, weight,
        lambda i: asked_ref[entry[i], :, 0:wide],
        lambda i: (asked_ref[entry[i], :, wide : wide + head], asked_ref[entry[i], :, wide + head : wide + 2 * head]),
        lambda i: lengths_ref[moves_ref[0, i]],
        put,
    )


def list_arrived(table_ref, listed, entries):
    for i in range(listed.shape[0]):
        listed[i] = 0
    count = 0
    for e in range(entries):
        listed[count] = e
        count = count + jnp.where(table_ref[e // CAP, e % CAP] > 0, 1, 0)


def arrived_kernel(table_ref, back_ref, weight_ref, out_ref, listed, heads, wbuf, wsem):
    load = pltpu.make_async_copy(weight_ref, wbuf, wsem)
    load.start()
    entries, steps = back_ref.shape[0], back_ref.shape[1]
    list_arrived(table_ref, listed, entries)
    rows = out_ref.shape[1] // steps
    columns = out_ref.shape[2]
    for j in range(heads.shape[0] // 16):
        four = [back_ref[listed[min(4 * j + u, rows - 1)]].astype(F32) for u in range(4)]
        heads[16 * j : 16 * j + 16, :] = jnp.concatenate(four, axis=0).astype(BF16)
    load.wait()

    def one(k, carry):
        terms = jnp.dot(
            heads[...],
            wbuf[:, pl.ds(pl.multiple_of(k * columns, columns), columns)],
            preferred_element_type=F32,
        )
        out_ref[k] = terms[: out_ref.shape[1]].astype(BF16)
        return carry

    lax.fori_loop(0, out_ref.shape[0], one, 0)


def place_kernel(moves_ref, flags_ref, own_ref, up_ref, down_ref, out_ref, gone, listed, total):
    steps = out_ref.shape[1]
    total[...] = own_ref[...] + up_ref[...].astype(F32) + down_ref[...].astype(F32)
    count = list_staying(moves_ref, flags_ref, gone, listed)
    out_ref[...] = jnp.zeros(out_ref.shape, BF16)
    for i in range(own_ref.shape[0] // steps):

        @pl.when(i < count)
        def _():
            out_ref[listed[i]] = total[i * steps : (i + 1) * steps, :].astype(BF16)


def finish_kernel(table_ref, placed_ref, blocks_ref, out_ref, listed, total):
    steps = out_ref.shape[1]
    entries = table_ref.shape[0] * CAP
    list_arrived(table_ref, listed, entries)
    out_ref[...] = placed_ref[...]
    terms = blocks_ref[0].astype(F32)
    for k in range(1, blocks_ref.shape[0]):
        terms = terms + blocks_ref[k].astype(F32)
    total[...] = terms
    for n in range(blocks_ref.shape[1] // steps):
        e = listed[n]
        slot = jnp.maximum(table_ref[e // CAP, lax.rem(e, CAP)] - 1, 0)
        out_ref[slot] = total[n * steps : (n + 1) * steps, :].astype(BF16)


def on_device(
    keys_cache,
    values_cache,
    lengths,
    guard_flags,
    migrations,
    queries,
    new_keys,
    new_values,
    out_weight,
):
    shape = jax.ShapeDtypeStruct
    slots, _, cache, head = keys_cache.shape
    steps, wide = queries.shape[1:]
    moves = migrations.shape[0]
    groups, ring = lax.axis_size("group"), lax.axis_size("tp")
    columns = out_weight.shape[1] // ring
    entries = groups * CAP
    staying = slots - 2 * moves
    lines = wide // head * steps
    positions = cache + FRESH
    moves_t = migrations.T
    place = lax.axis_index("tp").astype(I32).reshape(1)

    def exchange(x, axis):
        return lax.all_to_all(x, axis, split_axis=0, concat_axis=0, tiled=True)

    table = call(table_kernel, shape((groups, 128), I32), [VMEM], nbytes=1 << 16)(moves_t)
    table = exchange(table.reshape(groups, 1, 128), "group").reshape(groups, 128)

    def scratch(rows, batches):
        return [
            pltpu.VMEM((rows, positions, head), BF16),
            pltpu.VMEM((rows, positions, head), BF16),
            pltpu.VMEM((rows * lines, positions), F32),
            pltpu.VMEM((rows * lines, positions), BF16),
        ]

    tokens = staying * steps
    cut = tokens // 32 * 16
    cut = cut if cut * 2 == tokens else cut + 16
    up, down, own, terms = call(
        staying_kernel,
        [
            shape((cut, columns), BF16),
            shape((tokens - cut, columns), BF16),
            shape((tokens, columns), F32),
            shape((6, tokens, columns), F32),
        ],
        [SMEM] * 4 + [VMEM] * 3 + [ANY] * 3,
        [pltpu.SMEM((slots + 8,), I32), pltpu.SMEM((slots + 8,), I32)]
        + scratch(staying, 19)
        + [
            pltpu.VMEM((tokens, wide), BF16),
            pltpu.VMEM(out_weight.shape, BF16),
            pltpu.SemaphoreType.DMA((staying // 4,)),
            pltpu.SemaphoreType.DMA((staying // 4,)),
            pltpu.SemaphoreType.DMA,
        ],
        flops=2 * tokens * wide * out_weight.shape[1],
        nbytes=20 << 20,
        exps=tokens * positions * 4,
    )(place, moves_t, guard_flags, lengths, queries, new_keys, new_values, keys_cache, values_cache, out_weight)

    ahead = [(i, (i + 1) % ring) for i in range(ring)]
    astern = [(i, (i - 1) % ring) for i in range(ring)]

    def hop(u, d):
        u, d = lax.optimization_barrier((u, d))
        return lax.ppermute(u, "tp", ahead), lax.ppermute(d, "tp", astern)

    up, down = hop(up, down)
    up = jnp.concatenate([up, jnp.zeros((tokens - cut, columns), BF16)], axis=0)
    down = jnp.concatenate([jnp.zeros((cut, columns), BF16), down], axis=0)
    for k in (3, 2, 1):
        up, down = hop(
            (terms[k - 1] + up.astype(F32)).astype(BF16),
            (terms[6 - k] + down.astype(F32)).astype(BF16),
        )

    asked = call(
        payload_kernel, shape((entries, steps, wide + 2 * head), BF16), [SMEM] + [VMEM] * 3, nbytes=2 << 20
    )(table, queries, new_keys, new_values)
    asked = exchange(asked, "group")
    back = call(
        leaving_kernel,
        shape((entries, steps, wide), BF16),
        [SMEM] * 2 + [VMEM] + [ANY] * 2,
        [pltpu.SMEM((groups,), I32), pltpu.SMEM((moves,), I32)]
        + scratch(moves, 2)
        + [pltpu.SemaphoreType.DMA((2,)), pltpu.SemaphoreType.DMA((2,))],
        nbytes=8 << 20,
    )(moves_t, lengths, asked, keys_cache, values_cache)
    back = exchange(back, "group")
    arrived = moves * steps
    blocks = call(
        arrived_kernel,
        shape((ring, arrived, columns), BF16),
        [SMEM, VMEM, ANY],
        [
            pltpu.SMEM((entries + 8,), I32),
            pltpu.VMEM((-(-arrived // 16) * 16, wide), BF16),
            pltpu.VMEM(out_weight.shape, BF16),
            pltpu.SemaphoreType.DMA,
        ],
        nbytes=6 << 20,
    )(table, back, out_weight)
    blocks = exchange(blocks, "tp")

    placed = call(
        place_kernel,
        shape((slots, steps, columns), BF16),
        [SMEM] * 2 + [VMEM] * 3,
        [
            pltpu.SMEM((slots + 8,), I32),
            pltpu.SMEM((slots + 8,), I32),
            pltpu.VMEM((tokens, columns), F32),
        ],
        nbytes=4 << 20,
    )(moves_t, guard_flags, own, up, down)
    return call(
        finish_kernel,
        shape((slots, steps, columns), BF16),
        [SMEM] + [VMEM] * 2,
        [pltpu.SMEM((entries + 8,), I32), pltpu.VMEM((arrived, columns), F32)],
        nbytes=2 << 20,
    )(table, placed, blocks)


def solution(mesh):
    return jax.shard_map(
        on_device,
        mesh=mesh,
        in_specs=(
            P("group", "tp", None, None),
            P("group", "tp", None, None),
            P("group"),
            P("group"),
            P("group", None),
            P("group", None, "tp"),
            P("group", None, "tp"),
            P("group", None, "tp"),
            P("tp", None),
        ),
        out_specs=P("group", None, "tp"),
        check_vma=False,
    )
```

time: 252 us -> 153 us (0.61)
  the two profiles are of different devices: /device:TPU:1 before, /device:TPU:102 now
where the time goes in v1:
time: 153 us; the launch traced here: 152 us
  waiting for transfers between devices  47.6 us (31%)
  Pallas kernels  37.6 us (25%)
  starting transfers between devices  29.4 us (19%)
  local copies, waits for them, and re-layouts  19.8 us (13%)
  blocking collectives  12.9 us (8%)
  other arithmetic  4.32 us (3%)
    ppermute x8, waiting for transfers between devices, hop(): return (lax.ppermute(u, 'tp', ahead), lax.ppermute(d, 'tp', astern))  39.5 us
    pallas_call x1, Pallas kernels, on_device(): call(staying_kernel, [shape((cut, columns), BF16), shape((tokens - cut, c...  22 us
    unnamed x38, local copies, waits for them, and re-layouts  19.8 us
    all_to_all x3, starting transfers between devices, exchange(): return lax.all_to_all(x, axis, split_axis=0, concat_axis=0, tiled=True)  19.3 us
    all_to_all x1, blocking collectives, exchange(): return lax.all_to_all(x, axis, split_axis=0, concat_axis=0, tiled=True)  12.9 us
    ppermute x8, starting transfers between devices, hop(): return (lax.ppermute(u, 'tp', ahead), lax.ppermute(d, 'tp', astern))  10.1 us
    all_to_all x3, waiting for transfers between devices, exchange(): return lax.all_to_all(x, axis, split_axis=0, concat_axis=0, tiled=True)  8.04 us
    pallas_call x1, Pallas kernels, on_device(): call(leaving_kernel, shape((entries, steps, wide), BF16), [SMEM] * 2 + [V...  5.84 us
  transfers between devices with their start and end apart: 11, of which 7 were waited for; matrix products, arithmetic and copies ran while one was open for 3% of the time, Pallas kernels for 18%

profile of v1, /device:TPU:102, one launch (start us, length us, event | category | flops | bytes accessed | tf_op | source)
XLA Modules:
  0.0 151.8 jit_solution(10178805247998984330)
XLA Ops:
  0.9 12.9 %all_to_all.20 = s32[32,1,128]{2,1,0:T(1,128)S(1)} all-to-all(s32[32,1,128]{2,1,0:T(1,128)S(1)} %bitcast.33), channel_id=1, replica_groups=mesh['group'=32,'tp'=8] {'group'}, dimensions={0} | all-to-all | bytes 32768 | tf_op jit(solution)/shard_map/all_to_all | solution.py:357
  18.3 5.8 %all-to-all-start.1 = ((bf16[64,4,768]{2,1,0:T(4,128)(2,1)}), bf16[64,4,768]{2,1,0:T(4,128)(2,1)S(1)}, u32[]{:S(2)}, u32[]{:S(2)}) async-start(bf16[64,4,768]{2,1,0:T(4,128)(2,1)} %shard_map.94), calls=%async_computation.1 | async-start | bytes 786432 | tf_op jit(solution)/shard_map/all_to_all | solution.py:357
  24.1 8.0 %all-to-all-done.1.asked_ref = bf16[64,4,768]{2,1,0:T(4,128)(2,1)S(1)} async-done(((bf16[64,4,768]{2,1,0:T(4,128)(2,1)}), bf16[64,4,768]{2,1,0:T(4,128)(2,1)S(1)}, u32[]{:S(2)}, u32[]{:S(2)}) %all-to-all-start.1) | async-done | bytes 393248 | tf_op jit(solution)/shard_map/all_to_all | solution.py:357
  32.1 2.2 %copy-done = bf16[128,1,128,128]{3,2,1,0:T(8,128)(2,1)S(1)} copy-done((bf16[128,1,128,128]{3,2,1,0:T(8,128)(2,1)S(1)}, bf16[128,1,128,128]{3,2,1,0:T(8,128)(2,1)}, u32[]{:S(2)}) %copy-start) | copy-done | bytes 4194328
  34.3 2.2 %copy-done.2 = bf16[128,1,128,128]{3,2,1,0:T(8,128)(2,1)S(1)} copy-done((bf16[128,1,128,128]{3,2,1,0:T(8,128)(2,1)S(1)}, bf16[128,1,128,128]{3,2,1,0:T(8,128)(2,1)}, u32[]{:S(2)}) %copy-start.2) | copy-done | bytes 4194328
  37.9 5.8 %shard_map.95 = bf16[64,4,512]{2,1,0:T(4,128)(2,1)} custom-call(s32[3,26]{1,0:T(4,128)S(1)} %bitcast.35, s32[128]{0:T(128)S(1)} %copy-done.16, bf16[64,4,768]{2,1,0:T(4,128)(2,1)S(1)} %all-to-all-done.1.asked_ref, bf16[128,1,128,128]{3,2,1,0:T(8,128)(2,1)S(1)} %copy-done, bf16[128,1,128,128]{3,2,1,0:T(8,128)(2,1)S(1)} %copy-done.2), custom_call_target="tpu_custom_call" | custom-call | bytes 8388608 | tf_op jit(solution)/shard_map/pallas_call | solution.py:416
  43.7 5.8 %all-to-all-start.2 = ((bf16[64,4,512]{2,1,0:T(4,128)(2,1)}), bf16[64,4,512]{2,1,0:T(4,128)(2,1)S(1)}, u32[]{:S(2)}, u32[]{:S(2)}) async-start(bf16[64,4,512]{2,1,0:T(4,128)(2,1)} %shard_map.95), calls=%async_computation.2 | async-start | bytes 524288 | tf_op jit(solution)/shard_map/all_to_all | solution.py:357
  49.6 2.2 %copy-done.1 = bf16[128,1,128,128]{3,2,1,0:T(8,128)(2,1)S(1)} copy-done((bf16[128,1,128,128]{3,2,1,0:T(8,128)(2,1)S(1)}, bf16[128,1,128,128]{3,2,1,0:T(8,128)(2,1)}, u32[]{:S(2)}) %copy-start.1) | copy-done | bytes 4194328
  51.8 2.2 %copy-done.3 = bf16[128,1,128,128]{3,2,1,0:T(8,128)(2,1)S(1)} copy-done((bf16[128,1,128,128]{3,2,1,0:T(8,128)(2,1)S(1)}, bf16[128,1,128,128]{3,2,1,0:T(8,128)(2,1)}, u32[]{:S(2)}) %copy-start.3) | copy-done | bytes 4194328
  54.0 2.2 %copy-done.4 = bf16[512,4096]{1,0:T(8,128)(2,1)S(1)} copy-done((bf16[512,4096]{1,0:T(8,128)(2,1)S(1)}, bf16[512,4096]{1,0:T(8,128)(2,1)}, u32[]{:S(2)}) %copy-start.4) | copy-done | bytes 4194328
  56.2 22.0 %shard_map.92 = (bf16[160,512]{1,0:T(8,128)(2,1)S(1)}, bf16[144,512]{1,0:T(8,128)(2,1)S(1)}, f32[304,512]{1,0:T(8,128)S(1)}, f32[6,304,512]{2,1,0:T(8,128)S(1)}) custom-call(s32[1]{0:T(128)} %bitcast.4.place_ref, s32[3,26]{1,0:T(4,128)S(1)} %bitcast.36, s32[128]{0:T(128)S(1)} %copy-done.18, s32[128]{0:T(128)S(1)} %copy-done.17, ...), custom_call_target="tpu_custom_call" | custom-call | flops 1275068416 | bytes 20971520 | tf_op jit(solution)/shard_map/pallas_call | solution.py:373
  80.0 3.1 %collective-permute-start = (bf16[160,512]{1,0:T(8,128)(2,1)S(1)}, bf16[160,512]{1,0:T(8,128)(2,1)S(1)}, u32[]{:S(2)}, u32[]{:S(2)}) collective-permute-start(bf16[160,512]{1,0:T(8,128)(2,1)S(1)} %get-tuple-element.21), channel_id=1, source_target_pairs={{0,1},{1,2},{2,3},{3,4},{4,5},{5,6},{6,7},{7,0},{8,9},{9,10},{10,1... | collective-permute-start | bytes 491528 | tf_op jit(solution)/shard_map/ppermute | solution.py:401
  83.1 2.2 %copy-done.5 = bf16[512,4096]{1,0:T(8,128)(2,1)S(1)} copy-done((bf16[512,4096]{1,0:T(8,128)(2,1)S(1)}, bf16[512,4096]{1,0:T(8,128)(2,1)}, u32[]{:S(2)}) %copy-start.5) | copy-done | bytes 4194328
  85.3 4.0 %shard_map.96 = bf16[8,104,512]{2,1,0:T(8,128)(2,1)} custom-call(s32[32,128]{1,0:T(8,128)S(1)} %bitcast.31, bf16[64,4,512]{2,1,0:T(4,128)(2,1)S(1)} %all-to-all-done.2.back_ref, bf16[512,4096]{1,0:T(8,128)(2,1)S(1)} %copy-done.5), custom_call_target="tpu_custom_call" | custom-call | bytes 6291456 | tf_op jit(solution)/shard_map/pallas_call | solution.py:427
  89.3 7.8 %all-to-all-start.3 = ((bf16[8,104,512]{2,1,0:T(8,128)(2,1)}), bf16[8,104,512]{2,1,0:T(8,128)(2,1)S(1)}, u32[]{:S(2)}, u32[]{:S(2)}) async-start(bf16[8,104,512]{2,1,0:T(8,128)(2,1)} %shard_map.96), calls=%async_computation.3 | async-start | bytes 1703936 | tf_op jit(solution)/shard_map/all_to_all | solution.py:357
  98.5 2.8 %collective-permute-start.2 = (bf16[304,512]{1,0:T(8,128)(2,1)S(1)}, bf16[304,512]{1,0:T(8,128)(2,1)S(1)}, u32[]{:S(2)}, u32[]{:S(2)}) collective-permute-start(bf16[304,512]{1,0:T(8,128)(2,1)S(1)} %get-tuple-element.23), channel_id=1, source_target_pairs={{0,1},{1,2},{2,3},{3,4},{4,5},{5,6},{6,7},{7,0},{8,9},{9,10},{10,1... | collective-permute-start | bytes 933896 | tf_op jit(solution)/shard_map/ppermute | solution.py:401
  101.3 21.1 %collective-permute-done.2 = bf16[304,512]{1,0:T(8,128)(2,1)S(1)} collective-permute-done((bf16[304,512]{1,0:T(8,128)(2,1)S(1)}, bf16[304,512]{1,0:T(8,128)(2,1)S(1)}, u32[]{:S(2)}, u32[]{:S(2)}) %collective-permute-start.2) | collective-permute-done | bytes 311328 | tf_op jit(solution)/shard_map/ppermute | solution.py:401
  122.4 2.4 %collective-permute-done.3 = bf16[304,512]{1,0:T(8,128)(2,1)S(1)} collective-permute-done((bf16[304,512]{1,0:T(8,128)(2,1)S(1)}, bf16[304,512]{1,0:T(8,128)(2,1)S(1)}, u32[]{:S(2)}, u32[]{:S(2)}) %collective-permute-start.3) | collective-permute-done | bytes 311328 | tf_op jit(solution)/shard_map/ppermute | solution.py:401
  128.4 5.7 %collective-permute-done.4 = bf16[304,512]{1,0:T(8,128)(2,1)S(1)} collective-permute-done((bf16[304,512]{1,0:T(8,128)(2,1)S(1)}, bf16[304,512]{1,0:T(8,128)(2,1)S(1)}, u32[]{:S(2)}, u32[]{:S(2)}) %collective-permute-start.4) | collective-permute-done | bytes 311328 | tf_op jit(solution)/shard_map/ppermute | solution.py:401
  134.1 2.0 %collective-permute-done.5 = bf16[304,512]{1,0:T(8,128)(2,1)S(1)} collective-permute-done((bf16[304,512]{1,0:T(8,128)(2,1)S(1)}, bf16[304,512]{1,0:T(8,128)(2,1)S(1)}, u32[]{:S(2)}, u32[]{:S(2)}) %collective-permute-start.5) | collective-permute-done | bytes 311328 | tf_op jit(solution)/shard_map/ppermute | solution.py:401
  139.7 5.0 %collective-permute-done.6.up_ref = bf16[304,512]{1,0:T(8,128)(2,1)S(1)} collective-permute-done((bf16[304,512]{1,0:T(8,128)(2,1)S(1)}, bf16[304,512]{1,0:T(8,128)(2,1)S(1)}, u32[]{:S(2)}, u32[]{:S(2)}) %collective-permute-start.6) | collective-permute-done | bytes 311328 | tf_op jit(solution)/shard_map/ppermute | solution.py:401
  144.7 3.3 %collective-permute-done.7.down_ref = bf16[304,512]{1,0:T(8,128)(2,1)S(1)} collective-permute-done((bf16[304,512]{1,0:T(8,128)(2,1)S(1)}, bf16[304,512]{1,0:T(8,128)(2,1)S(1)}, u32[]{:S(2)}, u32[]{:S(2)}) %collective-permute-start.7) | collective-permute-done | bytes 311328 | tf_op jit(solution)/shard_map/ppermute | solution.py:401
  148.0 1.9 %shard_map.93.placed_ref = bf16[128,4,512]{2,1,0:T(4,128)(2,1)S(1)} custom-call(s32[3,26]{1,0:T(4,128)S(1)} %bitcast.37, s32[128]{0:T(128)S(1)} %copy-done.18, f32[304,512]{1,0:T(8,128)S(1)} %get-tuple-element.17.own_ref, bf16[304,512]{1,0:T(8,128)(2,1)S(1)} %collective-permute-done.6.up_ref, bf16[304,512]{1,0:T(8,128)(2,1)S(1)} %collective-permute-done.7.down_ref), custom_call_target="tpu_custom_call" | custom-call | bytes 4194304 | tf_op jit(solution)/shard_map/pallas_call | solution.py:441
  149.8 2.0 %shard_map.97 = bf16[128,4,512]{2,1,0:T(4,128)(2,1)} custom-call(s32[32,128]{1,0:T(8,128)S(1)} %bitcast.32, bf16[128,4,512]{2,1,0:T(4,128)(2,1)S(1)} %shard_map.93.placed_ref, bf16[8,104,512]{2,1,0:T(8,128)(2,1)S(1)} %all-to-all-done.3.blocks_ref), custom_call_target="tpu_custom_call" | custom-call | bytes 2097152 | tf_op jit(solution)/shard_map/pallas_call | solution.py:452
  (47 shorter events, 17.1 us)
Async XLA Ops:
  18.3 13.8 %all-to-all-start.1 = ((bf16[64,4,768]{2,1,0:T(4,128)(2,1)}), bf16[64,4,768]{2,1,0:T(4,128)(2,1)S(1)}, u32[]{:S(2)}, u32[]{:S(2)}) async-start(bf16[64,4,768]{2,1,0:T(4,128)(2,1)} %shard_map.94), calls=%async_computation.1 | async-start | bytes 786432 | tf_op jit(solution)/shard_map/all_to_all | solution.py:357
  32.1 2.2 %copy-start = (bf16[128,1,128,128]{3,2,1,0:T(8,128)(2,1)S(1)}, bf16[128,1,128,128]{3,2,1,0:T(8,128)(2,1)}, u32[]{:S(2)}) copy-start(bf16[128,1,128,128]{3,2,1,0:T(8,128)(2,1)} %keys_ref.3) | copy-start | bytes 12582916
  34.3 2.2 %copy-start.2 = (bf16[128,1,128,128]{3,2,1,0:T(8,128)(2,1)S(1)}, bf16[128,1,128,128]{3,2,1,0:T(8,128)(2,1)}, u32[]{:S(2)}) copy-start(bf16[128,1,128,128]{3,2,1,0:T(8,128)(2,1)} %values_ref.3) | copy-start | bytes 12582916
  37.9 11.7 %copy-start.8 = (bf16[128,4,512]{2,1,0:T(4,128)(2,1)S(1)}, bf16[128,4,512]{2,1,0:T(4,128)(2,1)}, u32[]{:S(2)}) copy-start(bf16[128,4,512]{2,1,0:T(4,128)(2,1)} %query_ref.3) | copy-start | bytes 1572868
  37.9 11.7 %copy-start.10 = (bf16[128,4,128]{2,1,0:T(4,128)(2,1)S(1)}, bf16[128,4,128]{2,1,0:T(4,128)(2,1)}, u32[]{:S(2)}) copy-start(bf16[128,4,128]{2,1,0:T(4,128)(2,1)} %key_ref.3) | copy-start | bytes 393220
  37.9 11.7 %copy-start.12 = (bf16[128,4,128]{2,1,0:T(4,128)(2,1)S(1)}, bf16[128,4,128]{2,1,0:T(4,128)(2,1)}, u32[]{:S(2)}) copy-start(bf16[128,4,128]{2,1,0:T(4,128)(2,1)} %value_ref.3) | copy-start | bytes 393220
  37.9 11.7 %copy-start.15 = (s32[26,3]{0,1:T(4,128)S(1)}, s32[26,3]{0,1:T(4,128)}, u32[]{:S(2)}) copy-start(s32[26,3]{0,1:T(4,128)} %param.13) | copy-start | bytes 940
  37.9 11.7 %copy-start.17 = (s32[128]{0:T(128)S(1)}, s32[128]{0:T(128)}, u32[]{:S(2)}) copy-start(s32[128]{0:T(128)} %lengths_ref.3) | copy-start | bytes 1540
  37.9 11.7 %copy-start.18 = (s32[128]{0:T(128)S(1)}, s32[128]{0:T(128)}, u32[]{:S(2)}) copy-start(s32[128]{0:T(128)} %flags_ref.3) | copy-start | bytes 1540
  43.7 39.4 %all-to-all-start.2 = ((bf16[64,4,512]{2,1,0:T(4,128)(2,1)}), bf16[64,4,512]{2,1,0:T(4,128)(2,1)S(1)}, u32[]{:S(2)}, u32[]{:S(2)}) async-start(bf16[64,4,512]{2,1,0:T(4,128)(2,1)} %shard_map.95), calls=%async_computation.2 | async-start | bytes 524288 | tf_op jit(solution)/shard_map/all_to_all | solution.py:357
  49.6 2.2 %copy-start.1 = (bf16[128,1,128,128]{3,2,1,0:T(8,128)(2,1)S(1)}, bf16[128,1,128,128]{3,2,1,0:T(8,128)(2,1)}, u32[]{:S(2)}) copy-start(bf16[128,1,128,128]{3,2,1,0:T(8,128)(2,1)} %keys_ref.3) | copy-start | bytes 12582916
  51.8 2.2 %copy-start.3 = (bf16[128,1,128,128]{3,2,1,0:T(8,128)(2,1)S(1)}, bf16[128,1,128,128]{3,2,1,0:T(8,128)(2,1)}, u32[]{:S(2)}) copy-start(bf16[128,1,128,128]{3,2,1,0:T(8,128)(2,1)} %values_ref.3) | copy-start | bytes 12582916
  54.0 2.2 %copy-start.4 = (bf16[512,4096]{1,0:T(8,128)(2,1)S(1)}, bf16[512,4096]{1,0:T(8,128)(2,1)}, u32[]{:S(2)}) copy-start(bf16[512,4096]{1,0:T(8,128)(2,1)} %weight_ref.3) | copy-start | bytes 12582916
  78.2 1.8 %copy-start.6 = (f32[6,304,512]{2,1,0:T(8,128)}, f32[6,304,512]{2,1,0:T(8,128)S(1)}, u32[]{:S(2)}) copy-start(f32[6,304,512]{2,1,0:T(8,128)S(1)} %get-tuple-element.18) | copy-start | bytes 11206660
  80.0 17.2 %collective-permute-start = (bf16[160,512]{1,0:T(8,128)(2,1)S(1)}, bf16[160,512]{1,0:T(8,128)(2,1)S(1)}, u32[]{:S(2)}, u32[]{:S(2)}) collective-permute-start(bf16[160,512]{1,0:T(8,128)(2,1)S(1)} %get-tuple-element.21), channel_id=1, source_target_pairs={{0,1},{1,2},{2,3},{3,4},{4,5},{5,6},{6,7},{7,0},{8,9},{9,10},{10,1... | collective-permute-start | bytes 491528 | tf_op jit(solution)/shard_map/ppermute | solution.py:401
  83.1 14.0 %collective-permute-start.1 = (bf16[144,512]{1,0:T(8,128)(2,1)S(1)}, bf16[144,512]{1,0:T(8,128)(2,1)S(1)}, u32[]{:S(2)}, u32[]{:S(2)}) collective-permute-start(bf16[144,512]{1,0:T(8,128)(2,1)S(1)} %get-tuple-element.22), channel_id=1, source_target_pairs={{0,7},{1,0},{2,1},{3,2},{4,3},{5,4},{6,5},{7,6},{8,15},{9,8},{10,9... | collective-permute-start | bytes 442376 | tf_op jit(solution)/shard_map/ppermute | solution.py:401
  83.1 2.2 %copy-start.5 = (bf16[512,4096]{1,0:T(8,128)(2,1)S(1)}, bf16[512,4096]{1,0:T(8,128)(2,1)}, u32[]{:S(2)}) copy-start(bf16[512,4096]{1,0:T(8,128)(2,1)} %weight_ref.3) | copy-start | bytes 12582916
  89.3 60.5 %all-to-all-start.3 = ((bf16[8,104,512]{2,1,0:T(8,128)(2,1)}), bf16[8,104,512]{2,1,0:T(8,128)(2,1)S(1)}, u32[]{:S(2)}, u32[]{:S(2)}) async-start(bf16[8,104,512]{2,1,0:T(8,128)(2,1)} %shard_map.96), calls=%async_computation.3 | async-start | bytes 1703936 | tf_op jit(solution)/shard_map/all_to_all | solution.py:357
  98.5 23.9 %collective-permute-start.2 = (bf16[304,512]{1,0:T(8,128)(2,1)S(1)}, bf16[304,512]{1,0:T(8,128)(2,1)S(1)}, u32[]{:S(2)}, u32[]{:S(2)}) collective-permute-start(bf16[304,512]{1,0:T(8,128)(2,1)S(1)} %get-tuple-element.23), channel_id=1, source_target_pairs={{0,1},{1,2},{2,3},{3,4},{4,5},{5,6},{6,7},{7,0},{8,9},{9,10},{10,1... | collective-permute-start | bytes 933896 | tf_op jit(solution)/shard_map/ppermute | solution.py:401
  101.3 23.5 %collective-permute-start.3 = (bf16[304,512]{1,0:T(8,128)(2,1)S(1)}, bf16[304,512]{1,0:T(8,128)(2,1)S(1)}, u32[]{:S(2)}, u32[]{:S(2)}) collective-permute-start(bf16[304,512]{1,0:T(8,128)(2,1)S(1)} %get-tuple-element.24), channel_id=1, source_target_pairs={{0,7},{1,0},{2,1},{3,2},{4,3},{5,4},{6,5},{7,6},{8,15},{9,8},{10,9... | collective-permute-start | bytes 933896 | tf_op jit(solution)/shard_map/ppermute | solution.py:401
  126.3 7.8 %collective-permute-start.4 = (bf16[304,512]{1,0:T(8,128)(2,1)S(1)}, bf16[304,512]{1,0:T(8,128)(2,1)S(1)}, u32[]{:S(2)}, u32[]{:S(2)}) collective-permute-start(bf16[304,512]{1,0:T(8,128)(2,1)S(1)} %get-tuple-element.25), channel_id=1, source_target_pairs={{0,1},{1,2},{2,3},{3,4},{4,5},{5,6},{6,7},{7,0},{8,9},{9,10},{10,1... | collective-permute-start | bytes 933896 | tf_op jit(solution)/shard_map/ppermute | solution.py:401
  126.9 9.2 %collective-permute-start.5 = (bf16[304,512]{1,0:T(8,128)(2,1)S(1)}, bf16[304,512]{1,0:T(8,128)(2,1)S(1)}, u32[]{:S(2)}, u32[]{:S(2)}) collective-permute-start(bf16[304,512]{1,0:T(8,128)(2,1)S(1)} %get-tuple-element.26), channel_id=1, source_target_pairs={{0,7},{1,0},{2,1},{3,2},{4,3},{5,4},{6,5},{7,6},{8,15},{9,8},{10,9... | collective-permute-start | bytes 933896 | tf_op jit(solution)/shard_map/ppermute | solution.py:401
  137.6 7.1 %collective-permute-start.6 = (bf16[304,512]{1,0:T(8,128)(2,1)S(1)}, bf16[304,512]{1,0:T(8,128)(2,1)S(1)}, u32[]{:S(2)}, u32[]{:S(2)}) collective-permute-start(bf16[304,512]{1,0:T(8,128)(2,1)S(1)} %get-tuple-element.27), channel_id=1, source_target_pairs={{0,1},{1,2},{2,3},{3,4},{4,5},{5,6},{6,7},{7,0},{8,9},{9,10},{10,1... | collective-permute-start | bytes 933896 | tf_op jit(solution)/shard_map/ppermute | solution.py:401
  138.9 9.0 %collective-permute-start.7 = (bf16[304,512]{1,0:T(8,128)(2,1)S(1)}, bf16[304,512]{1,0:T(8,128)(2,1)S(1)}, u32[]{:S(2)}, u32[]{:S(2)}) collective-permute-start(bf16[304,512]{1,0:T(8,128)(2,1)S(1)} %get-tuple-element.28), channel_id=1, source_target_pairs={{0,7},{1,0},{2,1},{3,2},{4,3},{5,4},{6,5},{7,6},{8,15},{9,8},{10,9... | collective-permute-start | bytes 933896 | tf_op jit(solution)/shard_map/ppermute | solution.py:401
  (6 other events, 4.9 us)

commit v2 on v1

v2 whole, which is shorter than its diff:
```python
import functools

import jax
import jax.numpy as jnp
from jax import lax
from jax.experimental import pallas as pl
from jax.experimental.pallas import tpu as pltpu
from jax.sharding import PartitionSpec as P

CAP = 2
F32, BF16, I32 = jnp.float32, jnp.bfloat16, jnp.int32
FRESH = 16
STAY_BATCH, LEAVE_BATCH = 76, 26
VMEM = pl.BlockSpec(memory_space=pltpu.VMEM)
SMEM = pl.BlockSpec(memory_space=pltpu.SMEM)
ANY = pl.BlockSpec(memory_space=pltpu.HBM)


def call(kernel, out_shape, in_specs, scratch=(), flops=0, nbytes=0, exps=0, limit=32):
    single = isinstance(out_shape, jax.ShapeDtypeStruct)
    return pl.pallas_call(
        kernel,
        out_shape=out_shape,
        in_specs=in_specs,
        out_specs=VMEM if single else [VMEM] * len(out_shape),
        scratch_shapes=list(scratch),
        cost_estimate=pl.CostEstimate(
            flops=flops, bytes_accessed=nbytes, transcendentals=exps
        ),
        compiler_params=pltpu.CompilerParams(vmem_limit_bytes=limit << 20),
    )


STAY_SLOT, STAY_LENGTH, LEAVE_SLOT, LEAVE_ENTRY, LEAVE_LENGTH, STAY_COUNT = range(6)


def lanes(rows, columns):
    return lax.broadcasted_iota(I32, (rows, columns), 1)


def lines_of(rows, columns):
    return lax.broadcasted_iota(I32, (rows, columns), 0)


def upright(row):
    n = row.shape[1]
    return jnp.sum(jnp.where(lanes(n, n) == lines_of(n, n), row, 0.0), axis=1, keepdims=True)


def plan_kernel(moves_ref, flags_ref, lengths_ref, table_ref, plan_ref):
    groups, wide = table_ref.shape
    moves, slots = moves_ref.shape[1], flags_ref.shape[1]
    source, target = moves_ref[0:1, :], moves_ref[1:2, :]
    slot = (moves_ref[2:3, :] + 1).astype(F32)
    hit = lines_of(groups, moves) == target
    earlier = (lines_of(moves, moves) < lanes(moves, moves)).astype(F32)
    before = jnp.dot(hit.astype(F32), earlier, preferred_element_type=F32).astype(I32)
    table = jnp.zeros((groups, wide), I32)
    for c in range(CAP):
        entry = jnp.sum(jnp.where(hit & (before == c), slot, 0.0), axis=1, keepdims=True)
        table = jnp.where(lanes(groups, wide) == c, entry.astype(I32), table)
    table_ref[...] = table

    place = jnp.sum(jnp.where(hit, lines_of(groups, moves) * CAP + before, 0).astype(F32), axis=0, keepdims=True)
    lengths = lengths_ref[...].astype(F32)
    taken = (upright(source.astype(F32)).astype(I32) == lanes(moves, slots)).astype(F32)
    leave_length = jnp.sum(taken * lengths, axis=1, keepdims=True)
    leave_length = jnp.sum(
        jnp.where(lanes(moves, moves) == lines_of(moves, moves), leave_length, 0.0), axis=0, keepdims=True
    )
    gone = jnp.sum(taken, axis=0, keepdims=True)
    stays = ((flags_ref[...] == 0) & (gone == 0.0)).astype(F32)
    rank = jnp.sum(jnp.where(lanes(slots, slots) < lines_of(slots, slots), stays, 0.0), axis=1, keepdims=True)
    chosen = (rank.astype(I32) == lanes(slots, slots)) & (upright(stays) > 0.0)
    listed = jnp.sum(jnp.where(chosen, lines_of(slots, slots).astype(F32), 0.0), axis=0, keepdims=True)
    listed_length = jnp.sum(jnp.where(chosen, upright(lengths), 0.0), axis=0, keepdims=True)
    plan_ref[...] = jnp.zeros(plan_ref.shape, I32)
    plan_ref[STAY_SLOT : STAY_SLOT + 1, :] = listed.astype(I32)
    plan_ref[STAY_LENGTH : STAY_LENGTH + 1, :] = listed_length.astype(I32)
    plan_ref[LEAVE_SLOT : LEAVE_SLOT + 1, 0:moves] = source
    plan_ref[LEAVE_ENTRY : LEAVE_ENTRY + 1, 0:moves] = place.astype(I32)
    plan_ref[LEAVE_LENGTH : LEAVE_LENGTH + 1, 0:moves] = leave_length.astype(I32)
    plan_ref[STAY_COUNT : STAY_COUNT + 1, 0:1] = jnp.sum(stays, axis=1, keepdims=True).astype(I32)


HERE_ENTRY, HERE_SLOT = range(2)


def payload_kernel(slot_ref, table_ref, query_ref, key_ref, value_ref, out_ref, here_ref):
    wide, narrow = query_ref.shape[2], key_ref.shape[2]
    for e in range(out_ref.shape[0]):
        slot = jnp.maximum(slot_ref[e // CAP, e % CAP] - 1, 0)
        out_ref[e, :, 0:wide] = query_ref[slot]
        out_ref[e, :, wide : wide + narrow] = key_ref[slot]
        out_ref[e, :, wide + narrow : wide + 2 * narrow] = value_ref[slot]
    groups, width = table_ref.shape
    table = table_ref[...]
    there = (table > 0).astype(F32)
    earlier = (lanes(groups, groups) < lines_of(groups, groups)).astype(F32)
    before = jnp.dot(earlier, there, preferred_element_type=F32)
    whole = jnp.sum(there, axis=0, keepdims=True)
    entry = jnp.zeros((1, width), F32)
    slot = jnp.zeros((1, width), F32)
    base = jnp.zeros((1, 1), F32)
    for c in range(CAP):
        rank = (before[:, c : c + 1] + base).astype(I32)
        chosen = (rank == lanes(groups, width)) & (there[:, c : c + 1] > 0.0)
        entry += jnp.sum(jnp.where(chosen, (lines_of(groups, width) * CAP + c).astype(F32), 0.0), axis=0, keepdims=True)
        slot += jnp.sum(jnp.where(chosen, (table[:, c : c + 1] - 1).astype(F32), 0.0), axis=0, keepdims=True)
        base = base + whole[:, c : c + 1]
    here_ref[...] = jnp.zeros(here_ref.shape, I32)
    here_ref[HERE_ENTRY : HERE_ENTRY + 1, :] = entry.astype(I32)
    here_ref[HERE_SLOT : HERE_SLOT + 1, :] = slot.astype(I32)


def attend(rows, batch, kbuf, vbuf, score, weight, cache, steps, heads, row_of, query_of, fresh_of, length_of, await_keys, await_values, put):
    positions, head = kbuf.shape[1:]
    lines = heads * steps

    def fresh_rows(value):
        pad = jnp.zeros((FRESH - steps, head), F32)
        return jnp.concatenate([value.astype(F32), pad], axis=0).astype(BF16)

    def scores(b, carry):
        lane = lanes(lines, positions)
        step = lax.rem(lines_of(lines, positions), steps)
        visible = (lane >= cache) & (lane - cache <= step)
        for u in range(batch):
            i = b * batch + u
            fresh_key, fresh_value = fresh_of(i)
            kbuf[row_of(i), cache:positions, :] = fresh_rows(fresh_key)
            vbuf[row_of(i), cache:positions, :] = fresh_rows(fresh_value)
        for u in range(batch):
            i = b * batch + u
            query = query_of(i).astype(F32)
            query = jnp.concatenate([query[:, h * head : (h + 1) * head] for h in range(heads)], axis=0)
            products = lax.dot_general(
                query.astype(BF16), kbuf[row_of(i)], (((1,), (1,)), ((), ())), preferred_element_type=F32
            )
            score[pl.ds(pl.multiple_of(i * lines, lines), lines), :] = jnp.where(
                (lane < length_of(i)) | visible, products * head**-0.5, -jnp.inf
            )
        return carry

    await_keys()
    lax.fori_loop(0, rows // batch, scores, 0)

    def soften(b, carry):
        chunk = pl.ds(pl.multiple_of(b * batch * lines, lines), batch * lines)
        s = score[chunk, :]
        e = jnp.exp(s - jnp.max(s, axis=1, keepdims=True))
        weight[chunk, :] = (e * (1.0 / jnp.sum(e, axis=1, keepdims=True))).astype(BF16)
        return carry

    lax.fori_loop(0, rows // batch, soften, 0)

    def mix(b, carry):
        mixed = []
        for u in range(batch):
            i = b * batch + u
            mixed.append(
                jnp.dot(
                    weight[pl.ds(pl.multiple_of(i * lines, lines), lines), :],
                    vbuf[row_of(i)],
                    preferred_element_type=F32,
                )
            )
        put(b, mixed)
        return carry

    await_values()
    lax.fori_loop(0, rows // batch, mix, 0)


def staying_kernel(
    place_ref, plan_ref, query_ref, key_ref, value_ref, keys_ref, values_ref, weight_ref,
    up_ref, down_ref, own_ref, *rest,
):
    terms_refs, (kbuf, vbuf, score, weight, heads, wbuf, ksem, vsem, wsem) = rest[:6], rest[6:]
    steps, wide = query_ref.shape[1:]
    slots, _, cache, head = keys_ref.shape
    tokens = heads.shape[0]
    ring, columns = 8, up_ref.shape[1]
    loads = [
        [
            pltpu.make_async_copy(
                ref.at[pl.ds(c * 32, 32), 0], buf.at[pl.ds(c * 32, 32), pl.ds(0, cache)], sem.at[c]
            )
            for c in range(slots // 32)
        ]
        for ref, buf, sem in ((keys_ref, kbuf, ksem), (values_ref, vbuf, vsem))
    ]
    for copy in loads[0] + loads[1]:
        copy.start()
    load = pltpu.make_async_copy(weight_ref, wbuf, wsem)
    load.start()
    def put(b, mixed):
        quads = len(mixed) // 4
        for j in range(quads):
            four = mixed[4 * j : 4 * j + 4]
            for h in range(wide // head):
                tile = jnp.concatenate([o[h * steps : (h + 1) * steps] for o in four], axis=0)
                at = pl.ds(pl.multiple_of((b * quads + j) * 16, 16), 16)
                heads[at, h * head : (h + 1) * head] = tile.astype(BF16)

    def slot(i):
        return plan_ref[STAY_SLOT, i]

    attend(
        tokens // steps, STAY_BATCH, kbuf, vbuf, score, weight, cache, steps, wide // head,
        slot,
        lambda i: query_ref[slot(i)],
        lambda i: (key_ref[slot(i)], value_ref[slot(i)]),
        lambda i: plan_ref[STAY_LENGTH, i],
        lambda: [copy.wait() for copy in loads[0]],
        lambda: [copy.wait() for copy in loads[1]],
        put,
    )
    load.wait()

    def block(k):
        at = lax.rem(place_ref[0] + k, ring) * columns
        return jnp.dot(
            heads[...], wbuf[:, pl.ds(pl.multiple_of(at, columns), columns)], preferred_element_type=F32
        )

    far = block(ring // 2)
    cut = up_ref.shape[0]
    up_ref[...] = far[:cut].astype(BF16)
    down_ref[...] = far[cut:].astype(BF16)
    own_ref[...] = block(0)
    for k, ref in zip((1, 2, 3, 5, 6, 7), terms_refs):
        ref[...] = block(k)


def leaving_kernel(plan_ref, asked_ref, keys_ref, values_ref, out_ref, kbuf, vbuf, score, weight, ksem, vsem):
    rows, cache, head = kbuf.shape[0], keys_ref.shape[2], keys_ref.shape[3]
    steps, wide = out_ref.shape[1:]
    loads = [
        [
            pltpu.make_async_copy(ref.at[plan_ref[LEAVE_SLOT, i], 0], buf.at[i, pl.ds(0, cache)], sem.at[i])
            for i in range(rows)
        ]
        for ref, buf, sem in ((keys_ref, kbuf, ksem), (values_ref, vbuf, vsem))
    ]
    for copy in loads[0] + loads[1]:
        copy.start()
    out_ref[...] = jnp.zeros(out_ref.shape, BF16)

    def entry(i):
        return plan_ref[LEAVE_ENTRY, i]

    def put(b, mixed):
        for u, o in enumerate(mixed):
            at = entry(b * LEAVE_BATCH + u)
            for h in range(wide // head):
                out_ref[at, :, h * head : (h + 1) * head] = o[h * steps : (h + 1) * steps].astype(BF16)

    attend(
        rows, LEAVE_BATCH, kbuf, vbuf, score, weight, cache, steps, wide // head,
        lambda i: i,
        lambda i: asked_ref[entry(i), :, 0:wide],
        lambda i: (asked_ref[entry(i), :, wide : wide + head], asked_ref[entry(i), :, wide + head : wide + 2 * head]),
        lambda i: plan_ref[LEAVE_LENGTH, i],
        lambda: [copy.wait() for copy in loads[0]],
        lambda: [copy.wait() for copy in loads[1]],
        put,
    )


def arrived_kernel(here_ref, back_ref, weight_ref, out_ref, heads, wbuf, wsem):
    load = pltpu.make_async_copy(weight_ref, wbuf, wsem)
    load.start()
    steps = back_ref.shape[1]
    rows, columns = out_ref.shape[1] // steps, out_ref.shape[2]
    for j in range(heads.shape[0] // 16):
        four = [back_ref[here_ref[HERE_ENTRY, min(4 * j + u, rows - 1)]].astype(F32) for u in range(4)]
        heads[16 * j : 16 * j + 16, :] = jnp.concatenate(four, axis=0).astype(BF16)
    load.wait()
    for k in range(out_ref.shape[0]):
        terms = jnp.dot(heads[...], wbuf[:, k * columns : (k + 1) * columns], preferred_element_type=F32)
        out_ref[k] = terms[: out_ref.shape[1]].astype(BF16)


def place_kernel(plan_ref, own_ref, up_ref, down_ref, out_ref, total):
    steps = out_ref.shape[1]
    total[...] = own_ref[...] + up_ref[...].astype(F32) + down_ref[...].astype(F32)
    out_ref[...] = jnp.zeros(out_ref.shape, BF16)
    for i in range(own_ref.shape[0] // steps):

        @pl.when(i < plan_ref[STAY_COUNT, 0])
        def _():
            out_ref[plan_ref[STAY_SLOT, i]] = total[i * steps : (i + 1) * steps, :].astype(BF16)


def finish_kernel(here_ref, placed_ref, blocks_ref, out_ref, total):
    steps = out_ref.shape[1]
    out_ref[...] = placed_ref[...]
    terms = blocks_ref[0].astype(F32)
    for k in range(1, blocks_ref.shape[0]):
        terms = terms + blocks_ref[k].astype(F32)
    total[...] = terms
    for n in range(blocks_ref.shape[1] // steps):
        out_ref[here_ref[HERE_SLOT, n]] = total[n * steps : (n + 1) * steps, :].astype(BF16)


def on_device(
    keys_cache,
    values_cache,
    lengths,
    guard_flags,
    migrations,
    queries,
    new_keys,
    new_values,
    out_weight,
):
    shape = jax.ShapeDtypeStruct
    slots, _, cache, head = keys_cache.shape
    steps, wide = queries.shape[1:]
    moves = migrations.shape[0]
    groups, ring = lax.axis_size("group"), lax.axis_size("tp")
    columns = out_weight.shape[1] // ring
    entries = groups * CAP
    staying = slots - 2 * moves
    lines = wide // head * steps
    positions = cache + FRESH
    place = lax.axis_index("tp").astype(I32).reshape(1)
    barrier = lax.optimization_barrier
    keys_cache, values_cache, out_weight = (
        pltpu.with_memory_space_constraint(x, pltpu.HBM) for x in (keys_cache, values_cache, out_weight)
    )

    def exchange(x, axis):
        return lax.all_to_all(x, axis, split_axis=0, concat_axis=0, tiled=True)

    def scratch(held, rows):
        return [
            pltpu.VMEM((held, positions, head), BF16),
            pltpu.VMEM((held, positions, head), BF16),
            pltpu.VMEM((rows * lines, positions), F32),
            pltpu.VMEM((rows * lines, positions), BF16),
        ]

    table, plan = call(plan_kernel, [shape((groups, 128), I32), shape((8, slots), I32)], [VMEM] * 3, nbytes=1 << 16)(
        migrations.T, guard_flags.reshape(1, slots), lengths.reshape(1, slots)
    )
    table = exchange(table.reshape(groups, 1, 128), "group").reshape(groups, 128)

    tokens = staying * steps
    cut = -(-tokens // 32) * 16
    up, down, own, *terms = call(
        staying_kernel,
        [shape((cut, columns), BF16), shape((tokens - cut, columns), BF16)] + [shape((tokens, columns), F32)] * 7,
        [SMEM] * 2 + [VMEM] * 3 + [ANY] * 3,
        scratch(slots, staying)
        + [
            pltpu.VMEM((tokens, wide), BF16),
            pltpu.VMEM(out_weight.shape, BF16),
            pltpu.SemaphoreType.DMA((slots // 32,)),
            pltpu.SemaphoreType.DMA((slots // 32,)),
            pltpu.SemaphoreType.DMA,
        ],
        flops=2 * tokens * wide * out_weight.shape[1],
        nbytes=20 << 20,
        exps=tokens * positions * 4,
    )(place, plan, queries, new_keys, new_values, keys_cache, values_cache, out_weight)

    ahead = [(i, (i + 1) % ring) for i in range(ring)]
    astern = [(i, (i - 1) % ring) for i in range(ring)]

    def hop(u, d):
        return lax.ppermute(u, "tp", ahead), lax.ppermute(d, "tp", astern)

    def add(k, u, d):
        return (terms[k - 1] + u.astype(F32)).astype(BF16), (terms[6 - k] + d.astype(F32)).astype(BF16)

    table, up, down = barrier((table, up, down))
    up, down = hop(up, down)
    asked, here = call(
        payload_kernel,
        [shape((entries, steps, wide + 2 * head), BF16), shape((8, 128), I32)],
        [SMEM] + [VMEM] * 4,
        nbytes=2 << 20,
    )(table, table, queries, new_keys, new_values)
    asked = exchange(asked, "group")

    asked, up, down = barrier((asked, up, down))
    up = jnp.concatenate([up, jnp.zeros((tokens - cut, columns), BF16)], axis=0)
    down = jnp.concatenate([jnp.zeros((cut, columns), BF16), down], axis=0)
    up, down = hop(*barrier(add(3, up, down)))
    back = call(
        leaving_kernel,
        shape((entries, steps, wide), BF16),
        [SMEM] + [VMEM] + [ANY] * 2,
        scratch(moves, moves) + [pltpu.SemaphoreType.DMA((moves,)), pltpu.SemaphoreType.DMA((moves,))],
        nbytes=8 << 20,
    )(plan, asked, keys_cache, values_cache)
    back = exchange(back, "group")

    back, up, down = barrier((back, up, down))
    up, down = hop(*barrier(add(2, up, down)))
    arrived = moves * steps
    blocks = call(
        arrived_kernel,
        shape((ring, arrived, columns), BF16),
        [SMEM, VMEM, ANY],
        [
            pltpu.VMEM((-(-arrived // 16) * 16, wide), BF16),
            pltpu.VMEM(out_weight.shape, BF16),
            pltpu.SemaphoreType.DMA,
        ],
        nbytes=6 << 20,
    )(here, back, out_weight)
    blocks = exchange(blocks, "tp")
    up, down = hop(*barrier(add(1, up, down)))

    placed = call(
        place_kernel,
        shape((slots, steps, columns), BF16),
        [SMEM] + [VMEM] * 3,
        [pltpu.VMEM((tokens, columns), F32)],
        nbytes=4 << 20,
    )(plan, own, up, down)
    return call(
        finish_kernel,
        shape((slots, steps, columns), BF16),
        [SMEM] + [VMEM] * 2,
        [pltpu.VMEM((arrived, columns), F32)],
        nbytes=2 << 20,
    )(here, placed, blocks)


def solution(mesh):
    return jax.shard_map(
        on_device,
        mesh=mesh,
        in_specs=(
            P("group", "tp", None, None),
            P("group", "tp", None, None),
            P("group"),
            P("group"),
            P("group", None),
            P("group", None, "tp"),
            P("group", None, "tp"),
            P("group", None, "tp"),
            P("tp", None),
        ),
        out_specs=P("group", None, "tp"),
        check_vma=False,
    )
```

time: 153 us -> 121 us (0.79)
  the two profiles are of different devices: /device:TPU:102 before, /device:TPU:1 now
where the time goes in v2:
time: 121 us
  starting transfers between devices  38.5 us (32%)
  waiting for transfers between devices  34.3 us (28%)
  Pallas kernels  21.2 us (18%)
  blocking collectives  13.9 us (11%)
  local copies, waits for them, and re-layouts  8.76 us (7%)
  other arithmetic  3.9 us (3%)
    ppermute x8, waiting for transfers between devices, hop(): return (lax.ppermute(u, 'tp', ahead), lax.ppermute(d, 'tp', astern))  34.1 us
    all_to_all x3, starting transfers between devices, exchange(): return lax.all_to_all(x, axis, split_axis=0, concat_axis=0, tiled=True)  21.2 us
    ppermute x8, starting transfers between devices, hop(): return (lax.ppermute(u, 'tp', ahead), lax.ppermute(d, 'tp', astern))  17.3 us
    all_to_all x1, blocking collectives, exchange(): return lax.all_to_all(x, axis, split_axis=0, concat_axis=0, tiled=True)  13.9 us
    unnamed x30, local copies, waits for them, and re-layouts  8.76 us
    pallas_call x1, Pallas kernels, on_device(): call(staying_kernel, [shape((cut, columns), BF16), shape((tokens - cut, c...  8.11 us
    pallas_call x1, Pallas kernels, on_device(): call(arrived_kernel, shape((ring, arrived, columns), BF16), [SMEM, VMEM,...  4.51 us
    pallas_call x1, Pallas kernels, on_device(): call(leaving_kernel, shape((entries, steps, wide), BF16), [SMEM] + [VMEM]...  3.63 us
  transfers between devices with their start and end apart: 11, of which 5 were waited for; matrix products, arithmetic and copies ran while one was open for 1% of the time, Pallas kernels for 11%

profile of v2, /device:TPU:1, one launch (start us, length us, event | category | flops | bytes accessed | tf_op | source)
XLA Modules:
  0.0 120.7 jit_solution(7349455818501015545)
XLA Ops:
  2.8 8.6 %all-to-all-start = ((s32[32,1,128]{2,1,0:T(1,128)}), s32[32,1,128]{2,1,0:T(1,128)S(1)}, u32[]{:S(2)}, u32[]{:S(2)}) async-start(s32[32,1,128]{2,1,0:T(1,128)} %bitcast.4), calls=%async_computation | async-start | bytes 32768 | tf_op jit(solution)/shard_map/all_to_all | solution.py:335
  11.4 1.0 copy-done
  14.3 8.1 %shard_map.92 = (bf16[160,512]{1,0:T(8,128)(2,1)S(1)}, bf16[144,512]{1,0:T(8,128)(2,1)S(1)}, f32[304,512]{1,0:T(8,128)S(1)}, f32[304,512]{1,0:T(8,128)S(1)}, f32...) custom-call(s32[1]{0:T(128)} %bitcast.6.place_ref, ...), custom_call_target="tpu_custom_call" | custom-call | flops 1275068416 | bytes 20971520 | tf_op jit(solution)/shard_map/pallas_call | solution.py:352
  25.6 1.1 shard_map.93
  27.5 7.4 %all-to-all-start.1 = ((bf16[64,4,768]{2,1,0:T(4,128)(2,1)}), bf16[64,4,768]{2,1,0:T(4,128)(2,1)S(1)}, u32[]{:S(2)}, u32[]{:S(2)}) async-start(bf16[64,4,768]{2,1,0:T(4,128)(2,1)} %copy-done.9), calls=%async_computation.1 | async-start | bytes 786432 | tf_op jit(solution)/shard_map/all_to_all | solution.py:335
  34.8 1.7 %collective-permute-start = (bf16[160,512]{1,0:T(8,128)(2,1)S(1)}, bf16[160,512]{1,0:T(8,128)(2,1)S(1)}, u32[]{:S(2)}, u32[]{:S(2)}) collective-permute-start(bf16[160,512]{1,0:T(8,128)(2,1)S(1)} %get-tuple-element.43), channel_id=1, source_target_pairs={{0,1},{1,2},{2,3},{3,4},{4,5},{5,6},{6,7},{7,0},{8,9},{9,10},{10,1... | collective-permute-start | bytes 491528 | tf_op jit(solution)/shard_map/ppermute | solution.py:373
  36.6 4.0 %collective-permute-start.1 = (bf16[144,512]{1,0:T(8,128)(2,1)}, bf16[144,512]{1,0:T(8,128)(2,1)S(1)}, u32[]{:S(2)}, u32[]{:S(2)}) collective-permute-start(bf16[144,512]{1,0:T(8,128)(2,1)} %copy-done.13), channel_id=1, source_target_pairs={{0,7},{1,0},{2,1},{3,2},{4,3},{5,4},{6,5},{7,6},{8,15},{9,8},{10,9... | collective-permute-start | bytes 442376 | tf_op jit(solution)/shard_map/ppermute | solution.py:373
  40.6 3.3 %collective-permute-done.1 = bf16[144,512]{1,0:T(8,128)(2,1)S(1)} collective-permute-done((bf16[144,512]{1,0:T(8,128)(2,1)}, bf16[144,512]{1,0:T(8,128)(2,1)S(1)}, u32[]{:S(2)}, u32[]{:S(2)}) %collective-permute-start.1) | collective-permute-done | bytes 147488 | tf_op jit(solution)/shard_map/ppermute | solution.py:373
  45.1 1.1 add_convert_fusion.4
  46.3 1.1 add_convert_fusion.5
  47.4 1.7 %collective-permute-start.2 = (bf16[304,512]{1,0:T(8,128)(2,1)S(1)}, bf16[304,512]{1,0:T(8,128)(2,1)S(1)}, u32[]{:S(2)}, u32[]{:S(2)}) collective-permute-start(bf16[304,512]{1,0:T(8,128)(2,1)S(1)} %add_convert_fusion.5), channel_id=1, source_target_pairs={{0,1},{1,2},{2,3},{3,4},{4,5},{5,6},{6,7},{7,0},{8,9},{9,10},{10,1... | collective-permute-start | bytes 933896 | tf_op jit(solution)/shard_map/ppermute | solution.py:373
  49.1 4.0 %collective-permute-start.3 = (bf16[304,512]{1,0:T(8,128)(2,1)S(1)}, bf16[304,512]{1,0:T(8,128)(2,1)}, u32[]{:S(2)}, u32[]{:S(2)}) collective-permute-start(bf16[304,512]{1,0:T(8,128)(2,1)S(1)} %add_convert_fusion.4), channel_id=1, source_target_pairs={{0,7},{1,0},{2,1},{3,2},{4,3},{5,4},{6,5},{7,6},{8,15},{9,8},{10,9... | collective-permute-start | bytes 933896 | tf_op jit(solution)/shard_map/ppermute | solution.py:373
  53.2 3.6 %shard_map.94 = bf16[64,4,512]{2,1,0:T(4,128)(2,1)S(1)} custom-call(s32[8,128]{1,0:T(8,128)S(1)} %get-tuple-element.34.plan_ref, bf16[64,4,768]{2,1,0:T(4,128)(2,1)S(1)} %all-to-all-done.1.asked_ref, bf16[128,1,128,128]{3,2,1,0:T(8,128)(2,1)} %keys_ref.3, bf16[128,1,128,128]{3,2,1,0:T(8,128)(2,1)} %values_ref.3), custom_call_target="tpu_custom_call" | custom-call | bytes 8388608 | tf_op jit(solution)/shard_map/pallas_call | solution.py:392
  56.8 13.9 %all_to_all.20.back_ref = bf16[64,4,512]{2,1,0:T(4,128)(2,1)S(1)} all-to-all(bf16[64,4,512]{2,1,0:T(4,128)(2,1)S(1)} %shard_map.94), channel_id=1, replica_groups=mesh['group'=32,'tp'=8] {'group'}, dimensions={0} | all-to-all | bytes 524288 | tf_op jit(solution)/shard_map/all_to_all | solution.py:335
  70.7 4.5 %shard_map.96 = bf16[8,104,512]{2,1,0:T(8,128)(2,1)} custom-call(s32[8,128]{1,0:T(8,128)S(1)} %get-tuple-element.38.here_ref, bf16[64,4,512]{2,1,0:T(4,128)(2,1)S(1)} %all_to_all.20.back_ref, bf16[512,4096]{1,0:T(8,128)(2,1)} %weight_ref.3), custom_call_target="tpu_custom_call" | custom-call | bytes 6291456 | tf_op jit(solution)/shard_map/pallas_call | solution.py:404
  75.2 5.3 %all-to-all-start.3 = ((bf16[8,104,512]{2,1,0:T(8,128)(2,1)}), bf16[8,104,512]{2,1,0:T(8,128)(2,1)S(1)}, u32[]{:S(2)}, u32[]{:S(2)}) async-start(bf16[8,104,512]{2,1,0:T(8,128)(2,1)} %shard_map.96), calls=%async_computation.3 | async-start | bytes 1703936 | tf_op jit(solution)/shard_map/all_to_all | solution.py:335
  80.5 1.4 %add_convert_fusion.2 = (bf16[304,512]{1,0:T(8,128)(2,1)S(1)}, bf16[304,512]{1,0:T(8,128)(2,1)S(1)}) fusion(f32[304,512]{1,0:T(8,128)} %copy-done.2, bf16[304,512]{1,0:T(8,128)(2,1)} %collective-permute-done.3, f32[304,512]{1,0:T(8,128)S(1)} %get-tuple-element.41, bf16[304,512]{1,0:T(8,128)(2,1)} %copy-done.14), kind=kLoop, calls=%fused_computation.2 | loop fusion | flops 933888 | bytes 2490368 | tf_op jit(solution)/shard_map/convert_element_type | solution.py:376
  81.9 1.5 %collective-permute-start.4 = (bf16[304,512]{1,0:T(8,128)(2,1)S(1)}, bf16[304,512]{1,0:T(8,128)(2,1)S(1)}, u32[]{:S(2)}, u32[]{:S(2)}) collective-permute-start(bf16[304,512]{1,0:T(8,128)(2,1)S(1)} %get-tuple-element.55), channel_id=1, source_target_pairs={{0,1},{1,2},{2,3},{3,4},{4,5},{5,6},{6,7},{7,0},{8,9},{9,10},{10,1... | collective-permute-start | bytes 933896 | tf_op jit(solution)/shard_map/ppermute | solution.py:373
  83.5 1.5 %collective-permute-start.5 = (bf16[304,512]{1,0:T(8,128)(2,1)S(1)}, bf16[304,512]{1,0:T(8,128)(2,1)S(1)}, u32[]{:S(2)}, u32[]{:S(2)}) collective-permute-start(bf16[304,512]{1,0:T(8,128)(2,1)S(1)} %get-tuple-element.57), channel_id=1, source_target_pairs={{0,7},{1,0},{2,1},{3,2},{4,3},{5,4},{6,5},{7,6},{8,15},{9,8},{10,9... | collective-permute-start | bytes 933896 | tf_op jit(solution)/shard_map/ppermute | solution.py:373
  85.0 23.7 %collective-permute-done.4 = bf16[304,512]{1,0:T(8,128)(2,1)S(1)} collective-permute-done((bf16[304,512]{1,0:T(8,128)(2,1)S(1)}, bf16[304,512]{1,0:T(8,128)(2,1)S(1)}, u32[]{:S(2)}, u32[]{:S(2)}) %collective-permute-start.4) | collective-permute-done | bytes 311328 | tf_op jit(solution)/shard_map/ppermute | solution.py:373
  108.9 2.7 %collective-permute-start.7 = (bf16[304,512]{1,0:T(8,128)(2,1)S(1)}, bf16[304,512]{1,0:T(8,128)(2,1)S(1)}, u32[]{:S(2)}, u32[]{:S(2)}) collective-permute-start(bf16[304,512]{1,0:T(8,128)(2,1)S(1)} %add_convert_fusion), channel_id=1, source_target_pairs={{0,7},{1,0},{2,1},{3,2},{4,3},{5,4},{6,5},{7,6},{8,15},{9,8},{10,9... | collective-permute-start | bytes 933896 | tf_op jit(solution)/shard_map/ppermute | solution.py:373
  111.6 6.1 %collective-permute-done.6.up_ref = bf16[304,512]{1,0:T(8,128)(2,1)S(1)} collective-permute-done((bf16[304,512]{1,0:T(8,128)(2,1)S(1)}, bf16[304,512]{1,0:T(8,128)(2,1)S(1)}, u32[]{:S(2)}, u32[]{:S(2)}) %collective-permute-start.6) | collective-permute-done | bytes 311328 | tf_op jit(solution)/shard_map/ppermute | solution.py:373
  117.7 1.4 %shard_map.95.placed_ref = bf16[128,4,512]{2,1,0:T(4,128)(2,1)S(1)} custom-call(s32[8,128]{1,0:T(8,128)S(1)} %get-tuple-element.34.plan_ref, f32[304,512]{1,0:T(8,128)S(1)} %get-tuple-element.39.own_ref, bf16[304,512]{1,0:T(8,128)(2,1)S(1)} %collective-permute-done.6.up_ref, bf16[304,512]{1,0:T(8,128)(2,1)S(1)} %collective-permute-done.7.down_ref), custom_call_target="tpu_custom_call" | custom-call | bytes 4194304 | tf_op jit(solution)/shard_map/pallas_call | solution.py:418
  119.1 1.6 %shard_map.97 = bf16[128,4,512]{2,1,0:T(4,128)(2,1)} custom-call(s32[8,128]{1,0:T(8,128)S(1)} %get-tuple-element.38.here_ref, bf16[128,4,512]{2,1,0:T(4,128)(2,1)S(1)} %shard_map.95.placed_ref, bf16[8,104,512]{2,1,0:T(8,128)(2,1)S(1)} %all-to-all-done.3.blocks_ref), custom_call_target="tpu_custom_call" | custom-call | bytes 2097152 | tf_op jit(solution)/shard_map/pallas_call | solution.py:425
  (41 shorter events, 10.1 us)
Async XLA Ops:
  0.0 0.7 copy-start.10
  1.3 0.7 copy-start.12
  2.8 22.8 %all-to-all-start = ((s32[32,1,128]{2,1,0:T(1,128)}), s32[32,1,128]{2,1,0:T(1,128)S(1)}, u32[]{:S(2)}, u32[]{:S(2)}) async-start(s32[32,1,128]{2,1,0:T(1,128)} %bitcast.4), calls=%async_computation | async-start | bytes 32768 | tf_op jit(solution)/shard_map/all_to_all | solution.py:335
  11.4 1.0 copy-start
  12.5 0.9 copy-start.5
  13.4 0.9 copy-start.7
  14.3 11.3 %copy-start.1 = (bf16[128,4,512]{2,1,0:T(4,128)(2,1)S(1)}, bf16[128,4,512]{2,1,0:T(4,128)(2,1)}, u32[]{:S(2)}) copy-start(bf16[128,4,512]{2,1,0:T(4,128)(2,1)} %query_ref.3) | copy-start | bytes 1572868
  14.3 11.3 %copy-start.6 = (bf16[128,4,128]{2,1,0:T(4,128)(2,1)S(1)}, bf16[128,4,128]{2,1,0:T(4,128)(2,1)}, u32[]{:S(2)}) copy-start(bf16[128,4,128]{2,1,0:T(4,128)(2,1)} %key_ref.3) | copy-start | bytes 393220
  14.3 11.3 %copy-start.8 = (bf16[128,4,128]{2,1,0:T(4,128)(2,1)S(1)}, bf16[128,4,128]{2,1,0:T(4,128)(2,1)}, u32[]{:S(2)}) copy-start(bf16[128,4,128]{2,1,0:T(4,128)(2,1)} %value_ref.3) | copy-start | bytes 393220
  22.4 0.8 copy-start.2
  23.2 0.9 copy-start.3
  24.1 0.8 copy-start.4
  26.7 0.7 copy-start.9
  27.5 17.7 %all-to-all-start.1 = ((bf16[64,4,768]{2,1,0:T(4,128)(2,1)}), bf16[64,4,768]{2,1,0:T(4,128)(2,1)S(1)}, u32[]{:S(2)}, u32[]{:S(2)}) async-start(bf16[64,4,768]{2,1,0:T(4,128)(2,1)} %copy-done.9), calls=%async_computation.1 | async-start | bytes 786432 | tf_op jit(solution)/shard_map/all_to_all | solution.py:335
  34.8 10.1 %collective-permute-start = (bf16[160,512]{1,0:T(8,128)(2,1)S(1)}, bf16[160,512]{1,0:T(8,128)(2,1)S(1)}, u32[]{:S(2)}, u32[]{:S(2)}) collective-permute-start(bf16[160,512]{1,0:T(8,128)(2,1)S(1)} %get-tuple-element.43), channel_id=1, source_target_pairs={{0,1},{1,2},{2,3},{3,4},{4,5},{5,6},{6,7},{7,0},{8,9},{9,10},{10,1... | collective-permute-start | bytes 491528 | tf_op jit(solution)/shard_map/ppermute | solution.py:373
  36.6 7.4 %collective-permute-start.1 = (bf16[144,512]{1,0:T(8,128)(2,1)}, bf16[144,512]{1,0:T(8,128)(2,1)S(1)}, u32[]{:S(2)}, u32[]{:S(2)}) collective-permute-start(bf16[144,512]{1,0:T(8,128)(2,1)} %copy-done.13), channel_id=1, source_target_pairs={{0,7},{1,0},{2,1},{3,2},{4,3},{5,4},{6,5},{7,6},{8,15},{9,8},{10,9... | collective-permute-start | bytes 442376 | tf_op jit(solution)/shard_map/ppermute | solution.py:373
  47.4 23.3 %collective-permute-start.2 = (bf16[304,512]{1,0:T(8,128)(2,1)S(1)}, bf16[304,512]{1,0:T(8,128)(2,1)S(1)}, u32[]{:S(2)}, u32[]{:S(2)}) collective-permute-start(bf16[304,512]{1,0:T(8,128)(2,1)S(1)} %add_convert_fusion.5), channel_id=1, source_target_pairs={{0,1},{1,2},{2,3},{3,4},{4,5},{5,6},{6,7},{7,0},{8,9},{9,10},{10,1... | collective-permute-start | bytes 933896 | tf_op jit(solution)/shard_map/ppermute | solution.py:373
  49.1 21.6 %collective-permute-start.3 = (bf16[304,512]{1,0:T(8,128)(2,1)S(1)}, bf16[304,512]{1,0:T(8,128)(2,1)}, u32[]{:S(2)}, u32[]{:S(2)}) collective-permute-start(bf16[304,512]{1,0:T(8,128)(2,1)S(1)} %add_convert_fusion.4), channel_id=1, source_target_pairs={{0,7},{1,0},{2,1},{3,2},{4,3},{5,4},{6,5},{7,6},{8,15},{9,8},{10,9... | collective-permute-start | bytes 933896 | tf_op jit(solution)/shard_map/ppermute | solution.py:373
  70.7 4.5 %copy-start.14 = (bf16[304,512]{1,0:T(8,128)(2,1)}, bf16[304,512]{1,0:T(8,128)(2,1)S(1)}, u32[]{:S(2)}) copy-start(bf16[304,512]{1,0:T(8,128)(2,1)S(1)} %collective-permute-done.2) | copy-start | bytes 933892
  75.2 43.9 %all-to-all-start.3 = ((bf16[8,104,512]{2,1,0:T(8,128)(2,1)}), bf16[8,104,512]{2,1,0:T(8,128)(2,1)S(1)}, u32[]{:S(2)}, u32[]{:S(2)}) async-start(bf16[8,104,512]{2,1,0:T(8,128)(2,1)} %shard_map.96), calls=%async_computation.3 | async-start | bytes 1703936 | tf_op jit(solution)/shard_map/all_to_all | solution.py:335
  81.9 26.7 %collective-permute-start.4 = (bf16[304,512]{1,0:T(8,128)(2,1)S(1)}, bf16[304,512]{1,0:T(8,128)(2,1)S(1)}, u32[]{:S(2)}, u32[]{:S(2)}) collective-permute-start(bf16[304,512]{1,0:T(8,128)(2,1)S(1)} %get-tuple-element.55), channel_id=1, source_target_pairs={{0,1},{1,2},{2,3},{3,4},{4,5},{5,6},{6,7},{7,0},{8,9},{9,10},{10,1... | collective-permute-start | bytes 933896 | tf_op jit(solution)/shard_map/ppermute | solution.py:373
  83.5 25.2 %collective-permute-start.5 = (bf16[304,512]{1,0:T(8,128)(2,1)S(1)}, bf16[304,512]{1,0:T(8,128)(2,1)S(1)}, u32[]{:S(2)}, u32[]{:S(2)}) collective-permute-start(bf16[304,512]{1,0:T(8,128)(2,1)S(1)} %get-tuple-element.57), channel_id=1, source_target_pairs={{0,7},{1,0},{2,1},{3,2},{4,3},{5,4},{6,5},{7,6},{8,15},{9,8},{10,9... | collective-permute-start | bytes 933896 | tf_op jit(solution)/shard_map/ppermute | solution.py:373
  108.8 8.8 %collective-permute-start.6 = (bf16[304,512]{1,0:T(8,128)(2,1)S(1)}, bf16[304,512]{1,0:T(8,128)(2,1)S(1)}, u32[]{:S(2)}, u32[]{:S(2)}) collective-permute-start(bf16[304,512]{1,0:T(8,128)(2,1)S(1)} %add_convert_fusion.1), channel_id=1, source_target_pairs={{0,1},{1,2},{2,3},{3,4},{4,5},{5,6},{6,7},{7,0},{8,9},{9,10},{10,1... | collective-permute-start | bytes 933896 | tf_op jit(solution)/shard_map/ppermute | solution.py:373
  108.9 8.7 %collective-permute-start.7 = (bf16[304,512]{1,0:T(8,128)(2,1)S(1)}, bf16[304,512]{1,0:T(8,128)(2,1)S(1)}, u32[]{:S(2)}, u32[]{:S(2)}) collective-permute-start(bf16[304,512]{1,0:T(8,128)(2,1)S(1)} %add_convert_fusion), channel_id=1, source_target_pairs={{0,7},{1,0},{2,1},{3,2},{4,3},{5,4},{6,5},{7,6},{8,15},{9,8},{10,9... | collective-permute-start | bytes 933896 | tf_op jit(solution)/shard_map/ppermute | solution.py:373
  (2 other events, 1.3 us)

commit v3 on v2

--- a/solution.py
+++ b/solution.py
@@ -16,7 +16,7 @@
 ANY = pl.BlockSpec(memory_space=pltpu.HBM)
 
 
-def call(kernel, out_shape, in_specs, scratch=(), flops=0, nbytes=0, exps=0, limit=32):
+def call(kernel, out_shape, in_specs, scratch=(), flops=0, nbytes=0, exps=0, limit=8):
     single = isinstance(out_shape, jax.ShapeDtypeStruct)
     return pl.pallas_call(
         kernel,
@@ -47,7 +47,17 @@
     return jnp.sum(jnp.where(lanes(n, n) == lines_of(n, n), row, 0.0), axis=1, keepdims=True)
 
 
-def plan_kernel(moves_ref, flags_ref, lengths_ref, table_ref, plan_ref):
+def plan_kernel(moves_hbm, flags_hbm, lengths_hbm, table_ref, plan_ref, moves_ref, flags_ref, lengths_ref, sem):
+    copies = [
+        pltpu.make_async_copy(src, dst, sem.at[i])
+        for i, (src, dst) in enumerate(
+            ((moves_hbm, moves_ref), (flags_hbm, flags_ref), (lengths_hbm, lengths_ref))
+        )
+    ]
+    for copy in copies:
+        copy.start()
+    for copy in copies:
+        copy.wait()
     groups, wide = table_ref.shape
     moves, slots = moves_ref.shape[1], flags_ref.shape[1]
     source, target = moves_ref[0:1, :], moves_ref[1:2, :]
@@ -86,13 +96,9 @@
 HERE_ENTRY, HERE_SLOT = range(2)
 
 
-def payload_kernel(slot_ref, table_ref, query_ref, key_ref, value_ref, out_ref, here_ref):
-    wide, narrow = query_ref.shape[2], key_ref.shape[2]
+def payload_kernel(slot_ref, table_ref, fresh_ref, out_ref, here_ref):
     for e in range(out_ref.shape[0]):
-        slot = jnp.maximum(slot_ref[e // CAP, e % CAP] - 1, 0)
-        out_ref[e, :, 0:wide] = query_ref[slot]
-        out_ref[e, :, wide : wide + narrow] = key_ref[slot]
-        out_ref[e, :, wide + narrow : wide + 2 * narrow] = value_ref[slot]
+        out_ref[e] = fresh_ref[jnp.maximum(slot_ref[e // CAP, e % CAP] - 1, 0)]
     groups, width = table_ref.shape
     table = table_ref[...]
     there = (table > 0).astype(F32)
@@ -176,12 +182,17 @@
     place_ref, plan_ref, query_ref, key_ref, value_ref, keys_ref, values_ref, weight_ref,
     up_ref, down_ref, own_ref, *rest,
 ):
-    terms_refs, (kbuf, vbuf, score, weight, heads, wbuf, ksem, vsem, wsem) = rest[:6], rest[6:]
+    terms_refs, fresh_ref = rest[:6], rest[6]
+    kbuf, vbuf, score, weight, heads, wbuf, fsem, ksem, vsem, wsem = rest[7:]
     steps, wide = query_ref.shape[1:]
     slots, _, cache, head = keys_ref.shape
     tokens = heads.shape[0]
     ring, columns = 8, up_ref.shape[1]
-    loads = [
+    fresh = [
+        pltpu.make_async_copy(src, fresh_ref.at[:, :, pl.ds(at, src.shape[2])], fsem.at[i])
+        for i, (src, at) in enumerate(((query_ref, 0), (key_ref, wide), (value_ref, wide + head)))
+    ]
+    keys, values = (
         [
             pltpu.make_async_copy(
                 ref.at[pl.ds(c * 32, 32), 0], buf.at[pl.ds(c * 32, 32), pl.ds(0, cache)], sem.at[c]
@@ -189,11 +200,17 @@
             for c in range(slots // 32)
         ]
         for ref, buf, sem in ((keys_ref, kbuf, ksem), (values_ref, vbuf, vsem))
-    ]
-    for copy in loads[0] + loads[1]:
+    )
+    order = (4, 3, 5, 2, 6, 1, 7, 0)
+
+    def part(k):
+        at = lax.rem(place_ref[0] + k, ring) * columns
+        return pl.ds(pl.multiple_of(at, columns), columns)
+
+    parts = [pltpu.make_async_copy(weight_ref.at[:, part(k)], wbuf.at[j], wsem.at[j]) for j, k in enumerate(order)]
+    for copy in fresh + keys + values + parts:
         copy.start()
-    load = pltpu.make_async_copy(weight_ref, wbuf, wsem)
-    load.start()
+
     def put(b, mixed):
         quads = len(mixed) // 4
         for j in range(quads):
@@ -206,31 +223,29 @@
     def slot(i):
         return plan_ref[STAY_SLOT, i]
 
+    for copy in fresh:
+        copy.wait()
     attend(
         tokens // steps, STAY_BATCH, kbuf, vbuf, score, weight, cache, steps, wide // head,
         slot,
-        lambda i: query_ref[slot(i)],
-        lambda i: (key_ref[slot(i)], value_ref[slot(i)]),
+        lambda i: fresh_ref[slot(i), :, 0:wide],
+        lambda i: (fresh_ref[slot(i), :, wide : wide + head], fresh_ref[slot(i), :, wide + head : wide + 2 * head]),
         lambda i: plan_ref[STAY_LENGTH, i],
-        lambda: [copy.wait() for copy in loads[0]],
-        lambda: [copy.wait() for copy in loads[1]],
+        lambda: [copy.wait() for copy in keys],
+        lambda: [copy.wait() for copy in values],
         put,
     )
-    load.wait()
-
-    def block(k):
-        at = lax.rem(place_ref[0] + k, ring) * columns
-        return jnp.dot(
-            heads[...], wbuf[:, pl.ds(pl.multiple_of(at, columns), columns)], preferred_element_type=F32
-        )
-
-    far = block(ring // 2)
     cut = up_ref.shape[0]
-    up_ref[...] = far[:cut].astype(BF16)
-    down_ref[...] = far[cut:].astype(BF16)
-    own_ref[...] = block(0)
-    for k, ref in zip((1, 2, 3, 5, 6, 7), terms_refs):
-        ref[...] = block(k)
+    for j, k in enumerate(order):
+        parts[j].wait()
+        block = jnp.dot(heads[...], wbuf[j], preferred_element_type=F32)
+        if k == ring // 2:
+            up_ref[...] = block[:cut].astype(BF16)
+            down_ref[...] = block[cut:].astype(BF16)
+        elif k == 0:
+            own_ref[...] = block
+        else:
+            terms_refs[k - 1 if k < 4 else k - 2][...] = block.astype(BF16)
 
 
 def leaving_kernel(plan_ref, asked_ref, keys_ref, values_ref, out_ref, kbuf, vbuf, score, weight, ksem, vsem):
@@ -269,16 +284,20 @@
 
 
 def arrived_kernel(here_ref, back_ref, weight_ref, out_ref, heads, wbuf, wsem):
-    load = pltpu.make_async_copy(weight_ref, wbuf, wsem)
-    load.start()
     steps = back_ref.shape[1]
     rows, columns = out_ref.shape[1] // steps, out_ref.shape[2]
+    parts = [
+        pltpu.make_async_copy(weight_ref.at[:, pl.ds(k * columns, columns)], wbuf.at[k], wsem.at[k])
+        for k in range(out_ref.shape[0])
+    ]
+    for copy in parts:
+        copy.start()
     for j in range(heads.shape[0] // 16):
         four = [back_ref[here_ref[HERE_ENTRY, min(4 * j + u, rows - 1)]].astype(F32) for u in range(4)]
         heads[16 * j : 16 * j + 16, :] = jnp.concatenate(four, axis=0).astype(BF16)
-    load.wait()
-    for k in range(out_ref.shape[0]):
-        terms = jnp.dot(heads[...], wbuf[:, k * columns : (k + 1) * columns], preferred_element_type=F32)
+    for k, copy in enumerate(parts):
+        copy.wait()
+        terms = jnp.dot(heads[...], wbuf[k], preferred_element_type=F32)
         out_ref[k] = terms[: out_ref.shape[1]].astype(BF16)
 
 
@@ -327,8 +346,12 @@
     positions = cache + FRESH
     place = lax.axis_index("tp").astype(I32).reshape(1)
     barrier = lax.optimization_barrier
-    keys_cache, values_cache, out_weight = (
-        pltpu.with_memory_space_constraint(x, pltpu.HBM) for x in (keys_cache, values_cache, out_weight)
+    keys_cache, values_cache, out_weight, queries, new_keys, new_values, moves_t, flags, reach = (
+        pltpu.with_memory_space_constraint(x, pltpu.HBM)
+        for x in (
+            keys_cache, values_cache, out_weight, queries, new_keys, new_values,
+            migrations.T, guard_flags.reshape(1, slots), lengths.reshape(1, slots),
+        )
     )
 
     def exchange(x, axis):
@@ -342,29 +365,43 @@
             pltpu.VMEM((rows * lines, positions), BF16),
         ]
 
-    table, plan = call(plan_kernel, [shape((groups, 128), I32), shape((8, slots), I32)], [VMEM] * 3, nbytes=1 << 16)(
-        migrations.T, guard_flags.reshape(1, slots), lengths.reshape(1, slots)
-    )
+    table, plan = call(
+        plan_kernel,
+        [shape((groups, 128), I32), shape((8, slots), I32)],
+        [ANY] * 3,
+        [
+            pltpu.VMEM((3, moves), I32),
+            pltpu.VMEM((1, slots), I32),
+            pltpu.VMEM((1, slots), I32),
+            pltpu.SemaphoreType.DMA((3,)),
+        ],
+        nbytes=1 << 16,
+    )(moves_t, flags, reach)
     table = exchange(table.reshape(groups, 1, 128), "group").reshape(groups, 128)
 
     tokens = staying * steps
     cut = -(-tokens // 32) * 16
     up, down, own, *terms = call(
         staying_kernel,
-        [shape((cut, columns), BF16), shape((tokens - cut, columns), BF16)] + [shape((tokens, columns), F32)] * 7,
-        [SMEM] * 2 + [VMEM] * 3 + [ANY] * 3,
+        [shape((cut, columns), BF16), shape((tokens - cut, columns), BF16), shape((tokens, columns), F32)]
+        + [shape((tokens, columns), BF16)] * 6
+        + [shape((slots, steps, wide + 2 * head), BF16)],
+        [SMEM] * 2 + [ANY] * 6,
         scratch(slots, staying)
         + [
             pltpu.VMEM((tokens, wide), BF16),
-            pltpu.VMEM(out_weight.shape, BF16),
+            pltpu.VMEM((ring, wide, columns), BF16),
+            pltpu.SemaphoreType.DMA((3,)),
             pltpu.SemaphoreType.DMA((slots // 32,)),
             pltpu.SemaphoreType.DMA((slots // 32,)),
-            pltpu.SemaphoreType.DMA,
+            pltpu.SemaphoreType.DMA((ring,)),
         ],
         flops=2 * tokens * wide * out_weight.shape[1],
         nbytes=20 << 20,
         exps=tokens * positions * 4,
+        limit=32,
     )(place, plan, queries, new_keys, new_values, keys_cache, values_cache, out_weight)
+    fresh = terms.pop()
 
     ahead = [(i, (i + 1) % ring) for i in range(ring)]
     astern = [(i, (i - 1) % ring) for i in range(ring)]
@@ -373,22 +410,25 @@
         return lax.ppermute(u, "tp", ahead), lax.ppermute(d, "tp", astern)
 
     def add(k, u, d):
-        return (terms[k - 1] + u.astype(F32)).astype(BF16), (terms[6 - k] + d.astype(F32)).astype(BF16)
-
-    table, up, down = barrier((table, up, down))
-    up, down = hop(up, down)
+        return (
+            (terms[k - 1].astype(F32) + u.astype(F32)).astype(BF16),
+            (terms[6 - k].astype(F32) + d.astype(F32)).astype(BF16),
+        )
+
+    table, up, down, fresh = barrier((table, up, down, fresh))
     asked, here = call(
         payload_kernel,
         [shape((entries, steps, wide + 2 * head), BF16), shape((8, 128), I32)],
-        [SMEM] + [VMEM] * 4,
+        [SMEM] + [VMEM] * 2,
         nbytes=2 << 20,
-    )(table, table, queries, new_keys, new_values)
+    )(table, table, fresh)
     asked = exchange(asked, "group")
-
-    asked, up, down = barrier((asked, up, down))
+    up, down = hop(up, down)
     up = jnp.concatenate([up, jnp.zeros((tokens - cut, columns), BF16)], axis=0)
     down = jnp.concatenate([jnp.zeros((cut, columns), BF16), down], axis=0)
-    up, down = hop(*barrier(add(3, up, down)))
+
+    asked, up, down = barrier((asked, *add(3, up, down)))
+    up, down = hop(up, down)
     back = call(
         leaving_kernel,
         shape((entries, steps, wide), BF16),
@@ -397,9 +437,8 @@
         nbytes=8 << 20,
     )(plan, asked, keys_cache, values_cache)
     back = exchange(back, "group")
-
-    back, up, down = barrier((back, up, down))
-    up, down = hop(*barrier(add(2, up, down)))
+    back, up, down = barrier((back, *add(2, up, down)))
+    up, down = hop(up, down)
     arrived = moves * steps
     blocks = call(
         arrived_kernel,
@@ -407,13 +446,15 @@
         [SMEM, VMEM, ANY],
         [
             pltpu.VMEM((-(-arrived // 16) * 16, wide), BF16),
-            pltpu.VMEM(out_weight.shape, BF16),
-            pltpu.SemaphoreType.DMA,
+            pltpu.VMEM((ring, wide, columns), BF16),
+            pltpu.SemaphoreType.DMA((ring,)),
         ],
         nbytes=6 << 20,
+        limit=12,
     )(here, back, out_weight)
+    blocks, up, down = barrier((blocks, *add(1, up, down)))
     blocks = exchange(blocks, "tp")
-    up, down = hop(*barrier(add(1, up, down)))
+    up, down = hop(up, down)
 
     placed = call(
         place_kernel,

time: 121 us -> 114 us (0.942)
  blocking collectives: 13.9 us -> 0 us
  waiting for transfers between devices: 34.3 us -> 44.1 us
  local copies, waits for them, and re-layouts: 8.76 us -> 0.66 us
  Pallas kernels: 21.2 us -> 25.8 us
    all_to_all x1 -> x0, blocking collectives: 13.9 us -> none  [exchange(): return lax.all_to_all(x, axis, split_axis=0, concat_axis=0, tiled=True)]
    all_to_all x3 -> x4, waiting for transfers between devices: 0.23 us -> 10.3 us  [exchange(): return lax.all_to_all(x, axis, split_axis=0, concat_axis=0, tiled=True)]
    unnamed x30 -> x10, local copies, waits for them, and re-layouts: 8.76 us -> 0.66 us
    all_to_all x3 -> x4, starting transfers between devices: 21.2 us -> 25.1 us  [exchange(): return lax.all_to_all(x, axis, split_axis=0, concat_axis=0, tiled=True)]
    ppermute x8, starting transfers between devices: 17.3 us -> 13.8 us  [hop(): return (lax.ppermute(u, 'tp', ahead), lax.ppermute(d, 'tp', astern))]
    pallas_call x1, Pallas kernels: 8.11 us -> 10.7 us  [on_device(): call(staying_kernel, [shape((cut, columns), BF16), shape((tokens - cut, c...]
    convert_element_type x5 -> x6, other arithmetic: 3.9 us -> 3.26 us  [the longest x3 2.08 us: add(): (terms[6 - k].astype(F32) + d.astype(F32)).astype(BF16)]
  transfers between devices with their start and end apart: 11 -> 12, of which waited for: 5 -> 5; matrix products, arithmetic and copies ran while one was open for 1% -> 3% of each run, Pallas kernels for 11% -> 20%
where the time goes in v3:
time: 114 us; the launch traced here: 113 us
  waiting for transfers between devices  44.1 us (39%)
  starting transfers between devices  38.9 us (34%)
  Pallas kernels  25.8 us (23%)
  other arithmetic  3.26 us (3%)
    ppermute x8, waiting for transfers between devices, hop(): return (lax.ppermute(u, 'tp', ahead), lax.ppermute(d, 'tp', astern))  33.9 us
    all_to_all x4, starting transfers between devices, exchange(): return lax.all_to_all(x, axis, split_axis=0, concat_axis=0, tiled=True)  25.1 us
    ppermute x8, starting transfers between devices, hop(): return (lax.ppermute(u, 'tp', ahead), lax.ppermute(d, 'tp', astern))  13.8 us
    pallas_call x1, Pallas kernels, on_device(): call(staying_kernel, [shape((cut, columns), BF16), shape((tokens - cut, c...  10.7 us
    all_to_all x4, waiting for transfers between devices, exchange(): return lax.all_to_all(x, axis, split_axis=0, concat_axis=0, tiled=True)  10.3 us
    pallas_call x1, Pallas kernels, on_device(): call(arrived_kernel, shape((ring, arrived, columns), BF16), [SMEM, VMEM,...  4.44 us
    pallas_call x1, Pallas kernels, on_device(): call(leaving_kernel, shape((entries, steps, wide), BF16), [SMEM] + [VMEM]...  4.33 us
  transfers between devices with their start and end apart: 12, of which 5 were waited for; matrix products, arithmetic and copies ran while one was open for 3% of the time, Pallas kernels for 20%

profile of v3, /device:TPU:1, one launch (start us, length us, event | category | flops | bytes accessed | tf_op | source)
XLA Modules:
  0.0 112.9 jit_solution(10438754230633835492)
XLA Ops:
  0.0 1.5 %shard_map.91 = (s32[32,128]{1,0:T(8,128)}, s32[8,128]{1,0:T(8,128)S(1)}) custom-call(s32[3,26]{1,0:T(4,128)} %bitcast.10, s32[1,128]{1,0:T(1,128)} %bitcast.11, s32[1,128]{1,0:T(1,128)} %bitcast.12), custom_call_target="tpu_custom_call" | custom-call | bytes 65536 | tf_op jit(solution)/shard_map/pallas_call | solution.py:368
  1.6 8.6 %all-to-all-start = ((s32[32,1,128]{2,1,0:T(1,128)}), s32[32,1,128]{2,1,0:T(1,128)S(1)}, u32[]{:S(2)}, u32[]{:S(2)}) async-start(s32[32,1,128]{2,1,0:T(1,128)} %bitcast.4), calls=%async_computation | async-start | bytes 32768 | tf_op jit(solution)/shard_map/all_to_all | solution.py:358
  10.2 10.7 %shard_map.92 = (bf16[160,512]{1,0:T(8,128)(2,1)S(1)}, bf16[144,512]{1,0:T(8,128)(2,1)S(1)}, f32[304,512]{1,0:T(8,128)S(1)}, bf16[304,512]{1,0:T(8,128)(2,1)S(1)...) custom-call(s32[1]{0:T(128)} %bitcast.6.place_ref, ...), custom_call_target="tpu_custom_call" | custom-call | flops 1275068416 | bytes 20971520 | tf_op jit(solution)/shard_map/pallas_call | solution.py:384
  21.5 5.6 %collective-permute-start.1 = (bf16[144,512]{1,0:T(8,128)(2,1)}, bf16[144,512]{1,0:T(8,128)(2,1)}, u32[]{:S(2)}, u32[]{:S(2)}) collective-permute-start(bf16[144,512]{1,0:T(8,128)(2,1)} %copy-done.4), channel_id=1, source_target_pairs={{0,7},{1,0},{2,1},{3,2},{4,3},{5,4},{6,5},{7,6},{8,15},{9,8},{10,9... | collective-permute-start | bytes 442376 | tf_op jit(solution)/shard_map/ppermute | solution.py:410
  27.1 1.8 %shard_map.93 = (bf16[64,4,768]{2,1,0:T(4,128)(2,1)}, s32[8,128]{1,0:T(8,128)S(1)}) custom-call(s32[32,128]{1,0:T(8,128)S(1)} %bitcast.8, s32[32,128]{1,0:T(8,128)S(1)} %bitcast.9, bf16[128,4,768]{2,1,0:T(4,128)(2,1)S(1)} %get-tuple-element.38.fresh_ref), custom_call_target="tpu_custom_call" | custom-call | bytes 2097152 | tf_op jit(solution)/shard_map/pallas_call | solution.py:419
  28.9 7.7 %all-to-all-start.1 = ((bf16[64,4,768]{2,1,0:T(4,128)(2,1)}), bf16[64,4,768]{2,1,0:T(4,128)(2,1)S(1)}, u32[]{:S(2)}, u32[]{:S(2)}) async-start(bf16[64,4,768]{2,1,0:T(4,128)(2,1)} %get-tuple-element.41), calls=%async_computation.1 | async-start | bytes 786432 | tf_op jit(solution)/shard_map/all_to_all | solution.py:358
  36.6 0.9 add_convert_fusion.4
  37.6 5.8 %collective-permute-done = bf16[160,512]{1,0:T(8,128)(2,1)S(1)} collective-permute-done((bf16[160,512]{1,0:T(8,128)(2,1)S(1)}, bf16[160,512]{1,0:T(8,128)(2,1)S(1)}, u32[]{:S(2)}, u32[]{:S(2)}) %collective-permute-start) | collective-permute-done | bytes 163872 | tf_op jit(solution)/shard_map/ppermute | solution.py:410
  43.4 3.4 %all-to-all-done.1.asked_ref = bf16[64,4,768]{2,1,0:T(4,128)(2,1)S(1)} async-done(((bf16[64,4,768]{2,1,0:T(4,128)(2,1)}), bf16[64,4,768]{2,1,0:T(4,128)(2,1)S(1)}, u32[]{:S(2)}, u32[]{:S(2)}) %all-to-all-start.1) | async-done | bytes 393248 | tf_op jit(solution)/shard_map/all_to_all | solution.py:358
  46.8 2.7 %collective-permute-start.3 = (bf16[304,512]{1,0:T(8,128)(2,1)S(1)}, bf16[304,512]{1,0:T(8,128)(2,1)}, u32[]{:S(2)}, u32[]{:S(2)}) collective-permute-start(bf16[304,512]{1,0:T(8,128)(2,1)S(1)} %add_convert_fusion.4), channel_id=1, source_target_pairs={{0,7},{1,0},{2,1},{3,2},{4,3},{5,4},{6,5},{7,6},{8,15},{9,8},{10,9... | collective-permute-start | bytes 933896 | tf_op jit(solution)/shard_map/ppermute | solution.py:410
  49.5 4.3 %shard_map.94 = bf16[64,4,512]{2,1,0:T(4,128)(2,1)} custom-call(s32[8,128]{1,0:T(8,128)S(1)} %get-tuple-element.33.plan_ref, bf16[64,4,768]{2,1,0:T(4,128)(2,1)S(1)} %all-to-all-done.1.asked_ref, bf16[128,1,128,128]{3,2,1,0:T(8,128)(2,1)} %keys_ref.3, bf16[128,1,128,128]{3,2,1,0:T(8,128)(2,1)} %values_ref.3), custom_call_target="tpu_custom_call" | custom-call | bytes 8388608 | tf_op jit(solution)/shard_map/pallas_call | solution.py:432
  53.9 5.3 %all-to-all-start.2 = ((bf16[64,4,512]{2,1,0:T(4,128)(2,1)}), bf16[64,4,512]{2,1,0:T(4,128)(2,1)S(1)}, u32[]{:S(2)}, u32[]{:S(2)}) async-start(bf16[64,4,512]{2,1,0:T(4,128)(2,1)} %shard_map.94), calls=%async_computation.2 | async-start | bytes 524288 | tf_op jit(solution)/shard_map/all_to_all | solution.py:358
  59.2 1.1 add_convert_fusion.3
  60.3 1.1 add_convert_fusion.2
  61.3 6.9 %all-to-all-done.2.back_ref = bf16[64,4,512]{2,1,0:T(4,128)(2,1)S(1)} async-done(((bf16[64,4,512]{2,1,0:T(4,128)(2,1)}), bf16[64,4,512]{2,1,0:T(4,128)(2,1)S(1)}, u32[]{:S(2)}, u32[]{:S(2)}) %all-to-all-start.2) | async-done | bytes 262176 | tf_op jit(solution)/shard_map/all_to_all | solution.py:358
  68.2 2.7 %collective-permute-start.5 = (bf16[304,512]{1,0:T(8,128)(2,1)S(1)}, bf16[304,512]{1,0:T(8,128)(2,1)S(1)}, u32[]{:S(2)}, u32[]{:S(2)}) collective-permute-start(bf16[304,512]{1,0:T(8,128)(2,1)S(1)} %add_convert_fusion.2), channel_id=1, source_target_pairs={{0,7},{1,0},{2,1},{3,2},{4,3},{5,4},{6,5},{7,6},{8,15},{9,8},{10,9... | collective-permute-start | bytes 933896 | tf_op jit(solution)/shard_map/ppermute | solution.py:410
  70.9 4.4 %shard_map.95 = bf16[8,104,512]{2,1,0:T(8,128)(2,1)} custom-call(s32[8,128]{1,0:T(8,128)S(1)} %get-tuple-element.39.here_ref, bf16[64,4,512]{2,1,0:T(4,128)(2,1)S(1)} %all-to-all-done.2.back_ref, bf16[512,4096]{1,0:T(8,128)(2,1)} %weight_ref.3), custom_call_target="tpu_custom_call" | custom-call | bytes 6291456 | tf_op jit(solution)/shard_map/pallas_call | solution.py:443
  75.3 2.8 %collective-permute-done.4 = bf16[304,512]{1,0:T(8,128)(2,1)S(1)} collective-permute-done((bf16[304,512]{1,0:T(8,128)(2,1)S(1)}, bf16[304,512]{1,0:T(8,128)(2,1)S(1)}, u32[]{:S(2)}, u32[]{:S(2)}) %collective-permute-start.4) | collective-permute-done | bytes 311328 | tf_op jit(solution)/shard_map/ppermute | solution.py:410
  78.3 3.6 %all-to-all-start.3 = ((bf16[8,104,512]{2,1,0:T(8,128)(2,1)}), bf16[8,104,512]{2,1,0:T(8,128)(2,1)S(1)}, u32[]{:S(2)}, u32[]{:S(2)}) async-start(bf16[8,104,512]{2,1,0:T(8,128)(2,1)} %shard_map.95), calls=%async_computation.3 | async-start | bytes 1703936 | tf_op jit(solution)/shard_map/all_to_all | solution.py:358
  81.9 1.4 %collective-permute-start.6 = (bf16[304,512]{1,0:T(8,128)(2,1)S(1)}, bf16[304,512]{1,0:T(8,128)(2,1)S(1)}, u32[]{:S(2)}, u32[]{:S(2)}) collective-permute-start(bf16[304,512]{1,0:T(8,128)(2,1)S(1)} %add_convert_fusion.1), channel_id=1, source_target_pairs={{0,1},{1,2},{2,3},{3,4},{4,5},{5,6},{6,7},{7,0},{8,9},{9,10},{10,1... | collective-permute-start | bytes 933896 | tf_op jit(solution)/shard_map/ppermute | solution.py:410
  83.4 1.3 %collective-permute-start.7 = (bf16[304,512]{1,0:T(8,128)(2,1)S(1)}, bf16[304,512]{1,0:T(8,128)(2,1)S(1)}, u32[]{:S(2)}, u32[]{:S(2)}) collective-permute-start(bf16[304,512]{1,0:T(8,128)(2,1)S(1)} %add_convert_fusion), channel_id=1, source_target_pairs={{0,7},{1,0},{2,1},{3,2},{4,3},{5,4},{6,5},{7,6},{8,15},{9,8},{10,9... | collective-permute-start | bytes 933896 | tf_op jit(solution)/shard_map/ppermute | solution.py:410
  84.7 25.2 %collective-permute-done.6.up_ref = bf16[304,512]{1,0:T(8,128)(2,1)S(1)} collective-permute-done((bf16[304,512]{1,0:T(8,128)(2,1)S(1)}, bf16[304,512]{1,0:T(8,128)(2,1)S(1)}, u32[]{:S(2)}, u32[]{:S(2)}) %collective-permute-start.6) | collective-permute-done | bytes 311328 | tf_op jit(solution)/shard_map/ppermute | solution.py:410
  109.9 1.4 %shard_map.96.placed_ref = bf16[128,4,512]{2,1,0:T(4,128)(2,1)S(1)} custom-call(s32[8,128]{1,0:T(8,128)S(1)} %copy-done.1, f32[304,512]{1,0:T(8,128)S(1)} %get-tuple-element.40.own_ref, bf16[304,512]{1,0:T(8,128)(2,1)S(1)} %collective-permute-done.6.up_ref, bf16[304,512]{1,0:T(8,128)(2,1)S(1)} %collective-permute-done.7.down_ref), custom_call_target="tpu_custom_call" | custom-call | bytes 4194304 | tf_op jit(solution)/shard_map/pallas_call | solution.py:459
  111.3 1.6 %shard_map.97 = bf16[128,4,512]{2,1,0:T(4,128)(2,1)} custom-call(s32[8,128]{1,0:T(8,128)S(1)} %copy-done.3, bf16[128,4,512]{2,1,0:T(4,128)(2,1)S(1)} %shard_map.96.placed_ref, bf16[8,104,512]{2,1,0:T(8,128)(2,1)S(1)} %all-to-all-done.3.blocks_ref), custom_call_target="tpu_custom_call" | custom-call | bytes 2097152 | tf_op jit(solution)/shard_map/pallas_call | solution.py:466
  (23 shorter events, 1.0 us)
Async XLA Ops:
  1.5 48.0 %copy-start = (s32[8,128]{1,0:T(8,128)}, s32[8,128]{1,0:T(8,128)S(1)}, u32[]{:S(2)}) copy-start(s32[8,128]{1,0:T(8,128)S(1)} %get-tuple-element.33.plan_ref) | copy-start | bytes 12292
  1.6 19.9 %all-to-all-start = ((s32[32,1,128]{2,1,0:T(1,128)}), s32[32,1,128]{2,1,0:T(1,128)S(1)}, u32[]{:S(2)}, u32[]{:S(2)}) async-start(s32[32,1,128]{2,1,0:T(1,128)} %bitcast.4), calls=%async_computation | async-start | bytes 32768 | tf_op jit(solution)/shard_map/all_to_all | solution.py:358
  20.8 0.7 copy-start.4
  21.5 15.1 %collective-permute-start.1 = (bf16[144,512]{1,0:T(8,128)(2,1)}, bf16[144,512]{1,0:T(8,128)(2,1)}, u32[]{:S(2)}, u32[]{:S(2)}) collective-permute-start(bf16[144,512]{1,0:T(8,128)(2,1)} %copy-done.4), channel_id=1, source_target_pairs={{0,7},{1,0},{2,1},{3,2},{4,3},{5,4},{6,5},{7,6},{8,15},{9,8},{10,9... | collective-permute-start | bytes 442376 | tf_op jit(solution)/shard_map/ppermute | solution.py:410
  28.9 42.0 %copy-start.2 = (s32[8,128]{1,0:T(8,128)}, s32[8,128]{1,0:T(8,128)S(1)}, u32[]{:S(2)}) copy-start(s32[8,128]{1,0:T(8,128)S(1)} %get-tuple-element.39.here_ref) | copy-start | bytes 12292
  28.9 18.0 %all-to-all-start.1 = ((bf16[64,4,768]{2,1,0:T(4,128)(2,1)}), bf16[64,4,768]{2,1,0:T(4,128)(2,1)S(1)}, u32[]{:S(2)}, u32[]{:S(2)}) async-start(bf16[64,4,768]{2,1,0:T(4,128)(2,1)} %get-tuple-element.41), calls=%async_computation.1 | async-start | bytes 786432 | tf_op jit(solution)/shard_map/all_to_all | solution.py:358
  36.5 6.9 %collective-permute-start = (bf16[160,512]{1,0:T(8,128)(2,1)S(1)}, bf16[160,512]{1,0:T(8,128)(2,1)S(1)}, u32[]{:S(2)}, u32[]{:S(2)}) collective-permute-start(bf16[160,512]{1,0:T(8,128)(2,1)S(1)} %get-tuple-element.43), channel_id=1, source_target_pairs={{0,1},{1,2},{2,3},{3,4},{4,5},{5,6},{6,7},{7,0},{8,9},{9,10},{10,1... | collective-permute-start | bytes 491528 | tf_op jit(solution)/shard_map/ppermute | solution.py:410
  46.8 12.4 %collective-permute-start.2 = (bf16[304,512]{1,0:T(8,128)(2,1)S(1)}, bf16[304,512]{1,0:T(8,128)(2,1)}, u32[]{:S(2)}, u32[]{:S(2)}) collective-permute-start(bf16[304,512]{1,0:T(8,128)(2,1)S(1)} %add_convert_fusion.5), channel_id=1, source_target_pairs={{0,1},{1,2},{2,3},{3,4},{4,5},{5,6},{6,7},{7,0},{8,9},{9,10},{10,1... | collective-permute-start | bytes 933896 | tf_op jit(solution)/shard_map/ppermute | solution.py:410
  46.8 13.4 %collective-permute-start.3 = (bf16[304,512]{1,0:T(8,128)(2,1)S(1)}, bf16[304,512]{1,0:T(8,128)(2,1)}, u32[]{:S(2)}, u32[]{:S(2)}) collective-permute-start(bf16[304,512]{1,0:T(8,128)(2,1)S(1)} %add_convert_fusion.4), channel_id=1, source_target_pairs={{0,7},{1,0},{2,1},{3,2},{4,3},{5,4},{6,5},{7,6},{8,15},{9,8},{10,9... | collective-permute-start | bytes 933896 | tf_op jit(solution)/shard_map/ppermute | solution.py:410
  53.9 14.3 %all-to-all-start.2 = ((bf16[64,4,512]{2,1,0:T(4,128)(2,1)}), bf16[64,4,512]{2,1,0:T(4,128)(2,1)S(1)}, u32[]{:S(2)}, u32[]{:S(2)}) async-start(bf16[64,4,512]{2,1,0:T(4,128)(2,1)} %shard_map.94), calls=%async_computation.2 | async-start | bytes 524288 | tf_op jit(solution)/shard_map/all_to_all | solution.py:358
  68.2 10.0 %collective-permute-start.4 = (bf16[304,512]{1,0:T(8,128)(2,1)S(1)}, bf16[304,512]{1,0:T(8,128)(2,1)S(1)}, u32[]{:S(2)}, u32[]{:S(2)}) collective-permute-start(bf16[304,512]{1,0:T(8,128)(2,1)S(1)} %add_convert_fusion.3), channel_id=1, source_target_pairs={{0,1},{1,2},{2,3},{3,4},{4,5},{5,6},{6,7},{7,0},{8,9},{9,10},{10,1... | collective-permute-start | bytes 933896 | tf_op jit(solution)/shard_map/ppermute | solution.py:410
  68.2 10.1 %collective-permute-start.5 = (bf16[304,512]{1,0:T(8,128)(2,1)S(1)}, bf16[304,512]{1,0:T(8,128)(2,1)S(1)}, u32[]{:S(2)}, u32[]{:S(2)}) collective-permute-start(bf16[304,512]{1,0:T(8,128)(2,1)S(1)} %add_convert_fusion.2), channel_id=1, source_target_pairs={{0,7},{1,0},{2,1},{3,2},{4,3},{5,4},{6,5},{7,6},{8,15},{9,8},{10,9... | collective-permute-start | bytes 933896 | tf_op jit(solution)/shard_map/ppermute | solution.py:410
  70.9 39.0 %copy-start.1 = (s32[8,128]{1,0:T(8,128)S(1)}, s32[8,128]{1,0:T(8,128)}, u32[]{:S(2)}) copy-start(s32[8,128]{1,0:T(8,128)} %copy-done) | copy-start | bytes 12292
  75.3 36.0 %copy-start.3 = (s32[8,128]{1,0:T(8,128)S(1)}, s32[8,128]{1,0:T(8,128)}, u32[]{:S(2)}) copy-start(s32[8,128]{1,0:T(8,128)} %copy-done.2) | copy-start | bytes 12292
  78.3 33.0 %all-to-all-start.3 = ((bf16[8,104,512]{2,1,0:T(8,128)(2,1)}), bf16[8,104,512]{2,1,0:T(8,128)(2,1)S(1)}, u32[]{:S(2)}, u32[]{:S(2)}) async-start(bf16[8,104,512]{2,1,0:T(8,128)(2,1)} %shard_map.95), calls=%async_computation.3 | async-start | bytes 1703936 | tf_op jit(solution)/shard_map/all_to_all | solution.py:358
  81.9 28.0 %collective-permute-start.6 = (bf16[304,512]{1,0:T(8,128)(2,1)S(1)}, bf16[304,512]{1,0:T(8,128)(2,1)S(1)}, u32[]{:S(2)}, u32[]{:S(2)}) collective-permute-start(bf16[304,512]{1,0:T(8,128)(2,1)S(1)} %add_convert_fusion.1), channel_id=1, source_target_pairs={{0,1},{1,2},{2,3},{3,4},{4,5},{5,6},{6,7},{7,0},{8,9},{9,10},{10,1... | collective-permute-start | bytes 933896 | tf_op jit(solution)/shard_map/ppermute | solution.py:410
  83.4 26.5 %collective-permute-start.7 = (bf16[304,512]{1,0:T(8,128)(2,1)S(1)}, bf16[304,512]{1,0:T(8,128)(2,1)S(1)}, u32[]{:S(2)}, u32[]{:S(2)}) collective-permute-start(bf16[304,512]{1,0:T(8,128)(2,1)S(1)} %add_convert_fusion), channel_id=1, source_target_pairs={{0,7},{1,0},{2,1},{3,2},{4,3},{5,4},{6,5},{7,6},{8,15},{9,8},{10,9... | collective-permute-start | bytes 933896 | tf_op jit(solution)/shard_map/ppermute | solution.py:410

commit v4 on v3

--- a/solution.py
+++ b/solution.py
@@ -10,7 +10,6 @@
 CAP = 2
 F32, BF16, I32 = jnp.float32, jnp.bfloat16, jnp.int32
 FRESH = 16
-STAY_BATCH, LEAVE_BATCH = 76, 26
 VMEM = pl.BlockSpec(memory_space=pltpu.VMEM)
 SMEM = pl.BlockSpec(memory_space=pltpu.SMEM)
 ANY = pl.BlockSpec(memory_space=pltpu.HBM)
@@ -31,7 +30,7 @@
     )
 
 
-STAY_SLOT, STAY_LENGTH, LEAVE_SLOT, LEAVE_ENTRY, LEAVE_LENGTH, STAY_COUNT = range(6)
+STAY_SLOT, STAY_LENGTH, LEAVE_SLOT, LEAVE_ENTRY, LEAVE_LENGTH, STAY_FIRST = range(6)
 
 
 def lanes(rows, columns):
@@ -81,7 +80,8 @@
     gone = jnp.sum(taken, axis=0, keepdims=True)
     stays = ((flags_ref[...] == 0) & (gone == 0.0)).astype(F32)
     rank = jnp.sum(jnp.where(lanes(slots, slots) < lines_of(slots, slots), stays, 0.0), axis=1, keepdims=True)
-    chosen = (rank.astype(I32) == lanes(slots, slots)) & (upright(stays) > 0.0)
+    first = slots - 2 * moves - jnp.sum(stays, axis=1, keepdims=True)
+    chosen = ((rank + first).astype(I32) == lanes(slots, slots)) & (upright(stays) > 0.0)
     listed = jnp.sum(jnp.where(chosen, lines_of(slots, slots).astype(F32), 0.0), axis=0, keepdims=True)
     listed_length = jnp.sum(jnp.where(chosen, upright(lengths), 0.0), axis=0, keepdims=True)
     plan_ref[...] = jnp.zeros(plan_ref.shape, I32)
@@ -90,7 +90,7 @@
     plan_ref[LEAVE_SLOT : LEAVE_SLOT + 1, 0:moves] = source
     plan_ref[LEAVE_ENTRY : LEAVE_ENTRY + 1, 0:moves] = place.astype(I32)
     plan_ref[LEAVE_LENGTH : LEAVE_LENGTH + 1, 0:moves] = leave_length.astype(I32)
-    plan_ref[STAY_COUNT : STAY_COUNT + 1, 0:1] = jnp.sum(stays, axis=1, keepdims=True).astype(I32)
+    plan_ref[STAY_FIRST : STAY_FIRST + 1, 0:1] = first.astype(I32)
 
 
 HERE_ENTRY, HERE_SLOT = range(2)
@@ -119,75 +119,57 @@
     here_ref[HERE_SLOT : HERE_SLOT + 1, :] = slot.astype(I32)
 
 
-def attend(rows, batch, kbuf, vbuf, score, weight, cache, steps, heads, row_of, query_of, fresh_of, length_of, await_keys, await_values, put):
+def attend(batches, kbuf, vbuf, score, weight, cache, steps, heads, row_of, query_of, fresh_of, length_of, await_keys, await_values):
     positions, head = kbuf.shape[1:]
     lines = heads * steps
+    lane = lanes(lines, positions)
+    step = lax.rem(lines_of(lines, positions), steps)
+    visible = (lane >= cache) & (lane - cache <= step)
 
     def fresh_rows(value):
         pad = jnp.zeros((FRESH - steps, head), F32)
         return jnp.concatenate([value.astype(F32), pad], axis=0).astype(BF16)
 
-    def scores(b, carry):
-        lane = lanes(lines, positions)
-        step = lax.rem(lines_of(lines, positions), steps)
-        visible = (lane >= cache) & (lane - cache <= step)
-        for u in range(batch):
-            i = b * batch + u
+    for b, batch in enumerate(batches):
+        for i in batch:
             fresh_key, fresh_value = fresh_of(i)
             kbuf[row_of(i), cache:positions, :] = fresh_rows(fresh_key)
             vbuf[row_of(i), cache:positions, :] = fresh_rows(fresh_value)
-        for u in range(batch):
-            i = b * batch + u
+        await_keys(b)
+        for i in batch:
             query = query_of(i).astype(F32)
             query = jnp.concatenate([query[:, h * head : (h + 1) * head] for h in range(heads)], axis=0)
             products = lax.dot_general(
                 query.astype(BF16), kbuf[row_of(i)], (((1,), (1,)), ((), ())), preferred_element_type=F32
             )
-            score[pl.ds(pl.multiple_of(i * lines, lines), lines), :] = jnp.where(
+            score[i * lines : (i + 1) * lines, :] = jnp.where(
                 (lane < length_of(i)) | visible, products * head**-0.5, -jnp.inf
             )
-        return carry
-
-    await_keys()
-    lax.fori_loop(0, rows // batch, scores, 0)
-
-    def soften(b, carry):
-        chunk = pl.ds(pl.multiple_of(b * batch * lines, lines), batch * lines)
+    for batch in batches:
+        chunk = slice(batch[0] * lines, (batch[-1] + 1) * lines)
         s = score[chunk, :]
         e = jnp.exp(s - jnp.max(s, axis=1, keepdims=True))
         weight[chunk, :] = (e * (1.0 / jnp.sum(e, axis=1, keepdims=True))).astype(BF16)
-        return carry
-
-    lax.fori_loop(0, rows // batch, soften, 0)
-
-    def mix(b, carry):
-        mixed = []
-        for u in range(batch):
-            i = b * batch + u
+    mixed = []
+    for b, batch in enumerate(batches):
+        await_values(b)
+        for i in batch:
             mixed.append(
-                jnp.dot(
-                    weight[pl.ds(pl.multiple_of(i * lines, lines), lines), :],
-                    vbuf[row_of(i)],
-                    preferred_element_type=F32,
-                )
+                jnp.dot(weight[i * lines : (i + 1) * lines, :], vbuf[row_of(i)], preferred_element_type=F32)
             )
-        put(b, mixed)
-        return carry
-
-    await_values()
-    lax.fori_loop(0, rows // batch, mix, 0)
+    return mixed
 
 
 def staying_kernel(
     place_ref, plan_ref, query_ref, key_ref, value_ref, keys_ref, values_ref, weight_ref,
-    up_ref, down_ref, own_ref, *rest,
+    up_ref, down_ref, heads_ref, fresh_ref, leave_keys_ref, leave_values_ref,
+    kbuf, vbuf, score, weight, wbuf, fsem, ksem, vsem, wsem,
 ):
-    terms_refs, fresh_ref = rest[:6], rest[6]
-    kbuf, vbuf, score, weight, heads, wbuf, fsem, ksem, vsem, wsem = rest[7:]
     steps, wide = query_ref.shape[1:]
     slots, _, cache, head = keys_ref.shape
-    tokens = heads.shape[0]
-    ring, columns = 8, up_ref.shape[1]
+    tokens, columns = heads_ref.shape[0], up_ref.shape[1]
+    rows, ring = tokens // steps, weight_ref.shape[1] // columns
+    chunk = slots // ksem.shape[0]
     fresh = [
         pltpu.make_async_copy(src, fresh_ref.at[:, :, pl.ds(at, src.shape[2])], fsem.at[i])
         for i, (src, at) in enumerate(((query_ref, 0), (key_ref, wide), (value_ref, wide + head)))
@@ -195,110 +177,107 @@
     keys, values = (
         [
             pltpu.make_async_copy(
-                ref.at[pl.ds(c * 32, 32), 0], buf.at[pl.ds(c * 32, 32), pl.ds(0, cache)], sem.at[c]
+                ref.at[pl.ds(c * chunk, chunk), 0], buf.at[pl.ds(c * chunk, chunk), pl.ds(0, cache)], sem.at[c]
             )
-            for c in range(slots // 32)
+            for c in range(slots // chunk)
         ]
         for ref, buf, sem in ((keys_ref, kbuf, ksem), (values_ref, vbuf, vsem))
     )
-    order = (4, 3, 5, 2, 6, 1, 7, 0)
-
-    def part(k):
-        at = lax.rem(place_ref[0] + k, ring) * columns
-        return pl.ds(pl.multiple_of(at, columns), columns)
-
-    parts = [pltpu.make_async_copy(weight_ref.at[:, part(k)], wbuf.at[j], wsem.at[j]) for j, k in enumerate(order)]
-    for copy in fresh + keys + values + parts:
+    at = lax.rem(place_ref[0] + ring // 2, ring) * columns
+    far = pltpu.make_async_copy(weight_ref.at[:, pl.ds(pl.multiple_of(at, columns), columns)], wbuf, wsem)
+    for copy in fresh + keys + values + [far]:
         copy.start()
 
-    def put(b, mixed):
-        quads = len(mixed) // 4
-        for j in range(quads):
-            four = mixed[4 * j : 4 * j + 4]
-            for h in range(wide // head):
-                tile = jnp.concatenate([o[h * steps : (h + 1) * steps] for o in four], axis=0)
-                at = pl.ds(pl.multiple_of((b * quads + j) * 16, 16), 16)
-                heads[at, h * head : (h + 1) * head] = tile.astype(BF16)
+    last = [(slots - rows + i) // chunk for i in range(rows)]
+    batches = [[i for i in range(rows) if last[i] == c] for c in sorted(set(last))]
+    due = [[c for c in range(slots // chunk) if c <= last[b[0]] and (j == 0 or c > last[batches[j - 1][0]])] for j, b in enumerate(batches)]
 
     def slot(i):
         return plan_ref[STAY_SLOT, i]
 
     for copy in fresh:
         copy.wait()
-    attend(
-        tokens // steps, STAY_BATCH, kbuf, vbuf, score, weight, cache, steps, wide // head,
+    mixed = attend(
+        batches, kbuf, vbuf, score, weight, cache, steps, wide // head,
         slot,
         lambda i: fresh_ref[slot(i), :, 0:wide],
         lambda i: (fresh_ref[slot(i), :, wide : wide + head], fresh_ref[slot(i), :, wide + head : wide + 2 * head]),
         lambda i: plan_ref[STAY_LENGTH, i],
-        lambda: [copy.wait() for copy in keys],
-        lambda: [copy.wait() for copy in values],
-        put,
-    )
+        lambda b: [keys[c].wait() for c in due[b]],
+        lambda b: [values[c].wait() for c in due[b]],
+    )
+    for j in range(rows // 4):
+        for h in range(wide // head):
+            tile = jnp.concatenate([o[h * steps : (h + 1) * steps] for o in mixed[4 * j : 4 * j + 4]], axis=0)
+            heads_ref[16 * j : 16 * j + 16, h * head : (h + 1) * head] = tile.astype(BF16)
+    for i in range(leave_keys_ref.shape[0]):
+        leave_keys_ref[i] = kbuf[plan_ref[LEAVE_SLOT, i], 0:cache, :]
+        leave_values_ref[i] = vbuf[plan_ref[LEAVE_SLOT, i], 0:cache, :]
+    far.wait()
     cut = up_ref.shape[0]
-    for j, k in enumerate(order):
-        parts[j].wait()
-        block = jnp.dot(heads[...], wbuf[j], preferred_element_type=F32)
+    block = jnp.dot(heads_ref[...], wbuf[...], preferred_element_type=F32)
+    up_ref[...] = block[:cut].astype(BF16)
+    down_ref[...] = block[cut:].astype(BF16)
+
+
+def terms_kernel(place_ref, heads_ref, weight_ref, own_ref, *rest):
+    terms_refs, wout, wsem = rest[:6], rest[6], rest[7]
+    ring, _, columns = wout.shape
+
+    def part(k):
+        at = lax.rem(place_ref[0] + k, ring) * columns
+        return pl.ds(pl.multiple_of(at, columns), columns)
+
+    order = (3, 5, 2, 6, 1, 7, 0, 4)
+    parts = [pltpu.make_async_copy(weight_ref.at[:, part(k)], wout.at[k], wsem.at[k]) for k in order]
+    for copy in parts:
+        copy.start()
+    for k, copy in zip(order, parts):
+        copy.wait()
         if k == ring // 2:
-            up_ref[...] = block[:cut].astype(BF16)
-            down_ref[...] = block[cut:].astype(BF16)
-        elif k == 0:
+            continue
+        block = jnp.dot(heads_ref[...], wout[k], preferred_element_type=F32)
+        if k == 0:
             own_ref[...] = block
         else:
             terms_refs[k - 1 if k < 4 else k - 2][...] = block.astype(BF16)
 
 
-def leaving_kernel(plan_ref, asked_ref, keys_ref, values_ref, out_ref, kbuf, vbuf, score, weight, ksem, vsem):
-    rows, cache, head = kbuf.shape[0], keys_ref.shape[2], keys_ref.shape[3]
+def leaving_kernel(plan_ref, asked_ref, keys_ref, values_ref, out_ref, kbuf, vbuf, score, weight):
+    rows, cache, head = keys_ref.shape
     steps, wide = out_ref.shape[1:]
-    loads = [
-        [
-            pltpu.make_async_copy(ref.at[plan_ref[LEAVE_SLOT, i], 0], buf.at[i, pl.ds(0, cache)], sem.at[i])
-            for i in range(rows)
-        ]
-        for ref, buf, sem in ((keys_ref, kbuf, ksem), (values_ref, vbuf, vsem))
-    ]
-    for copy in loads[0] + loads[1]:
-        copy.start()
     out_ref[...] = jnp.zeros(out_ref.shape, BF16)
+    for i in range(rows):
+        kbuf[i, 0:cache, :] = keys_ref[i]
+        vbuf[i, 0:cache, :] = values_ref[i]
 
     def entry(i):
         return plan_ref[LEAVE_ENTRY, i]
 
-    def put(b, mixed):
-        for u, o in enumerate(mixed):
-            at = entry(b * LEAVE_BATCH + u)
-            for h in range(wide // head):
-                out_ref[at, :, h * head : (h + 1) * head] = o[h * steps : (h + 1) * steps].astype(BF16)
-
-    attend(
-        rows, LEAVE_BATCH, kbuf, vbuf, score, weight, cache, steps, wide // head,
+    mixed = attend(
+        [list(range(rows))], kbuf, vbuf, score, weight, cache, steps, wide // head,
         lambda i: i,
         lambda i: asked_ref[entry(i), :, 0:wide],
         lambda i: (asked_ref[entry(i), :, wide : wide + head], asked_ref[entry(i), :, wide + head : wide + 2 * head]),
         lambda i: plan_ref[LEAVE_LENGTH, i],
-        lambda: [copy.wait() for copy in loads[0]],
-        lambda: [copy.wait() for copy in loads[1]],
-        put,
-    )
-
-
-def arrived_kernel(here_ref, back_ref, weight_ref, out_ref, heads, wbuf, wsem):
+        lambda b: None,
+        lambda b: None,
+    )
+    for i, o in enumerate(mixed):
+        for h in range(wide // head):
+            out_ref[entry(i), :, h * head : (h + 1) * head] = o[h * steps : (h + 1) * steps].astype(BF16)
+
+
+def arrived_kernel(place_ref, here_ref, back_ref, weight_ref, out_ref, heads):
     steps = back_ref.shape[1]
-    rows, columns = out_ref.shape[1] // steps, out_ref.shape[2]
-    parts = [
-        pltpu.make_async_copy(weight_ref.at[:, pl.ds(k * columns, columns)], wbuf.at[k], wsem.at[k])
-        for k in range(out_ref.shape[0])
-    ]
-    for copy in parts:
-        copy.start()
+    ring, lines, _ = out_ref.shape
+    rows = lines // steps
     for j in range(heads.shape[0] // 16):
         four = [back_ref[here_ref[HERE_ENTRY, min(4 * j + u, rows - 1)]].astype(F32) for u in range(4)]
         heads[16 * j : 16 * j + 16, :] = jnp.concatenate(four, axis=0).astype(BF16)
-    for k, copy in enumerate(parts):
-        copy.wait()
-        terms = jnp.dot(heads[...], wbuf[k], preferred_element_type=F32)
-        out_ref[k] = terms[: out_ref.shape[1]].astype(BF16)
+    for k in range(ring):
+        terms = jnp.dot(heads[...], weight_ref[k], preferred_element_type=F32)
+        out_ref[lax.rem(place_ref[0] + k, ring)] = terms[:lines].astype(BF16)
 
 
 def place_kernel(plan_ref, own_ref, up_ref, down_ref, out_ref, total):
@@ -307,7 +286,7 @@
     out_ref[...] = jnp.zeros(out_ref.shape, BF16)
     for i in range(own_ref.shape[0] // steps):
 
-        @pl.when(i < plan_ref[STAY_COUNT, 0])
+        @pl.when(i >= plan_ref[STAY_FIRST, 0])
         def _():
             out_ref[plan_ref[STAY_SLOT, i]] = total[i * steps : (i + 1) * steps, :].astype(BF16)
 
@@ -381,27 +360,30 @@
 
     tokens = staying * steps
     cut = -(-tokens // 32) * 16
-    up, down, own, *terms = call(
+    up, down, heads, fresh, leave_keys, leave_values = call(
         staying_kernel,
-        [shape((cut, columns), BF16), shape((tokens - cut, columns), BF16), shape((tokens, columns), F32)]
-        + [shape((tokens, columns), BF16)] * 6
-        + [shape((slots, steps, wide + 2 * head), BF16)],
+        [
+            shape((cut, columns), BF16),
+            shape((tokens - cut, columns), BF16),
+            shape((tokens, wide), BF16),
+            shape((slots, steps, wide + 2 * head), BF16),
+            shape((moves, cache, head), BF16),
+            shape((moves, cache, head), BF16),
+        ],
         [SMEM] * 2 + [ANY] * 6,
         scratch(slots, staying)
         + [
-            pltpu.VMEM((tokens, wide), BF16),
-            pltpu.VMEM((ring, wide, columns), BF16),
+            pltpu.VMEM((wide, columns), BF16),
             pltpu.SemaphoreType.DMA((3,)),
-            pltpu.SemaphoreType.DMA((slots // 32,)),
-            pltpu.SemaphoreType.DMA((slots // 32,)),
-            pltpu.SemaphoreType.DMA((ring,)),
+            pltpu.SemaphoreType.DMA((4,)),
+            pltpu.SemaphoreType.DMA((4,)),
+            pltpu.SemaphoreType.DMA,
         ],
-        flops=2 * tokens * wide * out_weight.shape[1],
-        nbytes=20 << 20,
+        flops=2 * tokens * wide * columns,
+        nbytes=16 << 20,
         exps=tokens * positions * 4,
-        limit=32,
+        limit=24,
     )(place, plan, queries, new_keys, new_values, keys_cache, values_cache, out_weight)
-    fresh = terms.pop()
 
     ahead = [(i, (i + 1) % ring) for i in range(ring)]
     astern = [(i, (i - 1) % ring) for i in range(ring)]
@@ -415,14 +397,27 @@
             (terms[6 - k].astype(F32) + d.astype(F32)).astype(BF16),
         )
 
-    table, up, down, fresh = barrier((table, up, down, fresh))
+    table, up, down, fresh, heads = barrier((table, up, down, fresh, heads))
     asked, here = call(
         payload_kernel,
         [shape((entries, steps, wide + 2 * head), BF16), shape((8, 128), I32)],
         [SMEM] + [VMEM] * 2,
         nbytes=2 << 20,
     )(table, table, fresh)
+    asked, heads = barrier((asked, heads))
     asked = exchange(asked, "group")
+    own, *terms = call(
+        terms_kernel,
+        [shape((tokens, columns), F32)]
+        + [shape((tokens, columns), BF16)] * 6
+        + [shape((ring, wide, columns), BF16)],
+        [SMEM, VMEM, ANY],
+        [pltpu.SemaphoreType.DMA((ring,))],
+        flops=2 * tokens * wide * out_weight.shape[1],
+        nbytes=8 << 20,
+        limit=10,
+    )(place, heads, out_weight)
+    weight = terms.pop()
     up, down = hop(up, down)
     up = jnp.concatenate([up, jnp.zeros((tokens - cut, columns), BF16)], axis=0)
     down = jnp.concatenate([jnp.zeros((cut, columns), BF16), down], axis=0)
@@ -432,10 +427,10 @@
     back = call(
         leaving_kernel,
         shape((entries, steps, wide), BF16),
-        [SMEM] + [VMEM] + [ANY] * 2,
-        scratch(moves, moves) + [pltpu.SemaphoreType.DMA((moves,)), pltpu.SemaphoreType.DMA((moves,))],
-        nbytes=8 << 20,
-    )(plan, asked, keys_cache, values_cache)
+        [SMEM] + [VMEM] * 3,
+        scratch(moves, moves),
+        nbytes=4 << 20,
+    )(plan, asked, leave_keys, leave_values)
     back = exchange(back, "group")
     back, up, down = barrier((back, *add(2, up, down)))
     up, down = hop(up, down)
@@ -443,15 +438,10 @@
     blocks = call(
         arrived_kernel,
         shape((ring, arrived, columns), BF16),
-        [SMEM, VMEM, ANY],
-        [
-            pltpu.VMEM((-(-arrived // 16) * 16, wide), BF16),
-            pltpu.VMEM((ring, wide, columns), BF16),
-            pltpu.SemaphoreType.DMA((ring,)),
-        ],
+        [SMEM] * 2 + [VMEM] * 2,
+        [pltpu.VMEM((-(-arrived // 16) * 16, wide), BF16)],
         nbytes=6 << 20,
-        limit=12,
-    )(here, back, out_weight)
+    )(place, here, back, weight)
     blocks, up, down = barrier((blocks, *add(1, up, down)))
     blocks = exchange(blocks, "tp")
     up, down = hop(up, down)

time: 114 us -> 111 us (0.974)
  waiting for transfers between devices: 44.1 us -> 35.4 us
  local copies, waits for them, and re-layouts: 0.66 us -> 5.81 us
  Pallas kernels: 25.8 us -> 22.4 us
  starting transfers between devices: 38.9 us -> 41.7 us
  other arithmetic: 3.26 us -> 4.99 us
    ppermute x8, waiting for transfers between devices: 33.9 us -> 28.1 us  [hop(): return (lax.ppermute(u, 'tp', ahead), lax.ppermute(d, 'tp', astern))]
    unnamed x10 -> x12, local copies, waits for them, and re-layouts: 0.66 us -> 5.81 us
    all_to_all x4, waiting for transfers between devices: 10.3 us -> 7.29 us  [exchange(): return lax.all_to_all(x, axis, split_axis=0, concat_axis=0, tiled=True)]
    all_to_all x4, starting transfers between devices: 25.1 us -> 27.9 us  [exchange(): return lax.all_to_all(x, axis, split_axis=0, concat_axis=0, tiled=True)]
    pallas_call x1, Pallas kernels: 10.7 us -> 8.06 us  [on_device(): call(staying_kernel, [shape((cut, columns), BF16), shape((tokens - cut, c...]
    pallas_call x1, Pallas kernels: 4.33 us -> 2.27 us  [on_device(): call(leaving_kernel, shape((entries, steps, wide), BF16), [SMEM] + [VMEM]...]
    pallas_call x1 -> x2, Pallas kernels: 4.44 us -> 5.68 us  [the longest x1 3.41 us: on_device(): call(terms_kernel, [shape((tokens, columns), F32)] + [shape((tokens, colu...]
  transfers between devices with their start and end apart: 12 -> 12, of which waited for: 5 -> 4; matrix products, arithmetic and copies ran while one was open for 3% -> 4% of each run, Pallas kernels for 20% -> 17%
where the time goes in v4:
time: 111 us; the launch traced here: 110 us
  starting transfers between devices  41.7 us (38%)
  waiting for transfers between devices  35.4 us (32%)
  Pallas kernels  22.4 us (20%)
  local copies, waits for them, and re-layouts  5.81 us (5%)
  other arithmetic  4.99 us (4%)
    ppermute x8, waiting for transfers between devices, hop(): return (lax.ppermute(u, 'tp', ahead), lax.ppermute(d, 'tp', astern))  28.1 us
    all_to_all x4, starting transfers between devices, exchange(): return lax.all_to_all(x, axis, split_axis=0, concat_axis=0, tiled=True)  27.9 us
    ppermute x8, starting transfers between devices, hop(): return (lax.ppermute(u, 'tp', ahead), lax.ppermute(d, 'tp', astern))  13.8 us
    pallas_call x1, Pallas kernels, on_device(): call(staying_kernel, [shape((cut, columns), BF16), shape((tokens - cut, c...  8.06 us
    all_to_all x4, waiting for transfers between devices, exchange(): return lax.all_to_all(x, axis, split_axis=0, concat_axis=0, tiled=True)  7.29 us
    unnamed x12, local copies, waits for them, and re-layouts  5.81 us
    pallas_call x1, Pallas kernels, on_device(): call(terms_kernel, [shape((tokens, columns), F32)] + [shape((tokens, colu...  3.41 us
    convert_element_type x3, other arithmetic, add(): (terms[6 - k].astype(F32) + d.astype(F32)).astype(BF16)  3.01 us
  transfers between devices with their start and end apart: 12, of which 4 were waited for; matrix products, arithmetic and copies ran while one was open for 4% of the time, Pallas kernels for 17%

profile of v4, /device:TPU:1, one launch (start us, length us, event | category | flops | bytes accessed | tf_op | source)
XLA Modules:
  0.0 110.5 jit_solution(1931978491074835847)
XLA Ops:
  0.0 1.5 %shard_map.91 = (s32[32,128]{1,0:T(8,128)}, s32[8,128]{1,0:T(8,128)S(1)}) custom-call(s32[3,26]{1,0:T(4,128)} %bitcast.10, s32[1,128]{1,0:T(1,128)} %bitcast.11, s32[1,128]{1,0:T(1,128)} %bitcast.12), custom_call_target="tpu_custom_call" | custom-call | bytes 65536 | tf_op jit(solution)/shard_map/pallas_call | solution.py:347
  1.5 8.6 %all-to-all-start = ((s32[32,1,128]{2,1,0:T(1,128)}), s32[32,1,128]{2,1,0:T(1,128)S(1)}, u32[]{:S(2)}, u32[]{:S(2)}) async-start(s32[32,1,128]{2,1,0:T(1,128)} %bitcast.4), calls=%async_computation | async-start | bytes 32768 | tf_op jit(solution)/shard_map/all_to_all | solution.py:337
  10.2 8.1 %shard_map.92 = (bf16[160,512]{1,0:T(8,128)(2,1)S(1)}, bf16[144,512]{1,0:T(8,128)(2,1)}, bf16[304,512]{1,0:T(8,128)(2,1)S(1)}, bf16[128,4,768]{2,1,0:T(4,128)(2,...) custom-call(s32[1]{0:T(128)} %bitcast.6.place_ref, ...), custom_call_target="tpu_custom_call" | custom-call | flops 159383552 | bytes 16777216 | tf_op jit(solution)/shard_map/pallas_call | solution.py:363
  18.2 5.7 %collective-permute-start.1 = (bf16[144,512]{1,0:T(8,128)(2,1)}, bf16[144,512]{1,0:T(8,128)(2,1)}, u32[]{:S(2)}, u32[]{:S(2)}) collective-permute-start(bf16[144,512]{1,0:T(8,128)(2,1)} %get-tuple-element.56), channel_id=1, source_target_pairs={{0,7},{1,0},{2,1},{3,2},{4,3},{5,4},{6,5},{7,6},{8,15},{9,8},{10,9... | collective-permute-start | bytes 442376 | tf_op jit(solution)/shard_map/ppermute | solution.py:392
  23.9 1.8 %shard_map.93 = (bf16[64,4,768]{2,1,0:T(4,128)(2,1)}, s32[8,128]{1,0:T(8,128)S(1)}) custom-call(s32[32,128]{1,0:T(8,128)S(1)} %bitcast.8, s32[32,128]{1,0:T(8,128)S(1)} %bitcast.9, bf16[128,4,768]{2,1,0:T(4,128)(2,1)S(1)} %get-tuple-element.46.fresh_ref), custom_call_target="tpu_custom_call" | custom-call | bytes 2097152 | tf_op jit(solution)/shard_map/pallas_call | solution.py:401
  25.7 7.7 %all-to-all-start.1 = ((bf16[64,4,768]{2,1,0:T(4,128)(2,1)}), bf16[64,4,768]{2,1,0:T(4,128)(2,1)S(1)}, u32[]{:S(2)}, u32[]{:S(2)}) async-start(bf16[64,4,768]{2,1,0:T(4,128)(2,1)} %get-tuple-element.52), calls=%async_computation.1 | async-start | bytes 786432 | tf_op jit(solution)/shard_map/all_to_all | solution.py:337
  34.4 3.4 %shard_map.94 = (f32[304,512]{1,0:T(8,128)S(1)}, bf16[304,512]{1,0:T(8,128)(2,1)S(1)}, bf16[304,512]{1,0:T(8,128)(2,1)S(1)}, bf16[304,512]{1,0:T(8,128)(2,1)S(1)...) custom-call(s32[1]{0:T(128)} %bitcast.6.place_ref, ...), custom_call_target="tpu_custom_call" | custom-call | flops 1275068416 | bytes 8388608 | tf_op jit(solution)/shard_map/pallas_call | solution.py:409
  37.8 1.9 %copy-done = bf16[8,512,512]{2,1,0:T(8,128)(2,1)} copy-done((bf16[8,512,512]{2,1,0:T(8,128)(2,1)}, bf16[8,512,512]{2,1,0:T(8,128)(2,1)S(1)}, u32[]{:S(2)}) %copy-start) | copy-done | bytes 4194328
  40.5 1.8 %add_convert_fusion.4 = bf16[304,512]{1,0:T(8,128)(2,1)} fusion(bf16[304,512]{1,0:T(8,128)(2,1)S(1)} %get-tuple-element.55, bf16[144,512]{1,0:T(8,128)(2,1)} %collective-permute-done.1), kind=kLoop, calls=%fused_computation.4 | loop fusion | flops 622592 | bytes 770048 | tf_op jit(solution)/shard_map/convert_element_type | solution.py:397
  43.6 2.7 %collective-permute-start.3 = (bf16[304,512]{1,0:T(8,128)(2,1)}, bf16[304,512]{1,0:T(8,128)(2,1)}, u32[]{:S(2)}, u32[]{:S(2)}) collective-permute-start(bf16[304,512]{1,0:T(8,128)(2,1)} %add_convert_fusion.4), channel_id=1, source_target_pairs={{0,7},{1,0},{2,1},{3,2},{4,3},{5,4},{6,5},{7,6},{8,15},{9,8},{10,9... | collective-permute-start | bytes 933896 | tf_op jit(solution)/shard_map/ppermute | solution.py:392
  46.3 2.3 %shard_map.95 = bf16[64,4,512]{2,1,0:T(4,128)(2,1)} custom-call(s32[8,128]{1,0:T(8,128)S(1)} %get-tuple-element.40.plan_ref, bf16[64,4,768]{2,1,0:T(4,128)(2,1)S(1)} %all-to-all-done.1.asked_ref, bf16[26,128,128]{2,1,0:T(8,128)(2,1)S(1)} %get-tuple-element.58.keys_ref, bf16[26,128,128]{2,1,0:T(8,128)(2,1)S(1)} %get-tuple-element.59.values_ref), custom_call_target="tpu_custom_call" | custom-call | bytes 4194304 | tf_op jit(solution)/shard_map/pallas_call | solution.py:427
  48.6 7.3 %all-to-all-start.2 = ((bf16[64,4,512]{2,1,0:T(4,128)(2,1)}), bf16[64,4,512]{2,1,0:T(4,128)(2,1)S(1)}, u32[]{:S(2)}, u32[]{:S(2)}) async-start(bf16[64,4,512]{2,1,0:T(4,128)(2,1)} %shard_map.95), calls=%async_computation.2 | async-start | bytes 524288 | tf_op jit(solution)/shard_map/all_to_all | solution.py:337
  55.9 1.1 %add_convert_fusion.3 = bf16[304,512]{1,0:T(8,128)(2,1)S(1)} fusion(bf16[304,512]{1,0:T(8,128)(2,1)} %collective-permute-done.2, bf16[304,512]{1,0:T(8,128)(2,1)} %copy-done.3), kind=kLoop, calls=%fused_computation.3 | loop fusion | flops 622592 | bytes 933888 | tf_op jit(solution)/shard_map/convert_element_type | solution.py:396
  58.2 6.7 %all-to-all-done.2.back_ref = bf16[64,4,512]{2,1,0:T(4,128)(2,1)S(1)} async-done(((bf16[64,4,512]{2,1,0:T(4,128)(2,1)}), bf16[64,4,512]{2,1,0:T(4,128)(2,1)S(1)}, u32[]{:S(2)}, u32[]{:S(2)}) %all-to-all-start.2) | async-done | bytes 262176 | tf_op jit(solution)/shard_map/all_to_all | solution.py:337
  64.9 2.7 %collective-permute-start.5 = (bf16[304,512]{1,0:T(8,128)(2,1)S(1)}, bf16[304,512]{1,0:T(8,128)(2,1)S(1)}, u32[]{:S(2)}, u32[]{:S(2)}) collective-permute-start(bf16[304,512]{1,0:T(8,128)(2,1)S(1)} %add_convert_fusion.2), channel_id=1, source_target_pairs={{0,7},{1,0},{2,1},{3,2},{4,3},{5,4},{6,5},{7,6},{8,15},{9,8},{10,9... | collective-permute-start | bytes 933896 | tf_op jit(solution)/shard_map/ppermute | solution.py:392
  67.6 2.2 %copy-done.1 = bf16[8,512,512]{2,1,0:T(8,128)(2,1)S(1)} copy-done((bf16[8,512,512]{2,1,0:T(8,128)(2,1)S(1)}, bf16[8,512,512]{2,1,0:T(8,128)(2,1)}, u32[]{:S(2)}) %copy-start.1) | copy-done | bytes 4194328
  69.8 2.3 %shard_map.96 = bf16[8,104,512]{2,1,0:T(8,128)(2,1)} custom-call(s32[1]{0:T(128)} %bitcast.6.place_ref, s32[8,128]{1,0:T(8,128)S(1)} %get-tuple-element.47.here_ref, bf16[64,4,512]{2,1,0:T(4,128)(2,1)S(1)} %all-to-all-done.2.back_ref, bf16[8,512,512]{2,1,0:T(8,128)(2,1)S(1)} %copy-done.1), custom_call_target="tpu_custom_call" | custom-call | bytes 6291456 | tf_op jit(solution)/shard_map/pallas_call | solution.py:438
  72.1 2.8 %collective-permute-done.4 = bf16[304,512]{1,0:T(8,128)(2,1)S(1)} collective-permute-done((bf16[304,512]{1,0:T(8,128)(2,1)S(1)}, bf16[304,512]{1,0:T(8,128)(2,1)S(1)}, u32[]{:S(2)}, u32[]{:S(2)}) %collective-permute-start.4) | collective-permute-done | bytes 311328 | tf_op jit(solution)/shard_map/ppermute | solution.py:392
  75.1 4.4 %all-to-all-start.3 = ((bf16[8,104,512]{2,1,0:T(8,128)(2,1)}), bf16[8,104,512]{2,1,0:T(8,128)(2,1)S(1)}, u32[]{:S(2)}, u32[]{:S(2)}) async-start(bf16[8,104,512]{2,1,0:T(8,128)(2,1)} %shard_map.96), calls=%async_computation.3 | async-start | bytes 1703936 | tf_op jit(solution)/shard_map/all_to_all | solution.py:337
  79.5 1.5 %collective-permute-start.6 = (bf16[304,512]{1,0:T(8,128)(2,1)S(1)}, bf16[304,512]{1,0:T(8,128)(2,1)S(1)}, u32[]{:S(2)}, u32[]{:S(2)}) collective-permute-start(bf16[304,512]{1,0:T(8,128)(2,1)S(1)} %add_convert_fusion.1), channel_id=1, source_target_pairs={{0,1},{1,2},{2,3},{3,4},{4,5},{5,6},{6,7},{7,0},{8,9},{9,10},{10,1... | collective-permute-start | bytes 933896 | tf_op jit(solution)/shard_map/ppermute | solution.py:392
  80.9 1.2 %collective-permute-start.7 = (bf16[304,512]{1,0:T(8,128)(2,1)S(1)}, bf16[304,512]{1,0:T(8,128)(2,1)S(1)}, u32[]{:S(2)}, u32[]{:S(2)}) collective-permute-start(bf16[304,512]{1,0:T(8,128)(2,1)S(1)} %add_convert_fusion), channel_id=1, source_target_pairs={{0,7},{1,0},{2,1},{3,2},{4,3},{5,4},{6,5},{7,6},{8,15},{9,8},{10,9... | collective-permute-start | bytes 933896 | tf_op jit(solution)/shard_map/ppermute | solution.py:392
  82.2 25.3 %collective-permute-done.6.up_ref = bf16[304,512]{1,0:T(8,128)(2,1)S(1)} collective-permute-done((bf16[304,512]{1,0:T(8,128)(2,1)S(1)}, bf16[304,512]{1,0:T(8,128)(2,1)S(1)}, u32[]{:S(2)}, u32[]{:S(2)}) %collective-permute-start.6) | collective-permute-done | bytes 311328 | tf_op jit(solution)/shard_map/ppermute | solution.py:392
  107.4 1.4 %shard_map.97.placed_ref = bf16[128,4,512]{2,1,0:T(4,128)(2,1)S(1)} custom-call(s32[8,128]{1,0:T(8,128)S(1)} %get-tuple-element.40.plan_ref, f32[304,512]{1,0:T(8,128)S(1)} %get-tuple-element.51.own_ref, bf16[304,512]{1,0:T(8,128)(2,1)S(1)} %collective-permute-done.6.up_ref, bf16[304,512]{1,0:T(8,128)(2,1)S(1)} %collective-permute-done.7.down_ref), custom_call_target="tpu_custom_call" | custom-call | bytes 4194304 | tf_op jit(solution)/shard_map/pallas_call | solution.py:449
  108.9 1.6 %shard_map.98 = bf16[128,4,512]{2,1,0:T(4,128)(2,1)} custom-call(s32[8,128]{1,0:T(8,128)S(1)} %get-tuple-element.47.here_ref, bf16[128,4,512]{2,1,0:T(4,128)(2,1)S(1)} %shard_map.97.placed_ref, bf16[8,104,512]{2,1,0:T(8,128)(2,1)S(1)} %all-to-all-done.3.blocks_ref), custom_call_target="tpu_custom_call" | custom-call | bytes 2097152 | tf_op jit(solution)/shard_map/pallas_call | solution.py:456
  (26 shorter events, 4.5 us)
Async XLA Ops:
  1.5 16.7 %all-to-all-start = ((s32[32,1,128]{2,1,0:T(1,128)}), s32[32,1,128]{2,1,0:T(1,128)S(1)}, u32[]{:S(2)}, u32[]{:S(2)}) async-start(s32[32,1,128]{2,1,0:T(1,128)} %bitcast.4), calls=%async_computation | async-start | bytes 32768 | tf_op jit(solution)/shard_map/all_to_all | solution.py:337
  18.2 7.5 %copy-start.4 = (bf16[304,512]{1,0:T(8,128)(2,1)}, bf16[304,512]{1,0:T(8,128)(2,1)S(1)}, u32[]{:S(2)}) copy-start(bf16[304,512]{1,0:T(8,128)(2,1)S(1)} %get-tuple-element.50.heads_ref) | copy-start | bytes 933892
  18.2 22.2 %collective-permute-start.1 = (bf16[144,512]{1,0:T(8,128)(2,1)}, bf16[144,512]{1,0:T(8,128)(2,1)}, u32[]{:S(2)}, u32[]{:S(2)}) collective-permute-start(bf16[144,512]{1,0:T(8,128)(2,1)} %get-tuple-element.56), channel_id=1, source_target_pairs={{0,7},{1,0},{2,1},{3,2},{4,3},{5,4},{6,5},{7,6},{8,15},{9,8},{10,9... | collective-permute-start | bytes 442376 | tf_op jit(solution)/shard_map/ppermute | solution.py:392
  25.7 18.0 %all-to-all-start.1 = ((bf16[64,4,768]{2,1,0:T(4,128)(2,1)}), bf16[64,4,768]{2,1,0:T(4,128)(2,1)S(1)}, u32[]{:S(2)}, u32[]{:S(2)}) async-start(bf16[64,4,768]{2,1,0:T(4,128)(2,1)} %get-tuple-element.52), calls=%async_computation.1 | async-start | bytes 786432 | tf_op jit(solution)/shard_map/all_to_all | solution.py:337
  33.3 8.9 %collective-permute-start = (bf16[160,512]{1,0:T(8,128)(2,1)S(1)}, bf16[160,512]{1,0:T(8,128)(2,1)S(1)}, u32[]{:S(2)}, u32[]{:S(2)}) collective-permute-start(bf16[160,512]{1,0:T(8,128)(2,1)S(1)} %get-tuple-element.54), channel_id=1, source_target_pairs={{0,1},{1,2},{2,3},{3,4},{4,5},{5,6},{6,7},{7,0},{8,9},{9,10},{10,1... | collective-permute-start | bytes 491528 | tf_op jit(solution)/shard_map/ppermute | solution.py:392
  33.4 1.0 copy-start.5
  37.8 1.9 %copy-start = (bf16[8,512,512]{2,1,0:T(8,128)(2,1)}, bf16[8,512,512]{2,1,0:T(8,128)(2,1)S(1)}, u32[]{:S(2)}) copy-start(bf16[8,512,512]{2,1,0:T(8,128)(2,1)S(1)} %get-tuple-element.65.weight_ref) | copy-start | bytes 12582916
  39.8 0.7 copy-start.2
  40.5 1.8 %copy-start.3 = (bf16[304,512]{1,0:T(8,128)(2,1)}, bf16[304,512]{1,0:T(8,128)(2,1)S(1)}, u32[]{:S(2)}) copy-start(bf16[304,512]{1,0:T(8,128)(2,1)S(1)} %get-tuple-element.60) | copy-start | bytes 933892
  43.6 12.3 %collective-permute-start.2 = (bf16[304,512]{1,0:T(8,128)(2,1)}, bf16[304,512]{1,0:T(8,128)(2,1)}, u32[]{:S(2)}, u32[]{:S(2)}) collective-permute-start(bf16[304,512]{1,0:T(8,128)(2,1)} %add_convert_fusion.5), channel_id=1, source_target_pairs={{0,1},{1,2},{2,3},{3,4},{4,5},{5,6},{6,7},{7,0},{8,9},{9,10},{10,1... | collective-permute-start | bytes 933896 | tf_op jit(solution)/shard_map/ppermute | solution.py:392
  43.6 13.4 %collective-permute-start.3 = (bf16[304,512]{1,0:T(8,128)(2,1)}, bf16[304,512]{1,0:T(8,128)(2,1)}, u32[]{:S(2)}, u32[]{:S(2)}) collective-permute-start(bf16[304,512]{1,0:T(8,128)(2,1)} %add_convert_fusion.4), channel_id=1, source_target_pairs={{0,7},{1,0},{2,1},{3,2},{4,3},{5,4},{6,5},{7,6},{8,15},{9,8},{10,9... | collective-permute-start | bytes 933896 | tf_op jit(solution)/shard_map/ppermute | solution.py:392
  48.6 16.3 %all-to-all-start.2 = ((bf16[64,4,512]{2,1,0:T(4,128)(2,1)}), bf16[64,4,512]{2,1,0:T(4,128)(2,1)S(1)}, u32[]{:S(2)}, u32[]{:S(2)}) async-start(bf16[64,4,512]{2,1,0:T(4,128)(2,1)} %shard_map.95), calls=%async_computation.2 | async-start | bytes 524288 | tf_op jit(solution)/shard_map/all_to_all | solution.py:337
  64.9 10.0 %collective-permute-start.4 = (bf16[304,512]{1,0:T(8,128)(2,1)S(1)}, bf16[304,512]{1,0:T(8,128)(2,1)S(1)}, u32[]{:S(2)}, u32[]{:S(2)}) collective-permute-start(bf16[304,512]{1,0:T(8,128)(2,1)S(1)} %add_convert_fusion.3), channel_id=1, source_target_pairs={{0,1},{1,2},{2,3},{3,4},{4,5},{5,6},{6,7},{7,0},{8,9},{9,10},{10,1... | collective-permute-start | bytes 933896 | tf_op jit(solution)/shard_map/ppermute | solution.py:392
  64.9 10.1 %collective-permute-start.5 = (bf16[304,512]{1,0:T(8,128)(2,1)S(1)}, bf16[304,512]{1,0:T(8,128)(2,1)S(1)}, u32[]{:S(2)}, u32[]{:S(2)}) collective-permute-start(bf16[304,512]{1,0:T(8,128)(2,1)S(1)} %add_convert_fusion.2), channel_id=1, source_target_pairs={{0,7},{1,0},{2,1},{3,2},{4,3},{5,4},{6,5},{7,6},{8,15},{9,8},{10,9... | collective-permute-start | bytes 933896 | tf_op jit(solution)/shard_map/ppermute | solution.py:392
  67.6 2.2 %copy-start.1 = (bf16[8,512,512]{2,1,0:T(8,128)(2,1)S(1)}, bf16[8,512,512]{2,1,0:T(8,128)(2,1)}, u32[]{:S(2)}) copy-start(bf16[8,512,512]{2,1,0:T(8,128)(2,1)} %copy-done) | copy-start | bytes 12582916
  75.1 33.8 %all-to-all-start.3 = ((bf16[8,104,512]{2,1,0:T(8,128)(2,1)}), bf16[8,104,512]{2,1,0:T(8,128)(2,1)S(1)}, u32[]{:S(2)}, u32[]{:S(2)}) async-start(bf16[8,104,512]{2,1,0:T(8,128)(2,1)} %shard_map.96), calls=%async_computation.3 | async-start | bytes 1703936 | tf_op jit(solution)/shard_map/all_to_all | solution.py:337
  79.5 28.0 %collective-permute-start.6 = (bf16[304,512]{1,0:T(8,128)(2,1)S(1)}, bf16[304,512]{1,0:T(8,128)(2,1)S(1)}, u32[]{:S(2)}, u32[]{:S(2)}) collective-permute-start(bf16[304,512]{1,0:T(8,128)(2,1)S(1)} %add_convert_fusion.1), channel_id=1, source_target_pairs={{0,1},{1,2},{2,3},{3,4},{4,5},{5,6},{6,7},{7,0},{8,9},{9,10},{10,1... | collective-permute-start | bytes 933896 | tf_op jit(solution)/shard_map/ppermute | solution.py:392
  80.9 26.5 %collective-permute-start.7 = (bf16[304,512]{1,0:T(8,128)(2,1)S(1)}, bf16[304,512]{1,0:T(8,128)(2,1)S(1)}, u32[]{:S(2)}, u32[]{:S(2)}) collective-permute-start(bf16[304,512]{1,0:T(8,128)(2,1)S(1)} %add_convert_fusion), channel_id=1, source_target_pairs={{0,7},{1,0},{2,1},{3,2},{4,3},{5,4},{6,5},{7,6},{8,15},{9,8},{10,9... | collective-permute-start | bytes 933896 | tf_op jit(solution)/shard_map/ppermute | solution.py:392

commit v5 on v4

--- a/solution.py
+++ b/solution.py
@@ -10,6 +10,7 @@
 CAP = 2
 F32, BF16, I32 = jnp.float32, jnp.bfloat16, jnp.int32
 FRESH = 16
+PAYLOAD_COST, HOP_COST, ARRIVED_COST, PLACE_COST = 8_000_000_000, 20_000_000_000, 8_000_000_000, 40_000_000_000
 VMEM = pl.BlockSpec(memory_space=pltpu.VMEM)
 SMEM = pl.BlockSpec(memory_space=pltpu.SMEM)
 ANY = pl.BlockSpec(memory_space=pltpu.HBM)
@@ -220,27 +221,27 @@
     down_ref[...] = block[cut:].astype(BF16)
 
 
-def terms_kernel(place_ref, heads_ref, weight_ref, own_ref, *rest):
-    terms_refs, wout, wsem = rest[:6], rest[6], rest[7]
-    ring, _, columns = wout.shape
-
-    def part(k):
-        at = lax.rem(place_ref[0] + k, ring) * columns
-        return pl.ds(pl.multiple_of(at, columns), columns)
-
-    order = (3, 5, 2, 6, 1, 7, 0, 4)
-    parts = [pltpu.make_async_copy(weight_ref.at[:, part(k)], wout.at[k], wsem.at[k]) for k in order]
-    for copy in parts:
+def hop_kernel(k, place_ref, heads_ref, up_ref, down_ref, weight_ref, up_out, down_out, ubuf, dbuf, wbuf, sem):
+    columns = wbuf.shape[2]
+    ring, tokens = weight_ref.shape[1] // columns, heads_ref.shape[0]
+    copies = []
+    for j, step in enumerate((k, ring - k)):
+        at = pl.multiple_of(lax.rem(place_ref[0] + step, ring) * columns, columns)
+        copies.append(pltpu.make_async_copy(weight_ref.at[:, pl.ds(at, columns)], wbuf.at[j], sem.at[j]))
+    copies.append(pltpu.make_async_copy(up_ref, ubuf, sem.at[2]))
+    copies.append(pltpu.make_async_copy(down_ref, dbuf, sem.at[3]))
+    for copy in copies:
         copy.start()
-    for k, copy in zip(order, parts):
-        copy.wait()
-        if k == ring // 2:
-            continue
-        block = jnp.dot(heads_ref[...], wout[k], preferred_element_type=F32)
-        if k == 0:
-            own_ref[...] = block
-        else:
-            terms_refs[k - 1 if k < 4 else k - 2][...] = block.astype(BF16)
+    for j, (buf, out, first) in enumerate(((ubuf, up_out, 0), (dbuf, down_out, tokens - dbuf.shape[0]))):
+        copies[j].wait()
+        terms = jnp.dot(heads_ref[...], wbuf[j], preferred_element_type=F32)
+        copies[2 + j].wait()
+        end = first + buf.shape[0]
+        out[first:end, :] = (terms[first:end] + buf[...].astype(F32)).astype(BF16)
+        if first > 0:
+            out[:first, :] = terms[:first].astype(BF16)
+        if end < tokens:
+            out[end:, :] = terms[end:].astype(BF16)
 
 
 def leaving_kernel(plan_ref, asked_ref, keys_ref, values_ref, out_ref, kbuf, vbuf, score, weight):
@@ -268,23 +269,34 @@
             out_ref[entry(i), :, h * head : (h + 1) * head] = o[h * steps : (h + 1) * steps].astype(BF16)
 
 
-def arrived_kernel(place_ref, here_ref, back_ref, weight_ref, out_ref, heads):
+def arrived_kernel(here_ref, back_ref, weight_ref, out_ref, heads, wbuf, wsem):
     steps = back_ref.shape[1]
-    ring, lines, _ = out_ref.shape
-    rows = lines // steps
+    rows, columns = out_ref.shape[1] // steps, out_ref.shape[2]
+    parts = [
+        pltpu.make_async_copy(weight_ref.at[:, pl.ds(k * columns, columns)], wbuf.at[k], wsem.at[k])
+        for k in range(out_ref.shape[0])
+    ]
+    for copy in parts:
+        copy.start()
     for j in range(heads.shape[0] // 16):
         four = [back_ref[here_ref[HERE_ENTRY, min(4 * j + u, rows - 1)]].astype(F32) for u in range(4)]
         heads[16 * j : 16 * j + 16, :] = jnp.concatenate(four, axis=0).astype(BF16)
-    for k in range(ring):
-        terms = jnp.dot(heads[...], weight_ref[k], preferred_element_type=F32)
-        out_ref[lax.rem(place_ref[0] + k, ring)] = terms[:lines].astype(BF16)
-
-
-def place_kernel(plan_ref, own_ref, up_ref, down_ref, out_ref, total):
-    steps = out_ref.shape[1]
-    total[...] = own_ref[...] + up_ref[...].astype(F32) + down_ref[...].astype(F32)
+    for k, copy in enumerate(parts):
+        copy.wait()
+        terms = jnp.dot(heads[...], wbuf[k], preferred_element_type=F32)
+        out_ref[k] = terms[: out_ref.shape[1]].astype(BF16)
+
+
+def place_kernel(place_ref, plan_ref, heads_ref, up_ref, down_ref, weight_ref, out_ref, total, wbuf, sem):
+    steps, columns = out_ref.shape[1:]
+    at = pl.multiple_of(place_ref[0] * columns, columns)
+    copy = pltpu.make_async_copy(weight_ref.at[:, pl.ds(at, columns)], wbuf, sem)
+    copy.start()
     out_ref[...] = jnp.zeros(out_ref.shape, BF16)
-    for i in range(own_ref.shape[0] // steps):
+    copy.wait()
+    own = jnp.dot(heads_ref[...], wbuf[...], preferred_element_type=F32)
+    total[...] = own + up_ref[...].astype(F32) + down_ref[...].astype(F32)
+    for i in range(heads_ref.shape[0] // steps):
 
         @pl.when(i >= plan_ref[STAY_FIRST, 0])
         def _():
@@ -392,67 +404,70 @@
         return lax.ppermute(u, "tp", ahead), lax.ppermute(d, "tp", astern)
 
     def add(k, u, d):
-        return (
-            (terms[k - 1].astype(F32) + u.astype(F32)).astype(BF16),
-            (terms[6 - k].astype(F32) + d.astype(F32)).astype(BF16),
-        )
-
-    table, up, down, fresh, heads = barrier((table, up, down, fresh, heads))
+        return call(
+            functools.partial(hop_kernel, k),
+            [shape((tokens, columns), BF16)] * 2,
+            [SMEM, VMEM] + [pl.BlockSpec(memory_space=pl.ANY)] * 2 + [ANY],
+            [
+                pltpu.VMEM(u.shape, BF16),
+                pltpu.VMEM(d.shape, BF16),
+                pltpu.VMEM((2, wide, columns), BF16),
+                pltpu.SemaphoreType.DMA((4,)),
+            ],
+            flops=HOP_COST,
+        )(place, heads, u, d, out_weight)
+
+    table, fresh, heads, leave_keys = barrier((table, fresh, heads, leave_keys))
     asked, here = call(
         payload_kernel,
         [shape((entries, steps, wide + 2 * head), BF16), shape((8, 128), I32)],
         [SMEM] + [VMEM] * 2,
-        nbytes=2 << 20,
+        flops=PAYLOAD_COST,
     )(table, table, fresh)
     asked, heads = barrier((asked, heads))
     asked = exchange(asked, "group")
-    own, *terms = call(
-        terms_kernel,
-        [shape((tokens, columns), F32)]
-        + [shape((tokens, columns), BF16)] * 6
-        + [shape((ring, wide, columns), BF16)],
-        [SMEM, VMEM, ANY],
-        [pltpu.SemaphoreType.DMA((ring,))],
-        flops=2 * tokens * wide * out_weight.shape[1],
-        nbytes=8 << 20,
-        limit=10,
-    )(place, heads, out_weight)
-    weight = terms.pop()
     up, down = hop(up, down)
-    up = jnp.concatenate([up, jnp.zeros((tokens - cut, columns), BF16)], axis=0)
-    down = jnp.concatenate([jnp.zeros((cut, columns), BF16), down], axis=0)
-
-    asked, up, down = barrier((asked, *add(3, up, down)))
+
+    up, down = add(3, up, down)
+    asked = barrier((asked, up, down))[0]
     up, down = hop(up, down)
     back = call(
         leaving_kernel,
         shape((entries, steps, wide), BF16),
         [SMEM] + [VMEM] * 3,
         scratch(moves, moves),
-        nbytes=4 << 20,
     )(plan, asked, leave_keys, leave_values)
+    back, heads = barrier((back, heads))
     back = exchange(back, "group")
-    back, up, down = barrier((back, *add(2, up, down)))
+    up, down = add(2, up, down)
+    back = barrier((back, up, down))[0]
     up, down = hop(up, down)
     arrived = moves * steps
     blocks = call(
         arrived_kernel,
         shape((ring, arrived, columns), BF16),
-        [SMEM] * 2 + [VMEM] * 2,
-        [pltpu.VMEM((-(-arrived // 16) * 16, wide), BF16)],
-        nbytes=6 << 20,
-    )(place, here, back, weight)
-    blocks, up, down = barrier((blocks, *add(1, up, down)))
+        [SMEM, VMEM, ANY],
+        [
+            pltpu.VMEM((-(-arrived // 16) * 16, wide), BF16),
+            pltpu.VMEM((ring, wide, columns), BF16),
+            pltpu.SemaphoreType.DMA((ring,)),
+        ],
+        flops=ARRIVED_COST,
+        limit=10,
+    )(here, back, out_weight)
+    blocks, heads = barrier((blocks, heads))
+    up, down = add(1, up, down)
+    blocks = barrier((blocks, up, down))[0]
     blocks = exchange(blocks, "tp")
     up, down = hop(up, down)
 
     placed = call(
         place_kernel,
         shape((slots, steps, columns), BF16),
-        [SMEM] + [VMEM] * 3,
-        [pltpu.VMEM((tokens, columns), F32)],
-        nbytes=4 << 20,
-    )(plan, own, up, down)
+        [SMEM] * 2 + [VMEM] * 3 + [ANY],
+        [pltpu.VMEM((tokens, columns), F32), pltpu.VMEM((wide, columns), BF16), pltpu.SemaphoreType.DMA],
+        flops=PLACE_COST,
+    )(place, plan, heads, up, down, out_weight)
     return call(
         finish_kernel,
         shape((slots, steps, columns), BF16),

time: 111 us -> 99.2 us (0.89)
  Pallas kernels: 22.4 us -> 27.9 us
  waiting for transfers between devices: 35.4 us -> 30.3 us
  other arithmetic: 4.99 us -> 0 us
  local copies, waits for them, and re-layouts: 5.81 us -> 1.56 us
  starting transfers between devices: 41.7 us -> 38.8 us
    ppermute x8, waiting for transfers between devices: 28.1 us -> 3.07 us  [hop(): return (lax.ppermute(u, 'tp', ahead), lax.ppermute(d, 'tp', astern))]
    all_to_all x4, waiting for transfers between devices: 7.29 us -> 27.2 us  [exchange(): return lax.all_to_all(x, axis, split_axis=0, concat_axis=0, tiled=True)]
    pallas_call x3 -> x5, Pallas kernels: 7.12 us -> 12.6 us  [the longest x3 5.49 us: add(): call(functools.partial(hop_kernel, k), [shape((tokens, columns), BF16)] *...]
    convert_element_type x6 -> x0, other arithmetic: 4.99 us -> none  [the longest x3 3.01 us: add(): (terms[6 - k].astype(F32) + d.astype(F32)).astype(BF16)]
    unnamed x12 -> x4, local copies, waits for them, and re-layouts: 5.81 us -> 1.56 us
    all_to_all x4, starting transfers between devices: 27.9 us -> 24.4 us  [exchange(): return lax.all_to_all(x, axis, split_axis=0, concat_axis=0, tiled=True)]
  transfers between devices with their start and end apart: 12 -> 12, of which waited for: 4 -> 4; matrix products, arithmetic and copies ran while one was open for 4% -> 0% of each run, Pallas kernels for 17% -> 23%
where the time goes in v5:
time: 99.2 us; the launch traced here: 98.7 us
  starting transfers between devices  38.8 us (39%)
  waiting for transfers between devices  30.3 us (31%)
  Pallas kernels  27.9 us (28%)
  local copies, waits for them, and re-layouts  1.56 us (2%)
    all_to_all x4, waiting for transfers between devices, exchange(): return lax.all_to_all(x, axis, split_axis=0, concat_axis=0, tiled=True)  27.2 us
    all_to_all x4, starting transfers between devices, exchange(): return lax.all_to_all(x, axis, split_axis=0, concat_axis=0, tiled=True)  24.4 us
    ppermute x8, starting transfers between devices, hop(): return (lax.ppermute(u, 'tp', ahead), lax.ppermute(d, 'tp', astern))  14.4 us
    pallas_call x1, Pallas kernels, on_device(): call(staying_kernel, [shape((cut, columns), BF16), shape((tokens - cut, c...  8.07 us
    pallas_call x3, Pallas kernels, add(): call(functools.partial(hop_kernel, k), [shape((tokens, columns), BF16)] *...  5.49 us
    pallas_call x1, Pallas kernels, on_device(): call(arrived_kernel, shape((ring, arrived, columns), BF16), [SMEM, VMEM,...  4.43 us
    ppermute x8, waiting for transfers between devices, hop(): return (lax.ppermute(u, 'tp', ahead), lax.ppermute(d, 'tp', astern))  3.07 us
    pallas_call x1, Pallas kernels, on_device(): call(place_kernel, shape((slots, steps, columns), BF16), [SMEM] * 2 + [VM...  2.72 us
  transfers between devices with their start and end apart: 12, of which 4 were waited for; matrix products, arithmetic and copies ran while one was open for 0% of the time, Pallas kernels for 23%

profile of v5, /device:TPU:1, one launch (start us, length us, event | category | flops | bytes accessed | tf_op | source)
XLA Modules:
  0.0 98.7 jit_solution(9990857764759167890)
XLA Ops:
  0.0 1.5 %shard_map.91 = (s32[32,128]{1,0:T(8,128)}, s32[8,128]{1,0:T(8,128)S(1)}) custom-call(s32[3,26]{1,0:T(4,128)} %bitcast.10, s32[1,128]{1,0:T(1,128)} %bitcast.11, s32[1,128]{1,0:T(1,128)} %bitcast.12), custom_call_target="tpu_custom_call" | custom-call | bytes 65536 | tf_op jit(solution)/shard_map/pallas_call | solution.py:359
  1.5 8.6 %all-to-all-start = ((s32[32,1,128]{2,1,0:T(1,128)}), s32[32,1,128]{2,1,0:T(1,128)S(1)}, u32[]{:S(2)}, u32[]{:S(2)}) async-start(s32[32,1,128]{2,1,0:T(1,128)} %bitcast.4), calls=%async_computation | async-start | bytes 32768 | tf_op jit(solution)/shard_map/all_to_all | solution.py:349
  10.2 8.1 %shard_map.92 = (bf16[160,512]{1,0:T(8,128)(2,1)S(1)}, bf16[144,512]{1,0:T(8,128)(2,1)}, bf16[304,512]{1,0:T(8,128)(2,1)S(1)}, bf16[128,4,768]{2,1,0:T(4,128)(2,...) custom-call(s32[1]{0:T(128)} %bitcast.6.place_ref, ...), custom_call_target="tpu_custom_call" | custom-call | flops 159383552 | bytes 16777216 | tf_op jit(solution)/shard_map/pallas_call | solution.py:375
  18.2 5.7 %collective-permute-start.1 = (bf16[144,512]{1,0:T(8,128)(2,1)}, bf16[144,512]{1,0:T(8,128)(2,1)}, u32[]{:S(2)}, u32[]{:S(2)}) collective-permute-start(bf16[144,512]{1,0:T(8,128)(2,1)} %get-tuple-element.47), channel_id=1, source_target_pairs={{0,7},{1,0},{2,1},{3,2},{4,3},{5,4},{6,5},{7,6},{8,15},{9,8},{10,9... | collective-permute-start | bytes 442376 | tf_op jit(solution)/shard_map/ppermute | solution.py:404
  23.9 1.8 %shard_map.93 = (bf16[64,4,768]{2,1,0:T(4,128)(2,1)}, s32[8,128]{1,0:T(8,128)S(1)}) custom-call(s32[32,128]{1,0:T(8,128)S(1)} %bitcast.8, s32[32,128]{1,0:T(8,128)S(1)} %bitcast.9, bf16[128,4,768]{2,1,0:T(4,128)(2,1)S(1)} %get-tuple-element.40.fresh_ref), custom_call_target="tpu_custom_call" | custom-call | flops 8000000000 | tf_op jit(solution)/shard_map/pallas_call | solution.py:421
  25.7 7.6 %all-to-all-start.1 = ((bf16[64,4,768]{2,1,0:T(4,128)(2,1)}), bf16[64,4,768]{2,1,0:T(4,128)(2,1)S(1)}, u32[]{:S(2)}, u32[]{:S(2)}) async-start(bf16[64,4,768]{2,1,0:T(4,128)(2,1)} %get-tuple-element.44), calls=%async_computation.1 | async-start | bytes 786432 | tf_op jit(solution)/shard_map/all_to_all | solution.py:349
  33.4 0.6 copy-done
  34.0 0.9 copy-done.1
  34.9 1.8 %shard_map.94 = (bf16[304,512]{1,0:T(8,128)(2,1)S(1)}, bf16[304,512]{1,0:T(8,128)(2,1)S(1)}) custom-call(s32[1]{0:T(128)} %bitcast.6.place_ref, bf16[304,512]{1,0:T(8,128)(2,1)S(1)} %get-tuple-element.58.heads_ref, bf16[160,512]{1,0:T(8,128)(2,1)S(1)} %copy-done.1, bf16[144,512]{1,0:T(8,128)(2,1)} %collective-permute-done.1.down_ref, ...), custom_call_target="tpu_custom_call" | custom-call | flops 20000000000 | tf_op jit(solution)/shard_map/pallas_call | solution.py:407
  36.8 3.0 %collective-permute-start.3 = (bf16[304,512]{1,0:T(8,128)(2,1)S(1)}, bf16[304,512]{1,0:T(8,128)(2,1)}, u32[]{:S(2)}, u32[]{:S(2)}) collective-permute-start(bf16[304,512]{1,0:T(8,128)(2,1)S(1)} %get-tuple-element.49), channel_id=1, source_target_pairs={{0,7},{1,0},{2,1},{3,2},{4,3},{5,4},{6,5},{7,6},{8,15},{9,8},{10,9... | collective-permute-start | bytes 933896 | tf_op jit(solution)/shard_map/ppermute | solution.py:404
  39.8 3.8 %all-to-all-done.1.asked_ref = bf16[64,4,768]{2,1,0:T(4,128)(2,1)S(1)} async-done(((bf16[64,4,768]{2,1,0:T(4,128)(2,1)}), bf16[64,4,768]{2,1,0:T(4,128)(2,1)S(1)}, u32[]{:S(2)}, u32[]{:S(2)}) %all-to-all-start.1) | async-done | bytes 393248 | tf_op jit(solution)/shard_map/all_to_all | solution.py:349
  43.6 2.3 %shard_map.95 = bf16[64,4,512]{2,1,0:T(4,128)(2,1)} custom-call(s32[8,128]{1,0:T(8,128)S(1)} %get-tuple-element.35.plan_ref, bf16[64,4,768]{2,1,0:T(4,128)(2,1)S(1)} %all-to-all-done.1.asked_ref, bf16[26,128,128]{2,1,0:T(8,128)(2,1)S(1)} %get-tuple-element.51.keys_ref, bf16[26,128,128]{2,1,0:T(8,128)(2,1)S(1)} %get-tuple-element.52.values_ref), custom_call_target="tpu_custom_call" | custom-call | tf_op jit(solution)/shard_map/pallas_call | solution.py:434
  45.9 3.9 %all-to-all-start.2 = ((bf16[64,4,512]{2,1,0:T(4,128)(2,1)}), bf16[64,4,512]{2,1,0:T(4,128)(2,1)S(1)}, u32[]{:S(2)}, u32[]{:S(2)}) async-start(bf16[64,4,512]{2,1,0:T(4,128)(2,1)} %shard_map.95), calls=%async_computation.2 | async-start | bytes 524288 | tf_op jit(solution)/shard_map/all_to_all | solution.py:349
  49.8 1.8 %shard_map.96 = (bf16[304,512]{1,0:T(8,128)(2,1)S(1)}, bf16[304,512]{1,0:T(8,128)(2,1)S(1)}) custom-call(s32[1]{0:T(128)} %bitcast.6.place_ref, bf16[304,512]{1,0:T(8,128)(2,1)S(1)} %get-tuple-element.58.heads_ref, bf16[304,512]{1,0:T(8,128)(2,1)S(1)} %collective-permute-done.2.up_ref, bf16[304,512]{1,0:T(8,128)(2,1)} %collective-permute-done.3.down_ref, ...), custom_call_target="tpu_custom_call" | custom-call | flops 20000000000 | tf_op jit(solution)/shard_map/pallas_call | solution.py:407
  51.8 2.8 %collective-permute-start.5 = (bf16[304,512]{1,0:T(8,128)(2,1)S(1)}, bf16[304,512]{1,0:T(8,128)(2,1)S(1)}, u32[]{:S(2)}, u32[]{:S(2)}) collective-permute-start(bf16[304,512]{1,0:T(8,128)(2,1)S(1)} %get-tuple-element.56), channel_id=1, source_target_pairs={{0,7},{1,0},{2,1},{3,2},{4,3},{5,4},{6,5},{7,6},{8,15},{9,8},{10,9... | collective-permute-start | bytes 933896 | tf_op jit(solution)/shard_map/ppermute | solution.py:404
  54.6 4.2 %all-to-all-done.2.back_ref = bf16[64,4,512]{2,1,0:T(4,128)(2,1)S(1)} async-done(((bf16[64,4,512]{2,1,0:T(4,128)(2,1)}), bf16[64,4,512]{2,1,0:T(4,128)(2,1)S(1)}, u32[]{:S(2)}, u32[]{:S(2)}) %all-to-all-start.2) | async-done | bytes 262176 | tf_op jit(solution)/shard_map/all_to_all | solution.py:349
  58.8 4.4 %shard_map.97 = bf16[8,104,512]{2,1,0:T(8,128)(2,1)} custom-call(s32[8,128]{1,0:T(8,128)S(1)} %get-tuple-element.41.here_ref, bf16[64,4,512]{2,1,0:T(4,128)(2,1)S(1)} %all-to-all-done.2.back_ref, bf16[512,4096]{1,0:T(8,128)(2,1)} %weight_ref.11), custom_call_target="tpu_custom_call" | custom-call | flops 8000000000 | tf_op jit(solution)/shard_map/pallas_call | solution.py:446
  63.2 1.8 %shard_map.98 = (bf16[304,512]{1,0:T(8,128)(2,1)S(1)}, bf16[304,512]{1,0:T(8,128)(2,1)S(1)}) custom-call(s32[1]{0:T(128)} %bitcast.6.place_ref, bf16[304,512]{1,0:T(8,128)(2,1)S(1)} %get-tuple-element.58.heads_ref, bf16[304,512]{1,0:T(8,128)(2,1)S(1)} %collective-permute-done.4.up_ref, bf16[304,512]{1,0:T(8,128)(2,1)S(1)} %collective-permute-done.5.down_ref, ...), custom_call_target="tpu_custom_call" | custom-call | flops 20000000000 | tf_op jit(solution)/shard_map/pallas_call | solution.py:407
  65.2 2.7 %collective-permute-start.7 = (bf16[304,512]{1,0:T(8,128)(2,1)S(1)}, bf16[304,512]{1,0:T(8,128)(2,1)S(1)}, u32[]{:S(2)}, u32[]{:S(2)}) collective-permute-start(bf16[304,512]{1,0:T(8,128)(2,1)S(1)} %get-tuple-element.60), channel_id=1, source_target_pairs={{0,7},{1,0},{2,1},{3,2},{4,3},{5,4},{6,5},{7,6},{8,15},{9,8},{10,9... | collective-permute-start | bytes 933896 | tf_op jit(solution)/shard_map/ppermute | solution.py:404
  67.9 4.2 %all-to-all-start.3 = ((bf16[8,104,512]{2,1,0:T(8,128)(2,1)}), bf16[8,104,512]{2,1,0:T(8,128)(2,1)S(1)}, u32[]{:S(2)}, u32[]{:S(2)}) async-start(bf16[8,104,512]{2,1,0:T(8,128)(2,1)} %shard_map.97), calls=%async_computation.3 | async-start | bytes 1703936 | tf_op jit(solution)/shard_map/all_to_all | solution.py:349
  72.1 3.0 %collective-permute-done.6.up_ref = bf16[304,512]{1,0:T(8,128)(2,1)S(1)} collective-permute-done((bf16[304,512]{1,0:T(8,128)(2,1)S(1)}, bf16[304,512]{1,0:T(8,128)(2,1)S(1)}, u32[]{:S(2)}, u32[]{:S(2)}) %collective-permute-start.6) | collective-permute-done | bytes 311328 | tf_op jit(solution)/shard_map/ppermute | solution.py:404
  75.2 2.7 %shard_map.99.placed_ref = bf16[128,4,512]{2,1,0:T(4,128)(2,1)S(1)} custom-call(s32[1]{0:T(128)} %bitcast.6.place_ref, s32[8,128]{1,0:T(8,128)S(1)} %get-tuple-element.35.plan_ref, bf16[304,512]{1,0:T(8,128)(2,1)S(1)} %get-tuple-element.58.heads_ref, bf16[304,512]{1,0:T(8,128)(2,1)S(1)} %collective-permute-done.6.up_ref, ...), custom_call_target="tpu_custom_call" | custom-call | flops 40000000000 | tf_op jit(solution)/shard_map/pallas_call | solution.py:464
  77.9 19.2 %all-to-all-done.3.blocks_ref = bf16[8,104,512]{2,1,0:T(8,128)(2,1)S(1)} async-done(((bf16[8,104,512]{2,1,0:T(8,128)(2,1)}), bf16[8,104,512]{2,1,0:T(8,128)(2,1)S(1)}, u32[]{:S(2)}, u32[]{:S(2)}) %all-to-all-start.3) | async-done | bytes 852000 | tf_op jit(solution)/shard_map/all_to_all | solution.py:349
  97.1 1.6 %shard_map.100 = bf16[128,4,512]{2,1,0:T(4,128)(2,1)} custom-call(s32[8,128]{1,0:T(8,128)S(1)} %get-tuple-element.41.here_ref, bf16[128,4,512]{2,1,0:T(4,128)(2,1)S(1)} %shard_map.99.placed_ref, bf16[8,104,512]{2,1,0:T(8,128)(2,1)S(1)} %all-to-all-done.3.blocks_ref), custom_call_target="tpu_custom_call" | custom-call | bytes 2097152 | tf_op jit(solution)/shard_map/pallas_call | solution.py:471
  (14 shorter events, 0.3 us)
Async XLA Ops:
  1.5 22.3 %all-to-all-start = ((s32[32,1,128]{2,1,0:T(1,128)}), s32[32,1,128]{2,1,0:T(1,128)S(1)}, u32[]{:S(2)}, u32[]{:S(2)}) async-start(s32[32,1,128]{2,1,0:T(1,128)} %bitcast.4), calls=%async_computation | async-start | bytes 32768 | tf_op jit(solution)/shard_map/all_to_all | solution.py:349
  18.2 15.1 %collective-permute-start.1 = (bf16[144,512]{1,0:T(8,128)(2,1)}, bf16[144,512]{1,0:T(8,128)(2,1)}, u32[]{:S(2)}, u32[]{:S(2)}) collective-permute-start(bf16[144,512]{1,0:T(8,128)(2,1)} %get-tuple-element.47), channel_id=1, source_target_pairs={{0,7},{1,0},{2,1},{3,2},{4,3},{5,4},{6,5},{7,6},{8,15},{9,8},{10,9... | collective-permute-start | bytes 442376 | tf_op jit(solution)/shard_map/ppermute | solution.py:404
  23.9 9.5 %collective-permute-start = (bf16[160,512]{1,0:T(8,128)(2,1)S(1)}, bf16[160,512]{1,0:T(8,128)(2,1)S(1)}, u32[]{:S(2)}, u32[]{:S(2)}) collective-permute-start(bf16[160,512]{1,0:T(8,128)(2,1)S(1)} %get-tuple-element.46), channel_id=1, source_target_pairs={{0,1},{1,2},{2,3},{3,4},{4,5},{5,6},{6,7},{7,0},{8,9},{9,10},{10,1... | collective-permute-start | bytes 491528 | tf_op jit(solution)/shard_map/ppermute | solution.py:404
  25.7 18.0 %all-to-all-start.1 = ((bf16[64,4,768]{2,1,0:T(4,128)(2,1)}), bf16[64,4,768]{2,1,0:T(4,128)(2,1)S(1)}, u32[]{:S(2)}, u32[]{:S(2)}) async-start(bf16[64,4,768]{2,1,0:T(4,128)(2,1)} %get-tuple-element.44), calls=%async_computation.1 | async-start | bytes 786432 | tf_op jit(solution)/shard_map/all_to_all | solution.py:349
  33.3 0.7 copy-start
  34.0 0.9 copy-start.1
  36.7 13.1 %collective-permute-start.2 = (bf16[304,512]{1,0:T(8,128)(2,1)S(1)}, bf16[304,512]{1,0:T(8,128)(2,1)S(1)}, u32[]{:S(2)}, u32[]{:S(2)}) collective-permute-start(bf16[304,512]{1,0:T(8,128)(2,1)S(1)} %get-tuple-element.48), channel_id=1, source_target_pairs={{0,1},{1,2},{2,3},{3,4},{4,5},{5,6},{6,7},{7,0},{8,9},{9,10},{10,1... | collective-permute-start | bytes 933896 | tf_op jit(solution)/shard_map/ppermute | solution.py:404
  36.8 13.0 %collective-permute-start.3 = (bf16[304,512]{1,0:T(8,128)(2,1)S(1)}, bf16[304,512]{1,0:T(8,128)(2,1)}, u32[]{:S(2)}, u32[]{:S(2)}) collective-permute-start(bf16[304,512]{1,0:T(8,128)(2,1)S(1)} %get-tuple-element.49), channel_id=1, source_target_pairs={{0,7},{1,0},{2,1},{3,2},{4,3},{5,4},{6,5},{7,6},{8,15},{9,8},{10,9... | collective-permute-start | bytes 933896 | tf_op jit(solution)/shard_map/ppermute | solution.py:404
  45.9 12.9 %all-to-all-start.2 = ((bf16[64,4,512]{2,1,0:T(4,128)(2,1)}), bf16[64,4,512]{2,1,0:T(4,128)(2,1)S(1)}, u32[]{:S(2)}, u32[]{:S(2)}) async-start(bf16[64,4,512]{2,1,0:T(4,128)(2,1)} %shard_map.95), calls=%async_computation.2 | async-start | bytes 524288 | tf_op jit(solution)/shard_map/all_to_all | solution.py:349
  51.7 11.6 %collective-permute-start.4 = (bf16[304,512]{1,0:T(8,128)(2,1)S(1)}, bf16[304,512]{1,0:T(8,128)(2,1)S(1)}, u32[]{:S(2)}, u32[]{:S(2)}) collective-permute-start(bf16[304,512]{1,0:T(8,128)(2,1)S(1)} %get-tuple-element.55), channel_id=1, source_target_pairs={{0,1},{1,2},{2,3},{3,4},{4,5},{5,6},{6,7},{7,0},{8,9},{9,10},{10,1... | collective-permute-start | bytes 933896 | tf_op jit(solution)/shard_map/ppermute | solution.py:404
  51.8 11.5 %collective-permute-start.5 = (bf16[304,512]{1,0:T(8,128)(2,1)S(1)}, bf16[304,512]{1,0:T(8,128)(2,1)S(1)}, u32[]{:S(2)}, u32[]{:S(2)}) collective-permute-start(bf16[304,512]{1,0:T(8,128)(2,1)S(1)} %get-tuple-element.56), channel_id=1, source_target_pairs={{0,7},{1,0},{2,1},{3,2},{4,3},{5,4},{6,5},{7,6},{8,15},{9,8},{10,9... | collective-permute-start | bytes 933896 | tf_op jit(solution)/shard_map/ppermute | solution.py:404
  65.1 10.1 %collective-permute-start.6 = (bf16[304,512]{1,0:T(8,128)(2,1)S(1)}, bf16[304,512]{1,0:T(8,128)(2,1)S(1)}, u32[]{:S(2)}, u32[]{:S(2)}) collective-permute-start(bf16[304,512]{1,0:T(8,128)(2,1)S(1)} %get-tuple-element.59), channel_id=1, source_target_pairs={{0,1},{1,2},{2,3},{3,4},{4,5},{5,6},{6,7},{7,0},{8,9},{9,10},{10,1... | collective-permute-start | bytes 933896 | tf_op jit(solution)/shard_map/ppermute | solution.py:404
  65.2 10.0 %collective-permute-start.7 = (bf16[304,512]{1,0:T(8,128)(2,1)S(1)}, bf16[304,512]{1,0:T(8,128)(2,1)S(1)}, u32[]{:S(2)}, u32[]{:S(2)}) collective-permute-start(bf16[304,512]{1,0:T(8,128)(2,1)S(1)} %get-tuple-element.60), channel_id=1, source_target_pairs={{0,7},{1,0},{2,1},{3,2},{4,3},{5,4},{6,5},{7,6},{8,15},{9,8},{10,9... | collective-permute-start | bytes 933896 | tf_op jit(solution)/shard_map/ppermute | solution.py:404
  67.9 29.2 %all-to-all-start.3 = ((bf16[8,104,512]{2,1,0:T(8,128)(2,1)}), bf16[8,104,512]{2,1,0:T(8,128)(2,1)S(1)}, u32[]{:S(2)}, u32[]{:S(2)}) async-start(bf16[8,104,512]{2,1,0:T(8,128)(2,1)} %shard_map.97), calls=%async_computation.3 | async-start | bytes 1703936 | tf_op jit(solution)/shard_map/all_to_all | solution.py:349

commit v6 on v5

--- a/solution.py
+++ b/solution.py
@@ -16,13 +16,13 @@
 ANY = pl.BlockSpec(memory_space=pltpu.HBM)
 
 
-def call(kernel, out_shape, in_specs, scratch=(), flops=0, nbytes=0, exps=0, limit=8):
+def call(kernel, out_shape, in_specs, scratch=(), flops=0, nbytes=0, exps=0, limit=8, out=VMEM):
     single = isinstance(out_shape, jax.ShapeDtypeStruct)
     return pl.pallas_call(
         kernel,
         out_shape=out_shape,
         in_specs=in_specs,
-        out_specs=VMEM if single else [VMEM] * len(out_shape),
+        out_specs=out if single else [out] * len(out_shape),
         scratch_shapes=list(scratch),
         cost_estimate=pl.CostEstimate(
             flops=flops, bytes_accessed=nbytes, transcendentals=exps
@@ -97,9 +97,9 @@
 HERE_ENTRY, HERE_SLOT = range(2)
 
 
-def payload_kernel(slot_ref, table_ref, fresh_ref, out_ref, here_ref):
-    for e in range(out_ref.shape[0]):
-        out_ref[e] = fresh_ref[jnp.maximum(slot_ref[e // CAP, e % CAP] - 1, 0)]
+def payload_kernel(slot_src, table_ref, fresh_ref, out_ref, here_ref, slot_ref, sem):
+    copy = pltpu.make_async_copy(slot_src, slot_ref, sem)
+    copy.start()
     groups, width = table_ref.shape
     table = table_ref[...]
     there = (table > 0).astype(F32)
@@ -118,6 +118,9 @@
     here_ref[...] = jnp.zeros(here_ref.shape, I32)
     here_ref[HERE_ENTRY : HERE_ENTRY + 1, :] = entry.astype(I32)
     here_ref[HERE_SLOT : HERE_SLOT + 1, :] = slot.astype(I32)
+    copy.wait()
+    for e in range(out_ref.shape[0]):
+        out_ref[e] = fresh_ref[jnp.maximum(slot_ref[e // CAP, e % CAP] - 1, 0)]
 
 
 def attend(batches, kbuf, vbuf, score, weight, cache, steps, heads, row_of, query_of, fresh_of, length_of, await_keys, await_values):
@@ -146,13 +149,12 @@
             score[i * lines : (i + 1) * lines, :] = jnp.where(
                 (lane < length_of(i)) | visible, products * head**-0.5, -jnp.inf
             )
-    for batch in batches:
+    mixed = []
+    for b, batch in enumerate(batches):
         chunk = slice(batch[0] * lines, (batch[-1] + 1) * lines)
         s = score[chunk, :]
         e = jnp.exp(s - jnp.max(s, axis=1, keepdims=True))
         weight[chunk, :] = (e * (1.0 / jnp.sum(e, axis=1, keepdims=True))).astype(BF16)
-    mixed = []
-    for b, batch in enumerate(batches):
         await_values(b)
         for i in batch:
             mixed.append(
@@ -162,9 +164,9 @@
 
 
 def staying_kernel(
-    place_ref, plan_ref, query_ref, key_ref, value_ref, keys_ref, values_ref, weight_ref,
+    plan_src, query_ref, key_ref, value_ref, keys_ref, values_ref, weight_ref,
     up_ref, down_ref, heads_ref, fresh_ref, leave_keys_ref, leave_values_ref,
-    kbuf, vbuf, score, weight, wbuf, fsem, ksem, vsem, wsem,
+    plan_ref, kbuf, vbuf, score, weight, wbuf, psem, fsem, ksem, vsem, wsem,
 ):
     steps, wide = query_ref.shape[1:]
     slots, _, cache, head = keys_ref.shape
@@ -184,9 +186,10 @@
         ]
         for ref, buf, sem in ((keys_ref, kbuf, ksem), (values_ref, vbuf, vsem))
     )
-    at = lax.rem(place_ref[0] + ring // 2, ring) * columns
+    listed = pltpu.make_async_copy(plan_src, plan_ref, psem)
+    at = lax.rem(lax.axis_index("tp") + ring // 2, ring) * columns
     far = pltpu.make_async_copy(weight_ref.at[:, pl.ds(pl.multiple_of(at, columns), columns)], wbuf, wsem)
-    for copy in fresh + keys + values + [far]:
+    for copy in [listed] + fresh + keys + values + [far]:
         copy.start()
 
     last = [(slots - rows + i) // chunk for i in range(rows)]
@@ -196,7 +199,7 @@
     def slot(i):
         return plan_ref[STAY_SLOT, i]
 
-    for copy in fresh:
+    for copy in [listed] + fresh:
         copy.wait()
     mixed = attend(
         batches, kbuf, vbuf, score, weight, cache, steps, wide // head,
@@ -221,12 +224,12 @@
     down_ref[...] = block[cut:].astype(BF16)
 
 
-def hop_kernel(k, place_ref, heads_ref, up_ref, down_ref, weight_ref, up_out, down_out, ubuf, dbuf, wbuf, sem):
+def hop_kernel(k, heads_ref, up_ref, down_ref, weight_ref, up_out, down_out, ubuf, dbuf, wbuf, sem):
     columns = wbuf.shape[2]
     ring, tokens = weight_ref.shape[1] // columns, heads_ref.shape[0]
     copies = []
     for j, step in enumerate((k, ring - k)):
-        at = pl.multiple_of(lax.rem(place_ref[0] + step, ring) * columns, columns)
+        at = pl.multiple_of(lax.rem(lax.axis_index("tp") + step, ring) * columns, columns)
         copies.append(pltpu.make_async_copy(weight_ref.at[:, pl.ds(at, columns)], wbuf.at[j], sem.at[j]))
     copies.append(pltpu.make_async_copy(up_ref, ubuf, sem.at[2]))
     copies.append(pltpu.make_async_copy(down_ref, dbuf, sem.at[3]))
@@ -244,13 +247,16 @@
             out[end:, :] = terms[end:].astype(BF16)
 
 
-def leaving_kernel(plan_ref, asked_ref, keys_ref, values_ref, out_ref, kbuf, vbuf, score, weight):
+def leaving_kernel(plan_src, asked_ref, keys_ref, values_ref, out_ref, plan_ref, kbuf, vbuf, score, weight, psem):
+    listed = pltpu.make_async_copy(plan_src, plan_ref, psem)
+    listed.start()
     rows, cache, head = keys_ref.shape
     steps, wide = out_ref.shape[1:]
     out_ref[...] = jnp.zeros(out_ref.shape, BF16)
     for i in range(rows):
         kbuf[i, 0:cache, :] = keys_ref[i]
         vbuf[i, 0:cache, :] = values_ref[i]
+    listed.wait()
 
     def entry(i):
         return plan_ref[LEAVE_ENTRY, i]
@@ -269,27 +275,36 @@
             out_ref[entry(i), :, h * head : (h + 1) * head] = o[h * steps : (h + 1) * steps].astype(BF16)
 
 
-def arrived_kernel(here_ref, back_ref, weight_ref, out_ref, heads, wbuf, wsem):
+def arrived_kernel(here_src, back_ref, weight_ref, out_ref, here_ref, heads, wbuf, sums, hsem, wsem, osem):
+    listed = pltpu.make_async_copy(here_src, here_ref, hsem)
+    listed.start()
     steps = back_ref.shape[1]
-    rows, columns = out_ref.shape[1] // steps, out_ref.shape[2]
+    ring, lines, columns = out_ref.shape
+    rows = lines // steps
     parts = [
         pltpu.make_async_copy(weight_ref.at[:, pl.ds(k * columns, columns)], wbuf.at[k], wsem.at[k])
-        for k in range(out_ref.shape[0])
+        for k in range(ring)
     ]
     for copy in parts:
         copy.start()
+    listed.wait()
     for j in range(heads.shape[0] // 16):
         four = [back_ref[here_ref[HERE_ENTRY, min(4 * j + u, rows - 1)]].astype(F32) for u in range(4)]
         heads[16 * j : 16 * j + 16, :] = jnp.concatenate(four, axis=0).astype(BF16)
+    done = []
     for k, copy in enumerate(parts):
         copy.wait()
         terms = jnp.dot(heads[...], wbuf[k], preferred_element_type=F32)
-        out_ref[k] = terms[: out_ref.shape[1]].astype(BF16)
-
-
-def place_kernel(place_ref, plan_ref, heads_ref, up_ref, down_ref, weight_ref, out_ref, total, wbuf, sem):
+        sums[k] = terms[:lines].astype(BF16)
+        done.append(pltpu.make_async_copy(sums.at[k], out_ref.at[k], osem.at[k]))
+        done[k].start()
+    for copy in done:
+        copy.wait()
+
+
+def place_kernel(plan_ref, heads_ref, up_ref, down_ref, weight_ref, out_ref, total, wbuf, sem):
     steps, columns = out_ref.shape[1:]
-    at = pl.multiple_of(place_ref[0] * columns, columns)
+    at = pl.multiple_of(lax.axis_index("tp") * columns, columns)
     copy = pltpu.make_async_copy(weight_ref.at[:, pl.ds(at, columns)], wbuf, sem)
     copy.start()
     out_ref[...] = jnp.zeros(out_ref.shape, BF16)
@@ -303,13 +318,16 @@
             out_ref[plan_ref[STAY_SLOT, i]] = total[i * steps : (i + 1) * steps, :].astype(BF16)
 
 
-def finish_kernel(here_ref, placed_ref, blocks_ref, out_ref, total):
+def finish_kernel(here_src, placed_ref, blocks_ref, out_ref, here_ref, total, hsem):
+    listed = pltpu.make_async_copy(here_src, here_ref, hsem)
+    listed.start()
     steps = out_ref.shape[1]
     out_ref[...] = placed_ref[...]
     terms = blocks_ref[0].astype(F32)
     for k in range(1, blocks_ref.shape[0]):
         terms = terms + blocks_ref[k].astype(F32)
     total[...] = terms
+    listed.wait()
     for n in range(blocks_ref.shape[1] // steps):
         out_ref[here_ref[HERE_SLOT, n]] = total[n * steps : (n + 1) * steps, :].astype(BF16)
 
@@ -335,7 +353,6 @@
     staying = slots - 2 * moves
     lines = wide // head * steps
     positions = cache + FRESH
-    place = lax.axis_index("tp").astype(I32).reshape(1)
     barrier = lax.optimization_barrier
     keys_cache, values_cache, out_weight, queries, new_keys, new_values, moves_t, flags, reach = (
         pltpu.with_memory_space_constraint(x, pltpu.HBM)
@@ -382,10 +399,12 @@
             shape((moves, cache, head), BF16),
             shape((moves, cache, head), BF16),
         ],
-        [SMEM] * 2 + [ANY] * 6,
-        scratch(slots, staying)
+        [pl.BlockSpec(memory_space=pl.ANY)] + [ANY] * 6,
+        [pltpu.SMEM((8, slots), I32)]
+        + scratch(slots, staying)
         + [
             pltpu.VMEM((wide, columns), BF16),
+            pltpu.SemaphoreType.DMA,
             pltpu.SemaphoreType.DMA((3,)),
             pltpu.SemaphoreType.DMA((4,)),
             pltpu.SemaphoreType.DMA((4,)),
@@ -395,7 +414,7 @@
         nbytes=16 << 20,
         exps=tokens * positions * 4,
         limit=24,
-    )(place, plan, queries, new_keys, new_values, keys_cache, values_cache, out_weight)
+    )(plan, queries, new_keys, new_values, keys_cache, values_cache, out_weight)
 
     ahead = [(i, (i + 1) % ring) for i in range(ring)]
     astern = [(i, (i - 1) % ring) for i in range(ring)]
@@ -407,7 +426,7 @@
         return call(
             functools.partial(hop_kernel, k),
             [shape((tokens, columns), BF16)] * 2,
-            [SMEM, VMEM] + [pl.BlockSpec(memory_space=pl.ANY)] * 2 + [ANY],
+            [VMEM] + [pl.BlockSpec(memory_space=pl.ANY)] * 2 + [ANY],
             [
                 pltpu.VMEM(u.shape, BF16),
                 pltpu.VMEM(d.shape, BF16),
@@ -415,13 +434,14 @@
                 pltpu.SemaphoreType.DMA((4,)),
             ],
             flops=HOP_COST,
-        )(place, heads, u, d, out_weight)
+        )(heads, u, d, out_weight)
 
     table, fresh, heads, leave_keys = barrier((table, fresh, heads, leave_keys))
     asked, here = call(
         payload_kernel,
         [shape((entries, steps, wide + 2 * head), BF16), shape((8, 128), I32)],
-        [SMEM] + [VMEM] * 2,
+        [pl.BlockSpec(memory_space=pl.ANY)] + [VMEM] * 2,
+        [pltpu.SMEM((groups, 128), I32), pltpu.SemaphoreType.DMA],
         flops=PAYLOAD_COST,
     )(table, table, fresh)
     asked, heads = barrier((asked, heads))
@@ -434,8 +454,8 @@
     back = call(
         leaving_kernel,
         shape((entries, steps, wide), BF16),
-        [SMEM] + [VMEM] * 3,
-        scratch(moves, moves),
+        [pl.BlockSpec(memory_space=pl.ANY)] + [VMEM] * 3,
+        [pltpu.SMEM((8, slots), I32)] + scratch(moves, moves) + [pltpu.SemaphoreType.DMA],
     )(plan, asked, leave_keys, leave_values)
     back, heads = barrier((back, heads))
     back = exchange(back, "group")
@@ -446,12 +466,17 @@
     blocks = call(
         arrived_kernel,
         shape((ring, arrived, columns), BF16),
-        [SMEM, VMEM, ANY],
+        [pl.BlockSpec(memory_space=pl.ANY), VMEM, ANY],
         [
+            pltpu.SMEM((8, 128), I32),
             pltpu.VMEM((-(-arrived // 16) * 16, wide), BF16),
             pltpu.VMEM((ring, wide, columns), BF16),
+            pltpu.VMEM((ring, arrived, columns), BF16),
+            pltpu.SemaphoreType.DMA,
+            pltpu.SemaphoreType.DMA((ring,)),
             pltpu.SemaphoreType.DMA((ring,)),
         ],
+        out=ANY,
         flops=ARRIVED_COST,
         limit=10,
     )(here, back, out_weight)
@@ -464,15 +489,15 @@
     placed = call(
         place_kernel,
         shape((slots, steps, columns), BF16),
-        [SMEM] * 2 + [VMEM] * 3 + [ANY],
+        [SMEM] + [VMEM] * 3 + [ANY],
         [pltpu.VMEM((tokens, columns), F32), pltpu.VMEM((wide, columns), BF16), pltpu.SemaphoreType.DMA],
         flops=PLACE_COST,
-    )(place, plan, heads, up, down, out_weight)
+    )(plan, heads, up, down, out_weight)
     return call(
         finish_kernel,
         shape((slots, steps, columns), BF16),
-        [SMEM] + [VMEM] * 2,
-        [pltpu.VMEM((arrived, columns), F32)],
+        [pl.BlockSpec(memory_space=pl.ANY)] + [VMEM] * 2,
+        [pltpu.SMEM((8, 128), I32), pltpu.VMEM((arrived, columns), F32), pltpu.SemaphoreType.DMA],
         nbytes=2 << 20,
     )(here, placed, blocks)
 

time: 99.2 us -> 97.4 us (0.982)
  Pallas kernels: 27.9 us -> 26.1 us
  transfers between devices with their start and end apart: 12 -> 12, of which waited for: 4 -> 4; matrix products, arithmetic and copies ran while one was open for 0% -> 0% of each run, Pallas kernels for 23% -> 22%
where the time goes in v6:
time: 97.4 us; the launch traced here: 96.9 us
  starting transfers between devices  38.8 us (40%)
  waiting for transfers between devices  30.3 us (31%)
  Pallas kernels  26.1 us (27%)
  local copies, waits for them, and re-layouts  1.56 us (2%)
    all_to_all x4, waiting for transfers between devices, exchange(): return lax.all_to_all(x, axis, split_axis=0, concat_axis=0, tiled=True)  27.4 us
    all_to_all x4, starting transfers between devices, exchange(): return lax.all_to_all(x, axis, split_axis=0, concat_axis=0, tiled=True)  24.4 us
    ppermute x8, starting transfers between devices, hop(): return (lax.ppermute(u, 'tp', ahead), lax.ppermute(d, 'tp', astern))  14.4 us
    pallas_call x1, Pallas kernels, on_device(): call(staying_kernel, [shape((cut, columns), BF16), shape((tokens - cut, c...  7.33 us
    pallas_call x3, Pallas kernels, add(): call(functools.partial(hop_kernel, k), [shape((tokens, columns), BF16)] *...  5.5 us
    pallas_call x1, Pallas kernels, on_device(): call(arrived_kernel, shape((ring, arrived, columns), BF16), [pl.BlockSpec...  3.65 us
    ppermute x8, waiting for transfers between devices, hop(): return (lax.ppermute(u, 'tp', ahead), lax.ppermute(d, 'tp', astern))  2.9 us
    pallas_call x1, Pallas kernels, on_device(): call(place_kernel, shape((slots, steps, columns), BF16), [SMEM] + [VMEM]...  2.72 us
  transfers between devices with their start and end apart: 12, of which 4 were waited for; matrix products, arithmetic and copies ran while one was open for 0% of the time, Pallas kernels for 22%

profile of v6, /device:TPU:1, one launch (start us, length us, event | category | flops | bytes accessed | tf_op | source)
XLA Modules:
  0.0 96.9 jit_solution(15030271877238438891)
XLA Ops:
  0.0 1.5 %shard_map.91 = (s32[32,128]{1,0:T(8,128)}, s32[8,128]{1,0:T(8,128)S(1)}) custom-call(s32[3,26]{1,0:T(4,128)} %bitcast.9, s32[1,128]{1,0:T(1,128)} %bitcast.10, s32[1,128]{1,0:T(1,128)} %bitcast.11), custom_call_target="tpu_custom_call" | custom-call | bytes 65536 | tf_op jit(solution)/shard_map/pallas_call | solution.py:376
  1.5 8.6 %all-to-all-start = ((s32[32,1,128]{2,1,0:T(1,128)}), s32[32,1,128]{2,1,0:T(1,128)S(1)}, u32[]{:S(2)}, u32[]{:S(2)}) async-start(s32[32,1,128]{2,1,0:T(1,128)} %bitcast.4), calls=%async_computation | async-start | bytes 32768 | tf_op jit(solution)/shard_map/all_to_all | solution.py:366
  10.2 7.3 %shard_map.92 = (bf16[160,512]{1,0:T(8,128)(2,1)S(1)}, bf16[144,512]{1,0:T(8,128)(2,1)}, bf16[304,512]{1,0:T(8,128)(2,1)S(1)}, bf16[128,4,768]{2,1,0:T(4,128)(2,...) custom-call(s32[8,128]{1,0:T(8,128)S(1)} %get-tuple-element.35.plan_src.plan_ref, ...), custom_call_target="tpu_custom_call" | custom-call | flops 159383552 | bytes 16777216 | tf_op jit(solution)/shard_map/pallas_call | solution.py:392
  17.5 5.7 %collective-permute-start.1 = (bf16[144,512]{1,0:T(8,128)(2,1)}, bf16[144,512]{1,0:T(8,128)(2,1)}, u32[]{:S(2)}, u32[]{:S(2)}) collective-permute-start(bf16[144,512]{1,0:T(8,128)(2,1)} %get-tuple-element.47), channel_id=1, source_target_pairs={{0,7},{1,0},{2,1},{3,2},{4,3},{5,4},{6,5},{7,6},{8,15},{9,8},{10,9... | collective-permute-start | bytes 442376 | tf_op jit(solution)/shard_map/ppermute | solution.py:423
  23.1 1.7 %shard_map.93 = (bf16[64,4,768]{2,1,0:T(4,128)(2,1)}, s32[8,128]{1,0:T(8,128)S(1)}) custom-call(s32[32,128]{1,0:T(8,128)S(1)} %bitcast.7, s32[32,128]{1,0:T(8,128)S(1)} %bitcast.8, bf16[128,4,768]{2,1,0:T(4,128)(2,1)S(1)} %get-tuple-element.40.fresh_ref), custom_call_target="tpu_custom_call" | custom-call | flops 8000000000 | tf_op jit(solution)/shard_map/pallas_call | solution.py:440
  24.8 7.7 %all-to-all-start.1 = ((bf16[64,4,768]{2,1,0:T(4,128)(2,1)}), bf16[64,4,768]{2,1,0:T(4,128)(2,1)S(1)}, u32[]{:S(2)}, u32[]{:S(2)}) async-start(bf16[64,4,768]{2,1,0:T(4,128)(2,1)} %get-tuple-element.44), calls=%async_computation.1 | async-start | bytes 786432 | tf_op jit(solution)/shard_map/all_to_all | solution.py:366
  32.5 0.6 copy-done
  33.2 0.9 copy-done.1
  34.1 1.8 %shard_map.94 = (bf16[304,512]{1,0:T(8,128)(2,1)S(1)}, bf16[304,512]{1,0:T(8,128)(2,1)S(1)}) custom-call(bf16[304,512]{1,0:T(8,128)(2,1)S(1)} %get-tuple-element.58.heads_ref, bf16[160,512]{1,0:T(8,128)(2,1)S(1)} %copy-done.1, bf16[144,512]{1,0:T(8,128)(2,1)} %collective-permute-done.1.down_ref, bf16[512,4096]{1,0:T(8,128)(2,1)} %weight_ref.11), custom_call_target="tpu_custom_call" | custom-call | flops 20000000000 | tf_op jit(solution)/shard_map/pallas_call | solution.py:426
  36.0 3.0 %collective-permute-start.3 = (bf16[304,512]{1,0:T(8,128)(2,1)S(1)}, bf16[304,512]{1,0:T(8,128)(2,1)}, u32[]{:S(2)}, u32[]{:S(2)}) collective-permute-start(bf16[304,512]{1,0:T(8,128)(2,1)S(1)} %get-tuple-element.49), channel_id=1, source_target_pairs={{0,7},{1,0},{2,1},{3,2},{4,3},{5,4},{6,5},{7,6},{8,15},{9,8},{10,9... | collective-permute-start | bytes 933896 | tf_op jit(solution)/shard_map/ppermute | solution.py:423
  39.0 3.8 %all-to-all-done.1.asked_ref = bf16[64,4,768]{2,1,0:T(4,128)(2,1)S(1)} async-done(((bf16[64,4,768]{2,1,0:T(4,128)(2,1)}), bf16[64,4,768]{2,1,0:T(4,128)(2,1)S(1)}, u32[]{:S(2)}, u32[]{:S(2)}) %all-to-all-start.1) | async-done | bytes 393248 | tf_op jit(solution)/shard_map/all_to_all | solution.py:366
  42.8 2.3 %shard_map.95 = bf16[64,4,512]{2,1,0:T(4,128)(2,1)} custom-call(s32[8,128]{1,0:T(8,128)S(1)} %get-tuple-element.35.plan_src.plan_ref, bf16[64,4,768]{2,1,0:T(4,128)(2,1)S(1)} %all-to-all-done.1.asked_ref, bf16[26,128,128]{2,1,0:T(8,128)(2,1)S(1)} %get-tuple-element.51.keys_ref, bf16[26,128,128]{2,1,0:T(8,128)(2,1)S(1)} %get-tuple-element.52.values_ref), custom_call_target="tpu_custom_call" | custom-call | tf_op jit(solution)/shard_map/pallas_call | solution.py:454
  45.1 3.9 %all-to-all-start.2 = ((bf16[64,4,512]{2,1,0:T(4,128)(2,1)}), bf16[64,4,512]{2,1,0:T(4,128)(2,1)S(1)}, u32[]{:S(2)}, u32[]{:S(2)}) async-start(bf16[64,4,512]{2,1,0:T(4,128)(2,1)} %shard_map.95), calls=%async_computation.2 | async-start | bytes 524288 | tf_op jit(solution)/shard_map/all_to_all | solution.py:366
  49.0 1.9 %shard_map.96 = (bf16[304,512]{1,0:T(8,128)(2,1)S(1)}, bf16[304,512]{1,0:T(8,128)(2,1)S(1)}) custom-call(bf16[304,512]{1,0:T(8,128)(2,1)S(1)} %get-tuple-element.58.heads_ref, bf16[304,512]{1,0:T(8,128)(2,1)S(1)} %collective-permute-done.2.up_ref, bf16[304,512]{1,0:T(8,128)(2,1)} %collective-permute-done.3.down_ref, bf16[512,4096]{1,0:T(8,128)(2,1)} %weight_ref.11), custom_call_target="tpu_custom_call" | custom-call | flops 20000000000 | tf_op jit(solution)/shard_map/pallas_call | solution.py:426
  50.9 2.8 %collective-permute-start.5 = (bf16[304,512]{1,0:T(8,128)(2,1)S(1)}, bf16[304,512]{1,0:T(8,128)(2,1)S(1)}, u32[]{:S(2)}, u32[]{:S(2)}) collective-permute-start(bf16[304,512]{1,0:T(8,128)(2,1)S(1)} %get-tuple-element.56), channel_id=1, source_target_pairs={{0,7},{1,0},{2,1},{3,2},{4,3},{5,4},{6,5},{7,6},{8,15},{9,8},{10,9... | collective-permute-start | bytes 933896 | tf_op jit(solution)/shard_map/ppermute | solution.py:423
  53.8 4.2 %all-to-all-done.2.back_ref = bf16[64,4,512]{2,1,0:T(4,128)(2,1)S(1)} async-done(((bf16[64,4,512]{2,1,0:T(4,128)(2,1)}), bf16[64,4,512]{2,1,0:T(4,128)(2,1)S(1)}, u32[]{:S(2)}, u32[]{:S(2)}) %all-to-all-start.2) | async-done | bytes 262176 | tf_op jit(solution)/shard_map/all_to_all | solution.py:366
  58.0 3.7 %shard_map.97 = bf16[8,104,512]{2,1,0:T(8,128)(2,1)} custom-call(s32[8,128]{1,0:T(8,128)S(1)} %get-tuple-element.41.here_src, bf16[64,4,512]{2,1,0:T(4,128)(2,1)S(1)} %all-to-all-done.2.back_ref, bf16[512,4096]{1,0:T(8,128)(2,1)} %weight_ref.11), custom_call_target="tpu_custom_call" | custom-call | flops 8000000000 | tf_op jit(solution)/shard_map/pallas_call | solution.py:466
  61.6 1.9 %shard_map.98 = (bf16[304,512]{1,0:T(8,128)(2,1)S(1)}, bf16[304,512]{1,0:T(8,128)(2,1)S(1)}) custom-call(bf16[304,512]{1,0:T(8,128)(2,1)S(1)} %get-tuple-element.58.heads_ref, bf16[304,512]{1,0:T(8,128)(2,1)S(1)} %collective-permute-done.4.up_ref, bf16[304,512]{1,0:T(8,128)(2,1)S(1)} %collective-permute-done.5.down_ref, bf16[512,4096]{1,0:T(8,128)(2,1)} %weight_ref.11), custom_call_target="tpu_custom_call" | custom-call | flops 20000000000 | tf_op jit(solution)/shard_map/pallas_call | solution.py:426
  63.6 2.7 %collective-permute-start.7 = (bf16[304,512]{1,0:T(8,128)(2,1)S(1)}, bf16[304,512]{1,0:T(8,128)(2,1)S(1)}, u32[]{:S(2)}, u32[]{:S(2)}) collective-permute-start(bf16[304,512]{1,0:T(8,128)(2,1)S(1)} %get-tuple-element.60), channel_id=1, source_target_pairs={{0,7},{1,0},{2,1},{3,2},{4,3},{5,4},{6,5},{7,6},{8,15},{9,8},{10,9... | collective-permute-start | bytes 933896 | tf_op jit(solution)/shard_map/ppermute | solution.py:423
  66.3 4.2 %all-to-all-start.3 = ((bf16[8,104,512]{2,1,0:T(8,128)(2,1)}), bf16[8,104,512]{2,1,0:T(8,128)(2,1)S(1)}, u32[]{:S(2)}, u32[]{:S(2)}) async-start(bf16[8,104,512]{2,1,0:T(8,128)(2,1)} %shard_map.97), calls=%async_computation.3 | async-start | bytes 1703936 | tf_op jit(solution)/shard_map/all_to_all | solution.py:366
  70.5 2.9 %collective-permute-done.6.up_ref = bf16[304,512]{1,0:T(8,128)(2,1)S(1)} collective-permute-done((bf16[304,512]{1,0:T(8,128)(2,1)S(1)}, bf16[304,512]{1,0:T(8,128)(2,1)S(1)}, u32[]{:S(2)}, u32[]{:S(2)}) %collective-permute-start.6) | collective-permute-done | bytes 311328 | tf_op jit(solution)/shard_map/ppermute | solution.py:423
  73.4 2.7 %shard_map.99.placed_ref = bf16[128,4,512]{2,1,0:T(4,128)(2,1)S(1)} custom-call(s32[8,128]{1,0:T(8,128)S(1)} %get-tuple-element.35.plan_src.plan_ref, bf16[304,512]{1,0:T(8,128)(2,1)S(1)} %get-tuple-element.58.heads_ref, bf16[304,512]{1,0:T(8,128)(2,1)S(1)} %collective-permute-done.6.up_ref, bf16[304,512]{1,0:T(8,128)(2,1)S(1)} %collective-permute-done.7.down_ref, ...), custom_call_target="tpu_custom_call" | custom-call | flops 40000000000 | tf_op jit(solution)/shard_map/pallas_call | solution.py:489
  76.1 19.4 %all-to-all-done.3.blocks_ref = bf16[8,104,512]{2,1,0:T(8,128)(2,1)S(1)} async-done(((bf16[8,104,512]{2,1,0:T(8,128)(2,1)}), bf16[8,104,512]{2,1,0:T(8,128)(2,1)S(1)}, u32[]{:S(2)}, u32[]{:S(2)}) %all-to-all-start.3) | async-done | bytes 852000 | tf_op jit(solution)/shard_map/all_to_all | solution.py:366
  95.5 1.4 %shard_map.100 = bf16[128,4,512]{2,1,0:T(4,128)(2,1)} custom-call(s32[8,128]{1,0:T(8,128)S(1)} %get-tuple-element.41.here_src, bf16[128,4,512]{2,1,0:T(4,128)(2,1)S(1)} %shard_map.99.placed_ref, bf16[8,104,512]{2,1,0:T(8,128)(2,1)S(1)} %all-to-all-done.3.blocks_ref), custom_call_target="tpu_custom_call" | custom-call | bytes 2097152 | tf_op jit(solution)/shard_map/pallas_call | solution.py:496
  (14 shorter events, 0.3 us)
Async XLA Ops:
  1.5 21.6 %all-to-all-start = ((s32[32,1,128]{2,1,0:T(1,128)}), s32[32,1,128]{2,1,0:T(1,128)S(1)}, u32[]{:S(2)}, u32[]{:S(2)}) async-start(s32[32,1,128]{2,1,0:T(1,128)} %bitcast.4), calls=%async_computation | async-start | bytes 32768 | tf_op jit(solution)/shard_map/all_to_all | solution.py:366
  17.5 15.0 %collective-permute-start.1 = (bf16[144,512]{1,0:T(8,128)(2,1)}, bf16[144,512]{1,0:T(8,128)(2,1)}, u32[]{:S(2)}, u32[]{:S(2)}) collective-permute-start(bf16[144,512]{1,0:T(8,128)(2,1)} %get-tuple-element.47), channel_id=1, source_target_pairs={{0,7},{1,0},{2,1},{3,2},{4,3},{5,4},{6,5},{7,6},{8,15},{9,8},{10,9... | collective-permute-start | bytes 442376 | tf_op jit(solution)/shard_map/ppermute | solution.py:423
  23.1 9.4 %collective-permute-start = (bf16[160,512]{1,0:T(8,128)(2,1)S(1)}, bf16[160,512]{1,0:T(8,128)(2,1)S(1)}, u32[]{:S(2)}, u32[]{:S(2)}) collective-permute-start(bf16[160,512]{1,0:T(8,128)(2,1)S(1)} %get-tuple-element.46), channel_id=1, source_target_pairs={{0,1},{1,2},{2,3},{3,4},{4,5},{5,6},{6,7},{7,0},{8,9},{9,10},{10,1... | collective-permute-start | bytes 491528 | tf_op jit(solution)/shard_map/ppermute | solution.py:423
  24.8 18.0 %all-to-all-start.1 = ((bf16[64,4,768]{2,1,0:T(4,128)(2,1)}), bf16[64,4,768]{2,1,0:T(4,128)(2,1)S(1)}, u32[]{:S(2)}, u32[]{:S(2)}) async-start(bf16[64,4,768]{2,1,0:T(4,128)(2,1)} %get-tuple-element.44), calls=%async_computation.1 | async-start | bytes 786432 | tf_op jit(solution)/shard_map/all_to_all | solution.py:366
  32.5 0.7 copy-start
  33.2 0.9 copy-start.1
  35.9 13.1 %collective-permute-start.2 = (bf16[304,512]{1,0:T(8,128)(2,1)S(1)}, bf16[304,512]{1,0:T(8,128)(2,1)S(1)}, u32[]{:S(2)}, u32[]{:S(2)}) collective-permute-start(bf16[304,512]{1,0:T(8,128)(2,1)S(1)} %get-tuple-element.48), channel_id=1, source_target_pairs={{0,1},{1,2},{2,3},{3,4},{4,5},{5,6},{6,7},{7,0},{8,9},{9,10},{10,1... | collective-permute-start | bytes 933896 | tf_op jit(solution)/shard_map/ppermute | solution.py:423
  36.0 13.0 %collective-permute-start.3 = (bf16[304,512]{1,0:T(8,128)(2,1)S(1)}, bf16[304,512]{1,0:T(8,128)(2,1)}, u32[]{:S(2)}, u32[]{:S(2)}) collective-permute-start(bf16[304,512]{1,0:T(8,128)(2,1)S(1)} %get-tuple-element.49), channel_id=1, source_target_pairs={{0,7},{1,0},{2,1},{3,2},{4,3},{5,4},{6,5},{7,6},{8,15},{9,8},{10,9... | collective-permute-start | bytes 933896 | tf_op jit(solution)/shard_map/ppermute | solution.py:423
  45.1 12.9 %all-to-all-start.2 = ((bf16[64,4,512]{2,1,0:T(4,128)(2,1)}), bf16[64,4,512]{2,1,0:T(4,128)(2,1)S(1)}, u32[]{:S(2)}, u32[]{:S(2)}) async-start(bf16[64,4,512]{2,1,0:T(4,128)(2,1)} %shard_map.95), calls=%async_computation.2 | async-start | bytes 524288 | tf_op jit(solution)/shard_map/all_to_all | solution.py:366
  50.8 10.8 %collective-permute-start.4 = (bf16[304,512]{1,0:T(8,128)(2,1)S(1)}, bf16[304,512]{1,0:T(8,128)(2,1)S(1)}, u32[]{:S(2)}, u32[]{:S(2)}) collective-permute-start(bf16[304,512]{1,0:T(8,128)(2,1)S(1)} %get-tuple-element.55), channel_id=1, source_target_pairs={{0,1},{1,2},{2,3},{3,4},{4,5},{5,6},{6,7},{7,0},{8,9},{9,10},{10,1... | collective-permute-start | bytes 933896 | tf_op jit(solution)/shard_map/ppermute | solution.py:423
  50.9 10.7 %collective-permute-start.5 = (bf16[304,512]{1,0:T(8,128)(2,1)S(1)}, bf16[304,512]{1,0:T(8,128)(2,1)S(1)}, u32[]{:S(2)}, u32[]{:S(2)}) collective-permute-start(bf16[304,512]{1,0:T(8,128)(2,1)S(1)} %get-tuple-element.56), channel_id=1, source_target_pairs={{0,7},{1,0},{2,1},{3,2},{4,3},{5,4},{6,5},{7,6},{8,15},{9,8},{10,9... | collective-permute-start | bytes 933896 | tf_op jit(solution)/shard_map/ppermute | solution.py:423
  63.5 9.9 %collective-permute-start.6 = (bf16[304,512]{1,0:T(8,128)(2,1)S(1)}, bf16[304,512]{1,0:T(8,128)(2,1)S(1)}, u32[]{:S(2)}, u32[]{:S(2)}) collective-permute-start(bf16[304,512]{1,0:T(8,128)(2,1)S(1)} %get-tuple-element.59), channel_id=1, source_target_pairs={{0,1},{1,2},{2,3},{3,4},{4,5},{5,6},{6,7},{7,0},{8,9},{9,10},{10,1... | collective-permute-start | bytes 933896 | tf_op jit(solution)/shard_map/ppermute | solution.py:423
  63.6 9.8 %collective-permute-start.7 = (bf16[304,512]{1,0:T(8,128)(2,1)S(1)}, bf16[304,512]{1,0:T(8,128)(2,1)S(1)}, u32[]{:S(2)}, u32[]{:S(2)}) collective-permute-start(bf16[304,512]{1,0:T(8,128)(2,1)S(1)} %get-tuple-element.60), channel_id=1, source_target_pairs={{0,7},{1,0},{2,1},{3,2},{4,3},{5,4},{6,5},{7,6},{8,15},{9,8},{10,9... | collective-permute-start | bytes 933896 | tf_op jit(solution)/shard_map/ppermute | solution.py:423
  66.3 29.2 %all-to-all-start.3 = ((bf16[8,104,512]{2,1,0:T(8,128)(2,1)}), bf16[8,104,512]{2,1,0:T(8,128)(2,1)S(1)}, u32[]{:S(2)}, u32[]{:S(2)}) async-start(bf16[8,104,512]{2,1,0:T(8,128)(2,1)} %shard_map.97), calls=%async_computation.3 | async-start | bytes 1703936 | tf_op jit(solution)/shard_map/all_to_all | solution.py:366

commit v7 on v6

--- a/solution.py
+++ b/solution.py
@@ -224,27 +224,33 @@
     down_ref[...] = block[cut:].astype(BF16)
 
 
-def hop_kernel(k, heads_ref, up_ref, down_ref, weight_ref, up_out, down_out, ubuf, dbuf, wbuf, sem):
-    columns = wbuf.shape[2]
-    ring, tokens = weight_ref.shape[1] // columns, heads_ref.shape[0]
-    copies = []
-    for j, step in enumerate((k, ring - k)):
-        at = pl.multiple_of(lax.rem(lax.axis_index("tp") + step, ring) * columns, columns)
-        copies.append(pltpu.make_async_copy(weight_ref.at[:, pl.ds(at, columns)], wbuf.at[j], sem.at[j]))
-    copies.append(pltpu.make_async_copy(up_ref, ubuf, sem.at[2]))
-    copies.append(pltpu.make_async_copy(down_ref, dbuf, sem.at[3]))
-    for copy in copies:
+def hop_kernel(blocks, held, heads_ref, up_ref, down_ref, weight_ref, *rest):
+    held_refs, rest = rest[:held], rest[held:]
+    outs, kept, (ubuf, dbuf, sem, *scratch) = rest[:2], rest[2 : len(blocks)], rest[len(blocks) :]
+    tokens, columns = heads_ref.shape[0], up_ref.shape[1]
+    ring = weight_ref.shape[1] // columns
+    parts = [*held_refs, *scratch, *kept]
+    loads = {}
+    for j in range(held, len(blocks)):
+        at = pl.multiple_of(lax.rem(lax.axis_index("tp") + blocks[j], ring) * columns, columns)
+        loads[j] = pltpu.make_async_copy(weight_ref.at[:, pl.ds(at, columns)], parts[j], sem.at[2 + j])
+    sums = [pltpu.make_async_copy(up_ref, ubuf, sem.at[0]), pltpu.make_async_copy(down_ref, dbuf, sem.at[1])]
+    for copy in [loads[j] for j in loads if j < 2] + sums + [loads[j] for j in loads if j >= 2]:
         copy.start()
-    for j, (buf, out, first) in enumerate(((ubuf, up_out, 0), (dbuf, down_out, tokens - dbuf.shape[0]))):
-        copies[j].wait()
-        terms = jnp.dot(heads_ref[...], wbuf[j], preferred_element_type=F32)
-        copies[2 + j].wait()
+    for j, (buf, out, first) in enumerate(((ubuf, outs[0], 0), (dbuf, outs[1], tokens - dbuf.shape[0]))):
+        if j in loads:
+            loads[j].wait()
+        terms = jnp.dot(heads_ref[...], parts[j][...], preferred_element_type=F32)
+        sums[j].wait()
         end = first + buf.shape[0]
         out[first:end, :] = (terms[first:end] + buf[...].astype(F32)).astype(BF16)
         if first > 0:
             out[:first, :] = terms[:first].astype(BF16)
         if end < tokens:
             out[end:, :] = terms[end:].astype(BF16)
+    for j in loads:
+        if j >= 2:
+            loads[j].wait()
 
 
 def leaving_kernel(plan_src, asked_ref, keys_ref, values_ref, out_ref, plan_ref, kbuf, vbuf, score, weight, psem):
@@ -422,19 +428,18 @@
     def hop(u, d):
         return lax.ppermute(u, "tp", ahead), lax.ppermute(d, "tp", astern)
 
-    def add(k, u, d):
+    part = ((wide, columns), BF16)
+
+    def add(k, u, d, keep=(), held=()):
+        blocks = (k, ring - k, *keep)
         return call(
-            functools.partial(hop_kernel, k),
-            [shape((tokens, columns), BF16)] * 2,
-            [VMEM] + [pl.BlockSpec(memory_space=pl.ANY)] * 2 + [ANY],
-            [
-                pltpu.VMEM(u.shape, BF16),
-                pltpu.VMEM(d.shape, BF16),
-                pltpu.VMEM((2, wide, columns), BF16),
-                pltpu.SemaphoreType.DMA((4,)),
-            ],
+            functools.partial(hop_kernel, blocks, len(held)),
+            [shape((tokens, columns), BF16)] * 2 + [shape(*part)] * len(keep),
+            [VMEM] + [pl.BlockSpec(memory_space=pl.ANY)] * 2 + [ANY] + [VMEM] * len(held),
+            [pltpu.VMEM(u.shape, BF16), pltpu.VMEM(d.shape, BF16), pltpu.SemaphoreType.DMA((2 + ring,))]
+            + [pltpu.VMEM(*part)] * (2 - len(held)),
             flops=HOP_COST,
-        )(heads, u, d, out_weight)
+        )(heads, u, d, out_weight, *held)
 
     table, fresh, heads, leave_keys = barrier((table, fresh, heads, leave_keys))
     asked, here = call(
@@ -459,7 +464,7 @@
     )(plan, asked, leave_keys, leave_values)
     back, heads = barrier((back, heads))
     back = exchange(back, "group")
-    up, down = add(2, up, down)
+    up, down, *kept = add(2, up, down, keep=(1, ring - 1))
     back = barrier((back, up, down))[0]
     up, down = hop(up, down)
     arrived = moves * steps
@@ -481,7 +486,7 @@
         limit=10,
     )(here, back, out_weight)
     blocks, heads = barrier((blocks, heads))
-    up, down = add(1, up, down)
+    up, down = add(1, up, down, held=kept)
     blocks = barrier((blocks, up, down))[0]
     blocks = exchange(blocks, "tp")
     up, down = hop(up, down)

time: 97.4 us -> 94.3 us (0.968)
  waiting for transfers between devices: 30.3 us -> 28.6 us
    all_to_all x4, waiting for transfers between devices: 27.4 us -> 25 us  [exchange(): return lax.all_to_all(x, axis, split_axis=0, concat_axis=0, tiled=True)]
  transfers between devices with their start and end apart: 12 -> 12, of which waited for: 4 -> 5; matrix products, arithmetic and copies ran while one was open for 0% -> 0% of each run, Pallas kernels for 22% -> 24%
where the time goes in v7:
time: 94.3 us; the launch traced here: 93.9 us
  starting transfers between devices  38.3 us (41%)
  waiting for transfers between devices  28.6 us (30%)
  Pallas kernels  26.1 us (28%)
    all_to_all x4, waiting for transfers between devices, exchange(): return lax.all_to_all(x, axis, split_axis=0, concat_axis=0, tiled=True)  25 us
    all_to_all x4, starting transfers between devices, exchange(): return lax.all_to_all(x, axis, split_axis=0, concat_axis=0, tiled=True)  23.8 us
    ppermute x8, starting transfers between devices, hop(): return (lax.ppermute(u, 'tp', ahead), lax.ppermute(d, 'tp', astern))  14.5 us
    pallas_call x1, Pallas kernels, on_device(): call(staying_kernel, [shape((cut, columns), BF16), shape((tokens - cut, c...  7.33 us
    pallas_call x3, Pallas kernels, add(): call(functools.partial(hop_kernel, blocks, len(held)), [shape((tokens, co...  5.43 us
    pallas_call x1, Pallas kernels, on_device(): call(arrived_kernel, shape((ring, arrived, columns), BF16), [pl.BlockSpec...  3.71 us
    ppermute x8, waiting for transfers between devices, hop(): return (lax.ppermute(u, 'tp', ahead), lax.ppermute(d, 'tp', astern))  3.54 us
    pallas_call x1, Pallas kernels, on_device(): call(place_kernel, shape((slots, steps, columns), BF16), [SMEM] + [VMEM]...  2.72 us
  transfers between devices with their start and end apart: 12, of which 5 were waited for; matrix products, arithmetic and copies ran while one was open for 0% of the time, Pallas kernels for 24%

profile of v7, /device:TPU:1, one launch (start us, length us, event | category | flops | bytes accessed | tf_op | source)
XLA Modules:
  0.0 93.9 jit_solution(5093853010299451686)
XLA Ops:
  0.0 1.5 %shard_map.91 = (s32[32,128]{1,0:T(8,128)}, s32[8,128]{1,0:T(8,128)S(1)}) custom-call(s32[3,26]{1,0:T(4,128)} %bitcast.9, s32[1,128]{1,0:T(1,128)} %bitcast.10, s32[1,128]{1,0:T(1,128)} %bitcast.11), custom_call_target="tpu_custom_call" | custom-call | bytes 65536 | tf_op jit(solution)/shard_map/pallas_call | solution.py:382
  1.5 8.6 %all-to-all-start = ((s32[32,1,128]{2,1,0:T(1,128)}), s32[32,1,128]{2,1,0:T(1,128)S(1)}, u32[]{:S(2)}, u32[]{:S(2)}) async-start(s32[32,1,128]{2,1,0:T(1,128)} %bitcast.4), calls=%async_computation | async-start | bytes 32768 | tf_op jit(solution)/shard_map/all_to_all | solution.py:372
  10.2 7.3 %shard_map.92 = (bf16[160,512]{1,0:T(8,128)(2,1)S(1)}, bf16[144,512]{1,0:T(8,128)(2,1)}, bf16[304,512]{1,0:T(8,128)(2,1)S(1)}, bf16[128,4,768]{2,1,0:T(4,128)(2,...) custom-call(s32[8,128]{1,0:T(8,128)S(1)} %get-tuple-element.37.plan_src.plan_ref, ...), custom_call_target="tpu_custom_call" | custom-call | flops 159383552 | bytes 16777216 | tf_op jit(solution)/shard_map/pallas_call | solution.py:398
  17.5 5.7 %collective-permute-start.1 = (bf16[144,512]{1,0:T(8,128)(2,1)}, bf16[144,512]{1,0:T(8,128)(2,1)}, u32[]{:S(2)}, u32[]{:S(2)}) collective-permute-start(bf16[144,512]{1,0:T(8,128)(2,1)} %get-tuple-element.49), channel_id=1, source_target_pairs={{0,7},{1,0},{2,1},{3,2},{4,3},{5,4},{6,5},{7,6},{8,15},{9,8},{10,9... | collective-permute-start | bytes 442376 | tf_op jit(solution)/shard_map/ppermute | solution.py:429
  23.2 1.7 %shard_map.93 = (bf16[64,4,768]{2,1,0:T(4,128)(2,1)}, s32[8,128]{1,0:T(8,128)S(1)}) custom-call(s32[32,128]{1,0:T(8,128)S(1)} %bitcast.7, s32[32,128]{1,0:T(8,128)S(1)} %bitcast.8, bf16[128,4,768]{2,1,0:T(4,128)(2,1)S(1)} %get-tuple-element.42.fresh_ref), custom_call_target="tpu_custom_call" | custom-call | flops 8000000000 | tf_op jit(solution)/shard_map/pallas_call | solution.py:445
  24.8 7.7 %all-to-all-start.1 = ((bf16[64,4,768]{2,1,0:T(4,128)(2,1)}), bf16[64,4,768]{2,1,0:T(4,128)(2,1)S(1)}, u32[]{:S(2)}, u32[]{:S(2)}) async-start(bf16[64,4,768]{2,1,0:T(4,128)(2,1)} %get-tuple-element.46), calls=%async_computation.1 | async-start | bytes 786432 | tf_op jit(solution)/shard_map/all_to_all | solution.py:372
  32.5 2.5 %shard_map.94 = (bf16[304,512]{1,0:T(8,128)(2,1)}, bf16[304,512]{1,0:T(8,128)(2,1)S(1)}) custom-call(bf16[304,512]{1,0:T(8,128)(2,1)S(1)} %get-tuple-element.60.heads_ref, bf16[160,512]{1,0:T(8,128)(2,1)S(1)} %collective-permute-done.up_ref, bf16[144,512]{1,0:T(8,128)(2,1)} %collective-permute-done.1.down_ref, bf16[512,4096]{1,0:T(8,128)(2,1)} %weight_ref.11), custom_call_target="tpu_custom_call" | custom-call | flops 20000000000 | tf_op jit(solution)/shard_map/pallas_call | solution.py:435
  35.2 3.0 %collective-permute-start.3 = (bf16[304,512]{1,0:T(8,128)(2,1)S(1)}, bf16[304,512]{1,0:T(8,128)(2,1)S(1)}, u32[]{:S(2)}, u32[]{:S(2)}) collective-permute-start(bf16[304,512]{1,0:T(8,128)(2,1)S(1)} %get-tuple-element.51), channel_id=1, source_target_pairs={{0,7},{1,0},{2,1},{3,2},{4,3},{5,4},{6,5},{7,6},{8,15},{9,8},{10,9... | collective-permute-start | bytes 933896 | tf_op jit(solution)/shard_map/ppermute | solution.py:429
  38.2 4.6 %all-to-all-done.1.asked_ref = bf16[64,4,768]{2,1,0:T(4,128)(2,1)S(1)} async-done(((bf16[64,4,768]{2,1,0:T(4,128)(2,1)}), bf16[64,4,768]{2,1,0:T(4,128)(2,1)S(1)}, u32[]{:S(2)}, u32[]{:S(2)}) %all-to-all-start.1) | async-done | bytes 393248 | tf_op jit(solution)/shard_map/all_to_all | solution.py:372
  42.8 2.2 %shard_map.95 = bf16[64,4,512]{2,1,0:T(4,128)(2,1)} custom-call(s32[8,128]{1,0:T(8,128)S(1)} %get-tuple-element.37.plan_src.plan_ref, bf16[64,4,768]{2,1,0:T(4,128)(2,1)S(1)} %all-to-all-done.1.asked_ref, bf16[26,128,128]{2,1,0:T(8,128)(2,1)S(1)} %get-tuple-element.53.keys_ref, bf16[26,128,128]{2,1,0:T(8,128)(2,1)S(1)} %get-tuple-element.54.values_ref), custom_call_target="tpu_custom_call" | custom-call | tf_op jit(solution)/shard_map/pallas_call | solution.py:459
  45.1 3.7 %all-to-all-start.2 = ((bf16[64,4,512]{2,1,0:T(4,128)(2,1)}), bf16[64,4,512]{2,1,0:T(4,128)(2,1)S(1)}, u32[]{:S(2)}, u32[]{:S(2)}) async-start(bf16[64,4,512]{2,1,0:T(4,128)(2,1)} %shard_map.95), calls=%async_computation.2 | async-start | bytes 524288 | tf_op jit(solution)/shard_map/all_to_all | solution.py:372
  48.8 1.9 %shard_map.96 = (bf16[304,512]{1,0:T(8,128)(2,1)S(1)}, bf16[304,512]{1,0:T(8,128)(2,1)S(1)}, bf16[512,512]{1,0:T(8,128)(2,1)S(1)}, bf16[512,512]{1,0:T(8,128)(2,1)S(1)}) custom-call(bf16[304,512]{1,0:T(8,128)(2,1)S(1)} %get-tuple-element.60.heads_ref, bf16[304,512]{1,0:T(8,128)(2,1)S(1)} %collective-permute-done.2.up_ref, ...), custom_call_target="tpu_custom_call" | custom-call | flops 20000000000 | tf_op jit(solution)/shard_map/pallas_call | solution.py:435
  50.7 0.8 copy-done
  51.5 3.0 %collective-permute-start.5 = (bf16[304,512]{1,0:T(8,128)(2,1)S(1)}, bf16[304,512]{1,0:T(8,128)(2,1)S(1)}, u32[]{:S(2)}, u32[]{:S(2)}) collective-permute-start(bf16[304,512]{1,0:T(8,128)(2,1)S(1)} %get-tuple-element.58), channel_id=1, source_target_pairs={{0,7},{1,0},{2,1},{3,2},{4,3},{5,4},{6,5},{7,6},{8,15},{9,8},{10,9... | collective-permute-start | bytes 933896 | tf_op jit(solution)/shard_map/ppermute | solution.py:429
  54.4 3.2 %all-to-all-done.2.back_ref = bf16[64,4,512]{2,1,0:T(4,128)(2,1)S(1)} async-done(((bf16[64,4,512]{2,1,0:T(4,128)(2,1)}), bf16[64,4,512]{2,1,0:T(4,128)(2,1)S(1)}, u32[]{:S(2)}, u32[]{:S(2)}) %all-to-all-start.2) | async-done | bytes 262176 | tf_op jit(solution)/shard_map/all_to_all | solution.py:372
  57.6 3.7 %shard_map.97 = bf16[8,104,512]{2,1,0:T(8,128)(2,1)} custom-call(s32[8,128]{1,0:T(8,128)S(1)} %get-tuple-element.43.here_src, bf16[64,4,512]{2,1,0:T(4,128)(2,1)S(1)} %all-to-all-done.2.back_ref, bf16[512,4096]{1,0:T(8,128)(2,1)} %weight_ref.11), custom_call_target="tpu_custom_call" | custom-call | flops 8000000000 | tf_op jit(solution)/shard_map/pallas_call | solution.py:471
  61.3 0.7 collective-permute-done.4.up_ref
  62.0 1.0 %shard_map.98 = (bf16[304,512]{1,0:T(8,128)(2,1)S(1)}, bf16[304,512]{1,0:T(8,128)(2,1)S(1)}) custom-call(bf16[304,512]{1,0:T(8,128)(2,1)S(1)} %get-tuple-element.60.heads_ref, bf16[304,512]{1,0:T(8,128)(2,1)S(1)} %collective-permute-done.4.up_ref, bf16[304,512]{1,0:T(8,128)(2,1)S(1)} %collective-permute-done.5.down_ref, bf16[512,4096]{1,0:T(8,128)(2,1)} %weight_ref.11, ...), custom_call_target="tpu_custom_call" | custom-call | flops 20000000000 | tf_op jit(solution)/shard_map/pallas_call | solution.py:435
  63.1 2.7 %collective-permute-start.7 = (bf16[304,512]{1,0:T(8,128)(2,1)S(1)}, bf16[304,512]{1,0:T(8,128)(2,1)S(1)}, u32[]{:S(2)}, u32[]{:S(2)}) collective-permute-start(bf16[304,512]{1,0:T(8,128)(2,1)S(1)} %get-tuple-element.64), channel_id=1, source_target_pairs={{0,7},{1,0},{2,1},{3,2},{4,3},{5,4},{6,5},{7,6},{8,15},{9,8},{10,9... | collective-permute-start | bytes 933896 | tf_op jit(solution)/shard_map/ppermute | solution.py:429
  65.8 3.9 %all-to-all-start.3 = ((bf16[8,104,512]{2,1,0:T(8,128)(2,1)}), bf16[8,104,512]{2,1,0:T(8,128)(2,1)S(1)}, u32[]{:S(2)}, u32[]{:S(2)}) async-start(bf16[8,104,512]{2,1,0:T(8,128)(2,1)} %shard_map.97), calls=%async_computation.3 | async-start | bytes 1703936 | tf_op jit(solution)/shard_map/all_to_all | solution.py:372
  69.6 2.8 %collective-permute-done.6.up_ref = bf16[304,512]{1,0:T(8,128)(2,1)S(1)} collective-permute-done((bf16[304,512]{1,0:T(8,128)(2,1)S(1)}, bf16[304,512]{1,0:T(8,128)(2,1)S(1)}, u32[]{:S(2)}, u32[]{:S(2)}) %collective-permute-start.6) | collective-permute-done | bytes 311328 | tf_op jit(solution)/shard_map/ppermute | solution.py:429
  72.5 2.7 %shard_map.99.placed_ref = bf16[128,4,512]{2,1,0:T(4,128)(2,1)S(1)} custom-call(s32[8,128]{1,0:T(8,128)S(1)} %get-tuple-element.37.plan_src.plan_ref, bf16[304,512]{1,0:T(8,128)(2,1)S(1)} %get-tuple-element.60.heads_ref, bf16[304,512]{1,0:T(8,128)(2,1)S(1)} %collective-permute-done.6.up_ref, bf16[304,512]{1,0:T(8,128)(2,1)S(1)} %collective-permute-done.7.down_ref, ...), custom_call_target="tpu_custom_call" | custom-call | flops 40000000000 | tf_op jit(solution)/shard_map/pallas_call | solution.py:494
  75.2 17.2 %all-to-all-done.3.blocks_ref = bf16[8,104,512]{2,1,0:T(8,128)(2,1)S(1)} async-done(((bf16[8,104,512]{2,1,0:T(8,128)(2,1)}), bf16[8,104,512]{2,1,0:T(8,128)(2,1)S(1)}, u32[]{:S(2)}, u32[]{:S(2)}) %all-to-all-start.3) | async-done | bytes 852000 | tf_op jit(solution)/shard_map/all_to_all | solution.py:372
  92.4 1.4 %shard_map.100 = bf16[128,4,512]{2,1,0:T(4,128)(2,1)} custom-call(s32[8,128]{1,0:T(8,128)S(1)} %get-tuple-element.43.here_src, bf16[128,4,512]{2,1,0:T(4,128)(2,1)S(1)} %shard_map.99.placed_ref, bf16[8,104,512]{2,1,0:T(8,128)(2,1)S(1)} %all-to-all-done.3.blocks_ref), custom_call_target="tpu_custom_call" | custom-call | bytes 2097152 | tf_op jit(solution)/shard_map/pallas_call | solution.py:501
  (14 shorter events, 0.2 us)
Async XLA Ops:
  1.5 21.6 %all-to-all-start = ((s32[32,1,128]{2,1,0:T(1,128)}), s32[32,1,128]{2,1,0:T(1,128)S(1)}, u32[]{:S(2)}, u32[]{:S(2)}) async-start(s32[32,1,128]{2,1,0:T(1,128)} %bitcast.4), calls=%async_computation | async-start | bytes 32768 | tf_op jit(solution)/shard_map/all_to_all | solution.py:372
  17.5 15.0 %collective-permute-start.1 = (bf16[144,512]{1,0:T(8,128)(2,1)}, bf16[144,512]{1,0:T(8,128)(2,1)}, u32[]{:S(2)}, u32[]{:S(2)}) collective-permute-start(bf16[144,512]{1,0:T(8,128)(2,1)} %get-tuple-element.49), channel_id=1, source_target_pairs={{0,7},{1,0},{2,1},{3,2},{4,3},{5,4},{6,5},{7,6},{8,15},{9,8},{10,9... | collective-permute-start | bytes 442376 | tf_op jit(solution)/shard_map/ppermute | solution.py:429
  23.1 9.4 %collective-permute-start = (bf16[160,512]{1,0:T(8,128)(2,1)S(1)}, bf16[160,512]{1,0:T(8,128)(2,1)S(1)}, u32[]{:S(2)}, u32[]{:S(2)}) collective-permute-start(bf16[160,512]{1,0:T(8,128)(2,1)S(1)} %get-tuple-element.48), channel_id=1, source_target_pairs={{0,1},{1,2},{2,3},{3,4},{4,5},{5,6},{6,7},{7,0},{8,9},{9,10},{10,1... | collective-permute-start | bytes 491528 | tf_op jit(solution)/shard_map/ppermute | solution.py:429
  24.8 18.0 %all-to-all-start.1 = ((bf16[64,4,768]{2,1,0:T(4,128)(2,1)}), bf16[64,4,768]{2,1,0:T(4,128)(2,1)S(1)}, u32[]{:S(2)}, u32[]{:S(2)}) async-start(bf16[64,4,768]{2,1,0:T(4,128)(2,1)} %get-tuple-element.46), calls=%async_computation.1 | async-start | bytes 786432 | tf_op jit(solution)/shard_map/all_to_all | solution.py:372
  35.1 13.7 %collective-permute-start.2 = (bf16[304,512]{1,0:T(8,128)(2,1)}, bf16[304,512]{1,0:T(8,128)(2,1)S(1)}, u32[]{:S(2)}, u32[]{:S(2)}) collective-permute-start(bf16[304,512]{1,0:T(8,128)(2,1)} %get-tuple-element.50), channel_id=1, source_target_pairs={{0,1},{1,2},{2,3},{3,4},{4,5},{5,6},{6,7},{7,0},{8,9},{9,10},{10,1... | collective-permute-start | bytes 933896 | tf_op jit(solution)/shard_map/ppermute | solution.py:429
  35.2 13.6 %collective-permute-start.3 = (bf16[304,512]{1,0:T(8,128)(2,1)S(1)}, bf16[304,512]{1,0:T(8,128)(2,1)S(1)}, u32[]{:S(2)}, u32[]{:S(2)}) collective-permute-start(bf16[304,512]{1,0:T(8,128)(2,1)S(1)} %get-tuple-element.51), channel_id=1, source_target_pairs={{0,7},{1,0},{2,1},{3,2},{4,3},{5,4},{6,5},{7,6},{8,15},{9,8},{10,9... | collective-permute-start | bytes 933896 | tf_op jit(solution)/shard_map/ppermute | solution.py:429
  45.1 12.5 %all-to-all-start.2 = ((bf16[64,4,512]{2,1,0:T(4,128)(2,1)}), bf16[64,4,512]{2,1,0:T(4,128)(2,1)S(1)}, u32[]{:S(2)}, u32[]{:S(2)}) async-start(bf16[64,4,512]{2,1,0:T(4,128)(2,1)} %shard_map.95), calls=%async_computation.2 | async-start | bytes 524288 | tf_op jit(solution)/shard_map/all_to_all | solution.py:372
  50.7 0.8 copy-start
  51.5 10.5 %collective-permute-start.4 = (bf16[304,512]{1,0:T(8,128)(2,1)S(1)}, bf16[304,512]{1,0:T(8,128)(2,1)S(1)}, u32[]{:S(2)}, u32[]{:S(2)}) collective-permute-start(bf16[304,512]{1,0:T(8,128)(2,1)S(1)} %get-tuple-element.57), channel_id=1, source_target_pairs={{0,1},{1,2},{2,3},{3,4},{4,5},{5,6},{6,7},{7,0},{8,9},{9,10},{10,1... | collective-permute-start | bytes 933896 | tf_op jit(solution)/shard_map/ppermute | solution.py:429
  51.5 10.5 %collective-permute-start.5 = (bf16[304,512]{1,0:T(8,128)(2,1)S(1)}, bf16[304,512]{1,0:T(8,128)(2,1)S(1)}, u32[]{:S(2)}, u32[]{:S(2)}) collective-permute-start(bf16[304,512]{1,0:T(8,128)(2,1)S(1)} %get-tuple-element.58), channel_id=1, source_target_pairs={{0,7},{1,0},{2,1},{3,2},{4,3},{5,4},{6,5},{7,6},{8,15},{9,8},{10,9... | collective-permute-start | bytes 933896 | tf_op jit(solution)/shard_map/ppermute | solution.py:429
  57.6 4.4 %copy-start.1 = (bf16[512,512]{1,0:T(8,128)(2,1)S(1)}, bf16[512,512]{1,0:T(8,128)(2,1)}, u32[]{:S(2)}) copy-start(bf16[512,512]{1,0:T(8,128)(2,1)} %copy-done) | copy-start | bytes 1572868
  63.0 9.5 %collective-permute-start.6 = (bf16[304,512]{1,0:T(8,128)(2,1)S(1)}, bf16[304,512]{1,0:T(8,128)(2,1)S(1)}, u32[]{:S(2)}, u32[]{:S(2)}) collective-permute-start(bf16[304,512]{1,0:T(8,128)(2,1)S(1)} %get-tuple-element.63), channel_id=1, source_target_pairs={{0,1},{1,2},{2,3},{3,4},{4,5},{5,6},{6,7},{7,0},{8,9},{9,10},{10,1... | collective-permute-start | bytes 933896 | tf_op jit(solution)/shard_map/ppermute | solution.py:429
  63.1 9.4 %collective-permute-start.7 = (bf16[304,512]{1,0:T(8,128)(2,1)S(1)}, bf16[304,512]{1,0:T(8,128)(2,1)S(1)}, u32[]{:S(2)}, u32[]{:S(2)}) collective-permute-start(bf16[304,512]{1,0:T(8,128)(2,1)S(1)} %get-tuple-element.64), channel_id=1, source_target_pairs={{0,7},{1,0},{2,1},{3,2},{4,3},{5,4},{6,5},{7,6},{8,15},{9,8},{10,9... | collective-permute-start | bytes 933896 | tf_op jit(solution)/shard_map/ppermute | solution.py:429
  65.8 26.7 %all-to-all-start.3 = ((bf16[8,104,512]{2,1,0:T(8,128)(2,1)}), bf16[8,104,512]{2,1,0:T(8,128)(2,1)S(1)}, u32[]{:S(2)}, u32[]{:S(2)}) async-start(bf16[8,104,512]{2,1,0:T(8,128)(2,1)} %shard_map.97), calls=%async_computation.3 | async-start | bytes 1703936 | tf_op jit(solution)/shard_map/all_to_all | solution.py:372

commit v8 on v7

--- a/solution.py
+++ b/solution.py
@@ -165,7 +165,7 @@
 
 def staying_kernel(
     plan_src, query_ref, key_ref, value_ref, keys_ref, values_ref, weight_ref,
-    up_ref, down_ref, heads_ref, fresh_ref, leave_keys_ref, leave_values_ref,
+    up_ref, heads_ref, fresh_ref, leave_keys_ref, leave_values_ref,
     plan_ref, kbuf, vbuf, score, weight, wbuf, psem, fsem, ksem, vsem, wsem,
 ):
     steps, wide = query_ref.shape[1:]
@@ -218,36 +218,32 @@
         leave_keys_ref[i] = kbuf[plan_ref[LEAVE_SLOT, i], 0:cache, :]
         leave_values_ref[i] = vbuf[plan_ref[LEAVE_SLOT, i], 0:cache, :]
     far.wait()
-    cut = up_ref.shape[0]
-    block = jnp.dot(heads_ref[...], wbuf[...], preferred_element_type=F32)
-    up_ref[...] = block[:cut].astype(BF16)
-    down_ref[...] = block[cut:].astype(BF16)
-
-
-def hop_kernel(blocks, held, heads_ref, up_ref, down_ref, weight_ref, *rest):
+    up_ref[...] = jnp.dot(heads_ref[...], wbuf[...], preferred_element_type=F32).astype(BF16)
+
+
+def hop_kernel(blocks, came, held, heads_ref, *rest):
+    sums, weight_ref, rest = rest[:came], rest[came], rest[came + 1 :]
     held_refs, rest = rest[:held], rest[held:]
-    outs, kept, (ubuf, dbuf, sem, *scratch) = rest[:2], rest[2 : len(blocks)], rest[len(blocks) :]
-    tokens, columns = heads_ref.shape[0], up_ref.shape[1]
+    outs, kept, rest = rest[:2], rest[2 : len(blocks)], rest[len(blocks) :]
+    bufs, sem, scratch = rest[:came], rest[came], rest[came + 1 :]
+    columns = outs[0].shape[1]
     ring = weight_ref.shape[1] // columns
     parts = [*held_refs, *scratch, *kept]
     loads = {}
     for j in range(held, len(blocks)):
         at = pl.multiple_of(lax.rem(lax.axis_index("tp") + blocks[j], ring) * columns, columns)
         loads[j] = pltpu.make_async_copy(weight_ref.at[:, pl.ds(at, columns)], parts[j], sem.at[2 + j])
-    sums = [pltpu.make_async_copy(up_ref, ubuf, sem.at[0]), pltpu.make_async_copy(down_ref, dbuf, sem.at[1])]
+    sums = [pltpu.make_async_copy(src, dst, sem.at[i]) for i, (src, dst) in enumerate(zip(sums, bufs))]
     for copy in [loads[j] for j in loads if j < 2] + sums + [loads[j] for j in loads if j >= 2]:
         copy.start()
-    for j, (buf, out, first) in enumerate(((ubuf, outs[0], 0), (dbuf, outs[1], tokens - dbuf.shape[0]))):
+    for j, out in enumerate(outs):
         if j in loads:
             loads[j].wait()
         terms = jnp.dot(heads_ref[...], parts[j][...], preferred_element_type=F32)
-        sums[j].wait()
-        end = first + buf.shape[0]
-        out[first:end, :] = (terms[first:end] + buf[...].astype(F32)).astype(BF16)
-        if first > 0:
-            out[:first, :] = terms[:first].astype(BF16)
-        if end < tokens:
-            out[end:, :] = terms[end:].astype(BF16)
+        if j < came:
+            sums[j].wait()
+            terms = terms + bufs[j][...].astype(F32)
+        out[...] = terms.astype(BF16)
     for j in loads:
         if j >= 2:
             loads[j].wait()
@@ -394,12 +390,10 @@
     table = exchange(table.reshape(groups, 1, 128), "group").reshape(groups, 128)
 
     tokens = staying * steps
-    cut = -(-tokens // 32) * 16
-    up, down, heads, fresh, leave_keys, leave_values = call(
+    up, heads, fresh, leave_keys, leave_values = call(
         staying_kernel,
         [
-            shape((cut, columns), BF16),
-            shape((tokens - cut, columns), BF16),
+            shape((tokens, columns), BF16),
             shape((tokens, wide), BF16),
             shape((slots, steps, wide + 2 * head), BF16),
             shape((moves, cache, head), BF16),
@@ -430,16 +424,17 @@
 
     part = ((wide, columns), BF16)
 
-    def add(k, u, d, keep=(), held=()):
+    def add(k, *sums, keep=(), held=()):
         blocks = (k, ring - k, *keep)
         return call(
-            functools.partial(hop_kernel, blocks, len(held)),
+            functools.partial(hop_kernel, blocks, len(sums), len(held)),
             [shape((tokens, columns), BF16)] * 2 + [shape(*part)] * len(keep),
-            [VMEM] + [pl.BlockSpec(memory_space=pl.ANY)] * 2 + [ANY] + [VMEM] * len(held),
-            [pltpu.VMEM(u.shape, BF16), pltpu.VMEM(d.shape, BF16), pltpu.SemaphoreType.DMA((2 + ring,))]
+            [VMEM] + [pl.BlockSpec(memory_space=pl.ANY)] * len(sums) + [ANY] + [VMEM] * len(held),
+            [pltpu.VMEM(x.shape, BF16) for x in sums]
+            + [pltpu.SemaphoreType.DMA((2 + ring,))]
             + [pltpu.VMEM(*part)] * (2 - len(held)),
             flops=HOP_COST,
-        )(heads, u, d, out_weight, *held)
+        )(heads, *sums, out_weight, *held)
 
     table, fresh, heads, leave_keys = barrier((table, fresh, heads, leave_keys))
     asked, here = call(
@@ -451,9 +446,9 @@
     )(table, table, fresh)
     asked, heads = barrier((asked, heads))
     asked = exchange(asked, "group")
-    up, down = hop(up, down)
-
-    up, down = add(3, up, down)
+    up = lax.ppermute(up, "tp", ahead)
+
+    up, down = add(3, up)
     asked = barrier((asked, up, down))[0]
     up, down = hop(up, down)
     back = call(

time: 94.3 us -> 92.7 us (0.983)
  starting transfers between devices: 38.3 us -> 37.1 us
    ppermute x8 -> x6, starting transfers between devices: 14.5 us -> 8.18 us  [hop(): return (lax.ppermute(u, 'tp', ahead), lax.ppermute(d, 'tp', astern))]
    all_to_all x4, starting transfers between devices: 23.8 us -> 27.3 us  [exchange(): return lax.all_to_all(x, axis, split_axis=0, concat_axis=0, tiled=True)]
    ppermute x8 -> x6, waiting for transfers between devices: 3.54 us -> 1.12 us  [hop(): return (lax.ppermute(u, 'tp', ahead), lax.ppermute(d, 'tp', astern))]
    ppermute x0 -> x1, waiting for transfers between devices: none -> 2.29 us  [on_device(): up = lax.ppermute(up, 'tp', ahead)]
    ppermute x0 -> x1, starting transfers between devices: none -> 1.71 us  [on_device(): up = lax.ppermute(up, 'tp', ahead)]
  transfers between devices with their start and end apart: 12 -> 11, of which waited for: 5 -> 6; matrix products, arithmetic and copies ran while one was open for 0% -> 0% of each run, Pallas kernels for 24% -> 23%
where the time goes in v8:
time: 92.7 us; the launch traced here: 92.2 us
  starting transfers between devices  37.1 us (40%)
  waiting for transfers between devices  28.8 us (31%)
  Pallas kernels  25.3 us (27%)
    all_to_all x4, starting transfers between devices, exchange(): return lax.all_to_all(x, axis, split_axis=0, concat_axis=0, tiled=True)  27.3 us
    all_to_all x4, waiting for transfers between devices, exchange(): return lax.all_to_all(x, axis, split_axis=0, concat_axis=0, tiled=True)  25.4 us
    ppermute x6, starting transfers between devices, hop(): return (lax.ppermute(u, 'tp', ahead), lax.ppermute(d, 'tp', astern))  8.18 us
    pallas_call x1, Pallas kernels, on_device(): call(staying_kernel, [shape((tokens, columns), BF16), shape((tokens, wide...  6.68 us
    pallas_call x3, Pallas kernels, add(): call(functools.partial(hop_kernel, blocks, len(sums), len(held)), [shape(...  5.33 us
    pallas_call x1, Pallas kernels, on_device(): call(arrived_kernel, shape((ring, arrived, columns), BF16), [pl.BlockSpec...  3.71 us
    pallas_call x1, Pallas kernels, on_device(): call(place_kernel, shape((slots, steps, columns), BF16), [SMEM] + [VMEM]...  2.72 us
    ppermute x1, waiting for transfers between devices, on_device(): up = lax.ppermute(up, 'tp', ahead)  2.29 us
  transfers between devices with their start and end apart: 11, of which 6 were waited for; matrix products, arithmetic and copies ran while one was open for 0% of the time, Pallas kernels for 23%

profile of v8, /device:TPU:1, one launch (start us, length us, event | category | flops | bytes accessed | tf_op | source)
XLA Modules:
  0.0 92.2 jit_solution(17124572168087522579)
XLA Ops:
  0.0 1.5 %shard_map.91 = (s32[32,128]{1,0:T(8,128)}, s32[8,128]{1,0:T(8,128)S(1)}) custom-call(s32[3,26]{1,0:T(4,128)} %bitcast.9, s32[1,128]{1,0:T(1,128)} %bitcast.10, s32[1,128]{1,0:T(1,128)} %bitcast.11), custom_call_target="tpu_custom_call" | custom-call | bytes 65536 | tf_op jit(solution)/shard_map/pallas_call | solution.py:378
  1.5 8.6 %all-to-all-start = ((s32[32,1,128]{2,1,0:T(1,128)}), s32[32,1,128]{2,1,0:T(1,128)S(1)}, u32[]{:S(2)}, u32[]{:S(2)}) async-start(s32[32,1,128]{2,1,0:T(1,128)} %bitcast.4), calls=%async_computation | async-start | bytes 32768 | tf_op jit(solution)/shard_map/all_to_all | solution.py:368
  10.2 6.7 %shard_map.92 = (bf16[304,512]{1,0:T(8,128)(2,1)S(1)}, bf16[304,512]{1,0:T(8,128)(2,1)S(1)}, bf16[128,4,768]{2,1,0:T(4,128)(2,1)S(1)}, bf16[26,128,128]{2,1,0:T(8,128)(2,1)S(1)}, bf16[26,128,128]{2,1,0:T(8,128)(2,1)S(1)}) custom-call(s32[8,128]{1,0:T(8,128)S(1)} %get-tuple-element.36.plan_src.plan_ref, bf16[128,4,512]{2,1,0:T(4,128)(2,1)} %query_ref.1, ...), custom_call_target="tpu_custom_call" | custom-call | flops 159383552 | bytes 16777216 | tf_op jit(solution)/shard_map/pallas_call | solution.py:393
  16.8 1.7 %collective-permute-start = (bf16[304,512]{1,0:T(8,128)(2,1)S(1)}, bf16[304,512]{1,0:T(8,128)(2,1)}, u32[]{:S(2)}, u32[]{:S(2)}) collective-permute-start(bf16[304,512]{1,0:T(8,128)(2,1)S(1)} %get-tuple-element.47), channel_id=1, source_target_pairs={{0,1},{1,2},{2,3},{3,4},{4,5},{5,6},{6,7},{7,0},{8,9},{9,10},{10,1... | collective-permute-start | bytes 933896 | tf_op jit(solution)/shard_map/ppermute | solution.py:449
  18.6 1.7 %shard_map.93 = (bf16[64,4,768]{2,1,0:T(4,128)(2,1)}, s32[8,128]{1,0:T(8,128)S(1)}) custom-call(s32[32,128]{1,0:T(8,128)S(1)} %bitcast.7, s32[32,128]{1,0:T(8,128)S(1)} %bitcast.8, bf16[128,4,768]{2,1,0:T(4,128)(2,1)S(1)} %get-tuple-element.41.fresh_ref), custom_call_target="tpu_custom_call" | custom-call | flops 8000000000 | tf_op jit(solution)/shard_map/pallas_call | solution.py:440
  20.2 7.7 %all-to-all-start.1 = ((bf16[64,4,768]{2,1,0:T(4,128)(2,1)}), bf16[64,4,768]{2,1,0:T(4,128)(2,1)S(1)}, u32[]{:S(2)}, u32[]{:S(2)}) async-start(bf16[64,4,768]{2,1,0:T(4,128)(2,1)} %get-tuple-element.45), calls=%async_computation.1 | async-start | bytes 786432 | tf_op jit(solution)/shard_map/all_to_all | solution.py:368
  27.9 2.3 %collective-permute-done.rest_0_ = bf16[304,512]{1,0:T(8,128)(2,1)} collective-permute-done((bf16[304,512]{1,0:T(8,128)(2,1)S(1)}, bf16[304,512]{1,0:T(8,128)(2,1)}, u32[]{:S(2)}, u32[]{:S(2)}) %collective-permute-start) | collective-permute-done | bytes 311328 | tf_op jit(solution)/shard_map/ppermute | solution.py:449
  30.2 2.4 %shard_map.94 = (bf16[304,512]{1,0:T(8,128)(2,1)}, bf16[304,512]{1,0:T(8,128)(2,1)S(1)}) custom-call(bf16[304,512]{1,0:T(8,128)(2,1)S(1)} %get-tuple-element.58.heads_ref, bf16[304,512]{1,0:T(8,128)(2,1)} %collective-permute-done.rest_0_, bf16[512,4096]{1,0:T(8,128)(2,1)} %weight_ref.5), custom_call_target="tpu_custom_call" | custom-call | flops 20000000000 | tf_op jit(solution)/shard_map/pallas_call | solution.py:429
  32.7 2.7 %collective-permute-start.2 = (bf16[304,512]{1,0:T(8,128)(2,1)S(1)}, bf16[304,512]{1,0:T(8,128)(2,1)S(1)}, u32[]{:S(2)}, u32[]{:S(2)}) collective-permute-start(bf16[304,512]{1,0:T(8,128)(2,1)S(1)} %get-tuple-element.49), channel_id=1, source_target_pairs={{0,7},{1,0},{2,1},{3,2},{4,3},{5,4},{6,5},{7,6},{8,15},{9,8},{10,9... | collective-permute-start | bytes 933896 | tf_op jit(solution)/shard_map/ppermute | solution.py:423
  35.4 2.8 %all-to-all-done.1.asked_ref = bf16[64,4,768]{2,1,0:T(4,128)(2,1)S(1)} async-done(((bf16[64,4,768]{2,1,0:T(4,128)(2,1)}), bf16[64,4,768]{2,1,0:T(4,128)(2,1)S(1)}, u32[]{:S(2)}, u32[]{:S(2)}) %all-to-all-start.1) | async-done | bytes 393248 | tf_op jit(solution)/shard_map/all_to_all | solution.py:368
  38.2 2.2 %shard_map.95 = bf16[64,4,512]{2,1,0:T(4,128)(2,1)} custom-call(s32[8,128]{1,0:T(8,128)S(1)} %get-tuple-element.36.plan_src.plan_ref, bf16[64,4,768]{2,1,0:T(4,128)(2,1)S(1)} %all-to-all-done.1.asked_ref, bf16[26,128,128]{2,1,0:T(8,128)(2,1)S(1)} %get-tuple-element.51.keys_ref, bf16[26,128,128]{2,1,0:T(8,128)(2,1)S(1)} %get-tuple-element.52.values_ref), custom_call_target="tpu_custom_call" | custom-call | tf_op jit(solution)/shard_map/pallas_call | solution.py:454
  40.5 5.5 %all-to-all-start.2 = ((bf16[64,4,512]{2,1,0:T(4,128)(2,1)}), bf16[64,4,512]{2,1,0:T(4,128)(2,1)S(1)}, u32[]{:S(2)}, u32[]{:S(2)}) async-start(bf16[64,4,512]{2,1,0:T(4,128)(2,1)} %shard_map.95), calls=%async_computation.2 | async-start | bytes 524288 | tf_op jit(solution)/shard_map/all_to_all | solution.py:368
  46.0 1.9 %shard_map.96 = (bf16[304,512]{1,0:T(8,128)(2,1)S(1)}, bf16[304,512]{1,0:T(8,128)(2,1)S(1)}, bf16[512,512]{1,0:T(8,128)(2,1)S(1)}, bf16[512,512]{1,0:T(8,128)(2,1)S(1)}) custom-call(bf16[304,512]{1,0:T(8,128)(2,1)S(1)} %get-tuple-element.58.heads_ref, bf16[304,512]{1,0:T(8,128)(2,1)S(1)} %collective-permute-done.1.rest_0_, ...), custom_call_target="tpu_custom_call" | custom-call | flops 20000000000 | tf_op jit(solution)/shard_map/pallas_call | solution.py:429
  48.7 2.7 %collective-permute-start.4 = (bf16[304,512]{1,0:T(8,128)(2,1)S(1)}, bf16[304,512]{1,0:T(8,128)(2,1)S(1)}, u32[]{:S(2)}, u32[]{:S(2)}) collective-permute-start(bf16[304,512]{1,0:T(8,128)(2,1)S(1)} %get-tuple-element.56), channel_id=1, source_target_pairs={{0,7},{1,0},{2,1},{3,2},{4,3},{5,4},{6,5},{7,6},{8,15},{9,8},{10,9... | collective-permute-start | bytes 933896 | tf_op jit(solution)/shard_map/ppermute | solution.py:423
  51.4 3.6 %all-to-all-done.2.back_ref = bf16[64,4,512]{2,1,0:T(4,128)(2,1)S(1)} async-done(((bf16[64,4,512]{2,1,0:T(4,128)(2,1)}), bf16[64,4,512]{2,1,0:T(4,128)(2,1)S(1)}, u32[]{:S(2)}, u32[]{:S(2)}) %all-to-all-start.2) | async-done | bytes 262176 | tf_op jit(solution)/shard_map/all_to_all | solution.py:368
  55.0 3.7 %shard_map.97 = bf16[8,104,512]{2,1,0:T(8,128)(2,1)} custom-call(s32[8,128]{1,0:T(8,128)S(1)} %get-tuple-element.42.here_src, bf16[64,4,512]{2,1,0:T(4,128)(2,1)S(1)} %all-to-all-done.2.back_ref, bf16[512,4096]{1,0:T(8,128)(2,1)} %weight_ref.5), custom_call_target="tpu_custom_call" | custom-call | flops 8000000000 | tf_op jit(solution)/shard_map/pallas_call | solution.py:466
  58.7 1.0 %shard_map.98 = (bf16[304,512]{1,0:T(8,128)(2,1)S(1)}, bf16[304,512]{1,0:T(8,128)(2,1)S(1)}) custom-call(bf16[304,512]{1,0:T(8,128)(2,1)S(1)} %get-tuple-element.58.heads_ref, bf16[304,512]{1,0:T(8,128)(2,1)S(1)} %collective-permute-done.3.rest_0_, bf16[304,512]{1,0:T(8,128)(2,1)S(1)} %collective-permute-done.4.rest_1_, bf16[512,4096]{1,0:T(8,128)(2,1)} %weight_ref.5, ...), custom_call_target="tpu_custom_call" | custom-call | flops 20000000000 | tf_op jit(solution)/shard_map/pallas_call | solution.py:429
  59.7 1.7 %collective-permute-start.5 = (bf16[304,512]{1,0:T(8,128)(2,1)S(1)}, bf16[304,512]{1,0:T(8,128)(2,1)S(1)}, u32[]{:S(2)}, u32[]{:S(2)}) collective-permute-start(bf16[304,512]{1,0:T(8,128)(2,1)S(1)} %get-tuple-element.61), channel_id=1, source_target_pairs={{0,1},{1,2},{2,3},{3,4},{4,5},{5,6},{6,7},{7,0},{8,9},{9,10},{10,1... | collective-permute-start | bytes 933896 | tf_op jit(solution)/shard_map/ppermute | solution.py:423
  61.4 1.0 %collective-permute-start.6 = (bf16[304,512]{1,0:T(8,128)(2,1)S(1)}, bf16[304,512]{1,0:T(8,128)(2,1)S(1)}, u32[]{:S(2)}, u32[]{:S(2)}) collective-permute-start(bf16[304,512]{1,0:T(8,128)(2,1)S(1)} %get-tuple-element.62), channel_id=1, source_target_pairs={{0,7},{1,0},{2,1},{3,2},{4,3},{5,4},{6,5},{7,6},{8,15},{9,8},{10,9... | collective-permute-start | bytes 933896 | tf_op jit(solution)/shard_map/ppermute | solution.py:423
  62.5 5.5 %all-to-all-start.3 = ((bf16[8,104,512]{2,1,0:T(8,128)(2,1)}), bf16[8,104,512]{2,1,0:T(8,128)(2,1)S(1)}, u32[]{:S(2)}, u32[]{:S(2)}) async-start(bf16[8,104,512]{2,1,0:T(8,128)(2,1)} %shard_map.97), calls=%async_computation.3 | async-start | bytes 1703936 | tf_op jit(solution)/shard_map/all_to_all | solution.py:368
  67.9 0.9 collective-permute-done.5.up_ref
  69.1 2.7 %shard_map.99.placed_ref = bf16[128,4,512]{2,1,0:T(4,128)(2,1)S(1)} custom-call(s32[8,128]{1,0:T(8,128)S(1)} %get-tuple-element.36.plan_src.plan_ref, bf16[304,512]{1,0:T(8,128)(2,1)S(1)} %get-tuple-element.58.heads_ref, bf16[304,512]{1,0:T(8,128)(2,1)S(1)} %collective-permute-done.5.up_ref, bf16[304,512]{1,0:T(8,128)(2,1)S(1)} %collective-permute-done.6.down_ref, ...), custom_call_target="tpu_custom_call" | custom-call | flops 40000000000 | tf_op jit(solution)/shard_map/pallas_call | solution.py:489
  71.8 19.0 %all-to-all-done.3.blocks_ref = bf16[8,104,512]{2,1,0:T(8,128)(2,1)S(1)} async-done(((bf16[8,104,512]{2,1,0:T(8,128)(2,1)}), bf16[8,104,512]{2,1,0:T(8,128)(2,1)S(1)}, u32[]{:S(2)}, u32[]{:S(2)}) %all-to-all-start.3) | async-done | bytes 852000 | tf_op jit(solution)/shard_map/all_to_all | solution.py:368
  90.8 1.4 %shard_map.100 = bf16[128,4,512]{2,1,0:T(4,128)(2,1)} custom-call(s32[8,128]{1,0:T(8,128)S(1)} %get-tuple-element.42.here_src, bf16[128,4,512]{2,1,0:T(4,128)(2,1)S(1)} %shard_map.99.placed_ref, bf16[8,104,512]{2,1,0:T(8,128)(2,1)S(1)} %all-to-all-done.3.blocks_ref), custom_call_target="tpu_custom_call" | custom-call | bytes 2097152 | tf_op jit(solution)/shard_map/pallas_call | solution.py:496
  (12 shorter events, 1.1 us)
Async XLA Ops:
  1.5 17.0 %all-to-all-start = ((s32[32,1,128]{2,1,0:T(1,128)}), s32[32,1,128]{2,1,0:T(1,128)S(1)}, u32[]{:S(2)}, u32[]{:S(2)}) async-start(s32[32,1,128]{2,1,0:T(1,128)} %bitcast.4), calls=%async_computation | async-start | bytes 32768 | tf_op jit(solution)/shard_map/all_to_all | solution.py:368
  16.8 13.4 %collective-permute-start = (bf16[304,512]{1,0:T(8,128)(2,1)S(1)}, bf16[304,512]{1,0:T(8,128)(2,1)}, u32[]{:S(2)}, u32[]{:S(2)}) collective-permute-start(bf16[304,512]{1,0:T(8,128)(2,1)S(1)} %get-tuple-element.47), channel_id=1, source_target_pairs={{0,1},{1,2},{2,3},{3,4},{4,5},{5,6},{6,7},{7,0},{8,9},{9,10},{10,1... | collective-permute-start | bytes 933896 | tf_op jit(solution)/shard_map/ppermute | solution.py:449
  20.2 18.0 %all-to-all-start.1 = ((bf16[64,4,768]{2,1,0:T(4,128)(2,1)}), bf16[64,4,768]{2,1,0:T(4,128)(2,1)S(1)}, u32[]{:S(2)}, u32[]{:S(2)}) async-start(bf16[64,4,768]{2,1,0:T(4,128)(2,1)} %get-tuple-element.45), calls=%async_computation.1 | async-start | bytes 786432 | tf_op jit(solution)/shard_map/all_to_all | solution.py:368
  32.7 13.3 %collective-permute-start.1 = (bf16[304,512]{1,0:T(8,128)(2,1)}, bf16[304,512]{1,0:T(8,128)(2,1)S(1)}, u32[]{:S(2)}, u32[]{:S(2)}) collective-permute-start(bf16[304,512]{1,0:T(8,128)(2,1)} %get-tuple-element.48), channel_id=1, source_target_pairs={{0,1},{1,2},{2,3},{3,4},{4,5},{5,6},{6,7},{7,0},{8,9},{9,10},{10,1... | collective-permute-start | bytes 933896 | tf_op jit(solution)/shard_map/ppermute | solution.py:423
  32.7 13.2 %collective-permute-start.2 = (bf16[304,512]{1,0:T(8,128)(2,1)S(1)}, bf16[304,512]{1,0:T(8,128)(2,1)S(1)}, u32[]{:S(2)}, u32[]{:S(2)}) collective-permute-start(bf16[304,512]{1,0:T(8,128)(2,1)S(1)} %get-tuple-element.49), channel_id=1, source_target_pairs={{0,7},{1,0},{2,1},{3,2},{4,3},{5,4},{6,5},{7,6},{8,15},{9,8},{10,9... | collective-permute-start | bytes 933896 | tf_op jit(solution)/shard_map/ppermute | solution.py:423
  40.5 14.5 %all-to-all-start.2 = ((bf16[64,4,512]{2,1,0:T(4,128)(2,1)}), bf16[64,4,512]{2,1,0:T(4,128)(2,1)S(1)}, u32[]{:S(2)}, u32[]{:S(2)}) async-start(bf16[64,4,512]{2,1,0:T(4,128)(2,1)} %shard_map.95), calls=%async_computation.2 | async-start | bytes 524288 | tf_op jit(solution)/shard_map/all_to_all | solution.py:368
  47.9 0.8 copy-start
  48.7 10.0 %collective-permute-start.3 = (bf16[304,512]{1,0:T(8,128)(2,1)S(1)}, bf16[304,512]{1,0:T(8,128)(2,1)S(1)}, u32[]{:S(2)}, u32[]{:S(2)}) collective-permute-start(bf16[304,512]{1,0:T(8,128)(2,1)S(1)} %get-tuple-element.55), channel_id=1, source_target_pairs={{0,1},{1,2},{2,3},{3,4},{4,5},{5,6},{6,7},{7,0},{8,9},{9,10},{10,1... | collective-permute-start | bytes 933896 | tf_op jit(solution)/shard_map/ppermute | solution.py:423
  48.7 10.0 %collective-permute-start.4 = (bf16[304,512]{1,0:T(8,128)(2,1)S(1)}, bf16[304,512]{1,0:T(8,128)(2,1)S(1)}, u32[]{:S(2)}, u32[]{:S(2)}) collective-permute-start(bf16[304,512]{1,0:T(8,128)(2,1)S(1)} %get-tuple-element.56), channel_id=1, source_target_pairs={{0,7},{1,0},{2,1},{3,2},{4,3},{5,4},{6,5},{7,6},{8,15},{9,8},{10,9... | collective-permute-start | bytes 933896 | tf_op jit(solution)/shard_map/ppermute | solution.py:423
  55.0 3.7 %copy-start.1 = (bf16[512,512]{1,0:T(8,128)(2,1)S(1)}, bf16[512,512]{1,0:T(8,128)(2,1)}, u32[]{:S(2)}) copy-start(bf16[512,512]{1,0:T(8,128)(2,1)} %copy-done) | copy-start | bytes 1572868
  59.7 9.2 %collective-permute-start.5 = (bf16[304,512]{1,0:T(8,128)(2,1)S(1)}, bf16[304,512]{1,0:T(8,128)(2,1)S(1)}, u32[]{:S(2)}, u32[]{:S(2)}) collective-permute-start(bf16[304,512]{1,0:T(8,128)(2,1)S(1)} %get-tuple-element.61), channel_id=1, source_target_pairs={{0,1},{1,2},{2,3},{3,4},{4,5},{5,6},{6,7},{7,0},{8,9},{9,10},{10,1... | collective-permute-start | bytes 933896 | tf_op jit(solution)/shard_map/ppermute | solution.py:423
  61.4 7.6 %collective-permute-start.6 = (bf16[304,512]{1,0:T(8,128)(2,1)S(1)}, bf16[304,512]{1,0:T(8,128)(2,1)S(1)}, u32[]{:S(2)}, u32[]{:S(2)}) collective-permute-start(bf16[304,512]{1,0:T(8,128)(2,1)S(1)} %get-tuple-element.62), channel_id=1, source_target_pairs={{0,7},{1,0},{2,1},{3,2},{4,3},{5,4},{6,5},{7,6},{8,15},{9,8},{10,9... | collective-permute-start | bytes 933896 | tf_op jit(solution)/shard_map/ppermute | solution.py:423
  62.5 28.3 %all-to-all-start.3 = ((bf16[8,104,512]{2,1,0:T(8,128)(2,1)}), bf16[8,104,512]{2,1,0:T(8,128)(2,1)S(1)}, u32[]{:S(2)}, u32[]{:S(2)}) async-start(bf16[8,104,512]{2,1,0:T(8,128)(2,1)} %shard_map.97), calls=%async_computation.3 | async-start | bytes 1703936 | tf_op jit(solution)/shard_map/all_to_all | solution.py:368

commit v9 on v8

--- a/solution.py
+++ b/solution.py
@@ -22,7 +22,7 @@
         kernel,
         out_shape=out_shape,
         in_specs=in_specs,
-        out_specs=out if single else [out] * len(out_shape),
+        out_specs=out if single or isinstance(out, list) else [out] * len(out_shape),
         scratch_shapes=list(scratch),
         cost_estimate=pl.CostEstimate(
             flops=flops, bytes_accessed=nbytes, transcendentals=exps
@@ -221,18 +221,23 @@
     up_ref[...] = jnp.dot(heads_ref[...], wbuf[...], preferred_element_type=F32).astype(BF16)
 
 
+def load_blocks(blocks, weight_ref, parts, sem):
+    columns = parts[0].shape[1] if parts else 1
+    ring = weight_ref.shape[1] // columns
+    copies = []
+    for j, step in enumerate(blocks):
+        at = pl.multiple_of(lax.rem(lax.axis_index("tp") + step, ring) * columns, columns)
+        copies.append(pltpu.make_async_copy(weight_ref.at[:, pl.ds(at, columns)], parts[j], sem.at[j]))
+    return copies
+
+
 def hop_kernel(blocks, came, held, heads_ref, *rest):
     sums, weight_ref, rest = rest[:came], rest[came], rest[came + 1 :]
     held_refs, rest = rest[:held], rest[held:]
     outs, kept, rest = rest[:2], rest[2 : len(blocks)], rest[len(blocks) :]
     bufs, sem, scratch = rest[:came], rest[came], rest[came + 1 :]
-    columns = outs[0].shape[1]
-    ring = weight_ref.shape[1] // columns
     parts = [*held_refs, *scratch, *kept]
-    loads = {}
-    for j in range(held, len(blocks)):
-        at = pl.multiple_of(lax.rem(lax.axis_index("tp") + blocks[j], ring) * columns, columns)
-        loads[j] = pltpu.make_async_copy(weight_ref.at[:, pl.ds(at, columns)], parts[j], sem.at[2 + j])
+    loads = dict(enumerate(load_blocks(blocks[held:], weight_ref, parts[held:], sem.at[pl.ds(2, 8)]), held))
     sums = [pltpu.make_async_copy(src, dst, sem.at[i]) for i, (src, dst) in enumerate(zip(sums, bufs))]
     for copy in [loads[j] for j in loads if j < 2] + sums + [loads[j] for j in loads if j >= 2]:
         copy.start()
@@ -277,29 +282,29 @@
             out_ref[entry(i), :, h * head : (h + 1) * head] = o[h * steps : (h + 1) * steps].astype(BF16)
 
 
-def arrived_kernel(here_src, back_ref, weight_ref, out_ref, here_ref, heads, wbuf, sums, hsem, wsem, osem):
+def arrived_kernel(order, here_src, back_ref, weight_ref, out_ref, *rest):
+    kept, (here_ref, heads, wbuf, sums, hsem, wsem, osem) = rest[:2], rest[2:]
     listed = pltpu.make_async_copy(here_src, here_ref, hsem)
     listed.start()
     steps = back_ref.shape[1]
-    ring, lines, columns = out_ref.shape
+    ring, lines, _ = out_ref.shape
     rows = lines // steps
-    parts = [
-        pltpu.make_async_copy(weight_ref.at[:, pl.ds(k * columns, columns)], wbuf.at[k], wsem.at[k])
-        for k in range(ring)
-    ]
-    for copy in parts:
+    parts = [*kept, *(wbuf.at[j] for j in range(ring - 2))]
+    loads = load_blocks(order, weight_ref, parts, wsem)
+    for copy in loads:
         copy.start()
     listed.wait()
     for j in range(heads.shape[0] // 16):
         four = [back_ref[here_ref[HERE_ENTRY, min(4 * j + u, rows - 1)]].astype(F32) for u in range(4)]
         heads[16 * j : 16 * j + 16, :] = jnp.concatenate(four, axis=0).astype(BF16)
     done = []
-    for k, copy in enumerate(parts):
-        copy.wait()
-        terms = jnp.dot(heads[...], wbuf[k], preferred_element_type=F32)
-        sums[k] = terms[:lines].astype(BF16)
-        done.append(pltpu.make_async_copy(sums.at[k], out_ref.at[k], osem.at[k]))
-        done[k].start()
+    for j, k in enumerate(order):
+        loads[j].wait()
+        terms = jnp.dot(heads[...], parts[j][...], preferred_element_type=F32)
+        sums[j] = terms[:lines].astype(BF16)
+        to = lax.rem(lax.axis_index("tp") + k, ring)
+        done.append(pltpu.make_async_copy(sums.at[j], out_ref.at[to], osem.at[j]))
+        done[j].start()
     for copy in done:
         copy.wait()
 
@@ -459,29 +464,30 @@
     )(plan, asked, leave_keys, leave_values)
     back, heads = barrier((back, heads))
     back = exchange(back, "group")
-    up, down, *kept = add(2, up, down, keep=(1, ring - 1))
+    up, down = add(2, up, down)
     back = barrier((back, up, down))[0]
     up, down = hop(up, down)
     arrived = moves * steps
-    blocks = call(
-        arrived_kernel,
-        shape((ring, arrived, columns), BF16),
+    order = (1, ring - 1, 0, *range(2, ring - 1))
+    blocks, *late = call(
+        functools.partial(arrived_kernel, order),
+        [shape((ring, arrived, columns), BF16)] + [shape(*part)] * 2,
         [pl.BlockSpec(memory_space=pl.ANY), VMEM, ANY],
         [
             pltpu.SMEM((8, 128), I32),
             pltpu.VMEM((-(-arrived // 16) * 16, wide), BF16),
-            pltpu.VMEM((ring, wide, columns), BF16),
+            pltpu.VMEM((ring - 2, wide, columns), BF16),
             pltpu.VMEM((ring, arrived, columns), BF16),
             pltpu.SemaphoreType.DMA,
             pltpu.SemaphoreType.DMA((ring,)),
             pltpu.SemaphoreType.DMA((ring,)),
         ],
-        out=ANY,
+        out=[ANY, VMEM, VMEM],
         flops=ARRIVED_COST,
         limit=10,
     )(here, back, out_weight)
     blocks, heads = barrier((blocks, heads))
-    up, down = add(1, up, down, held=kept)
+    up, down = add(1, up, down, held=late)
     blocks = barrier((blocks, up, down))[0]
     blocks = exchange(blocks, "tp")
     up, down = hop(up, down)

time: 92.7 us -> 92.5 us (level)
  transfers between devices with their start and end apart: 11 -> 11, of which waited for: 6 -> 5; matrix products, arithmetic and copies ran while one was open for 0% -> 0% of each run, Pallas kernels for 23% -> 23%
where the time goes in v9:
time: 92.5 us; the launch traced here: 92.1 us
  starting transfers between devices  37.1 us (40%)
  waiting for transfers between devices  29.6 us (32%)
  Pallas kernels  25.3 us (27%)
    all_to_all x4, starting transfers between devices, exchange(): return lax.all_to_all(x, axis, split_axis=0, concat_axis=0, tiled=True)  27.1 us
    all_to_all x4, waiting for transfers between devices, exchange(): return lax.all_to_all(x, axis, split_axis=0, concat_axis=0, tiled=True)  25.5 us
    ppermute x6, starting transfers between devices, hop(): return (lax.ppermute(u, 'tp', ahead), lax.ppermute(d, 'tp', astern))  8.25 us
    pallas_call x1, Pallas kernels, on_device(): call(staying_kernel, [shape((tokens, columns), BF16), shape((tokens, wide...  6.68 us
    pallas_call x3, Pallas kernels, add(): call(functools.partial(hop_kernel, blocks, len(sums), len(held)), [shape(...  5.33 us
    pallas_call x1, Pallas kernels, on_device(): call(functools.partial(arrived_kernel, order), [shape((ring, arrived, col...  3.65 us
    pallas_call x1, Pallas kernels, on_device(): call(place_kernel, shape((slots, steps, columns), BF16), [SMEM] + [VMEM]...  2.72 us
    ppermute x1, waiting for transfers between devices, on_device(): up = lax.ppermute(up, 'tp', ahead)  2.26 us
  transfers between devices with their start and end apart: 11, of which 5 were waited for; matrix products, arithmetic and copies ran while one was open for 0% of the time, Pallas kernels for 23%

profile of v9, /device:TPU:1, one launch (start us, length us, event | category | flops | bytes accessed | tf_op | source)
XLA Modules:
  0.0 92.1 jit_solution(13048860371561164153)
XLA Ops:
  0.0 1.5 %shard_map.91 = (s32[32,128]{1,0:T(8,128)}, s32[8,128]{1,0:T(8,128)S(1)}) custom-call(s32[3,26]{1,0:T(4,128)} %bitcast.9, s32[1,128]{1,0:T(1,128)} %bitcast.10, s32[1,128]{1,0:T(1,128)} %bitcast.11), custom_call_target="tpu_custom_call" | custom-call | bytes 65536 | tf_op jit(solution)/shard_map/pallas_call | solution.py:383
  1.5 8.6 %all-to-all-start = ((s32[32,1,128]{2,1,0:T(1,128)}), s32[32,1,128]{2,1,0:T(1,128)S(1)}, u32[]{:S(2)}, u32[]{:S(2)}) async-start(s32[32,1,128]{2,1,0:T(1,128)} %bitcast.4), calls=%async_computation | async-start | bytes 32768 | tf_op jit(solution)/shard_map/all_to_all | solution.py:373
  10.2 6.7 %shard_map.92 = (bf16[304,512]{1,0:T(8,128)(2,1)S(1)}, bf16[304,512]{1,0:T(8,128)(2,1)S(1)}, bf16[128,4,768]{2,1,0:T(4,128)(2,1)S(1)}, bf16[26,128,128]{2,1,0:T(8,128)(2,1)S(1)}, bf16[26,128,128]{2,1,0:T(8,128)(2,1)S(1)}) custom-call(s32[8,128]{1,0:T(8,128)S(1)} %get-tuple-element.37.plan_src.plan_ref, bf16[128,4,512]{2,1,0:T(4,128)(2,1)} %query_ref.1, ...), custom_call_target="tpu_custom_call" | custom-call | flops 159383552 | bytes 16777216 | tf_op jit(solution)/shard_map/pallas_call | solution.py:398
  16.8 1.7 %collective-permute-start = (bf16[304,512]{1,0:T(8,128)(2,1)S(1)}, bf16[304,512]{1,0:T(8,128)(2,1)}, u32[]{:S(2)}, u32[]{:S(2)}) collective-permute-start(bf16[304,512]{1,0:T(8,128)(2,1)S(1)} %get-tuple-element.48), channel_id=1, source_target_pairs={{0,1},{1,2},{2,3},{3,4},{4,5},{5,6},{6,7},{7,0},{8,9},{9,10},{10,1... | collective-permute-start | bytes 933896 | tf_op jit(solution)/shard_map/ppermute | solution.py:454
  18.6 1.7 %shard_map.93 = (bf16[64,4,768]{2,1,0:T(4,128)(2,1)}, s32[8,128]{1,0:T(8,128)S(1)}) custom-call(s32[32,128]{1,0:T(8,128)S(1)} %bitcast.7, s32[32,128]{1,0:T(8,128)S(1)} %bitcast.8, bf16[128,4,768]{2,1,0:T(4,128)(2,1)S(1)} %get-tuple-element.42.fresh_ref), custom_call_target="tpu_custom_call" | custom-call | flops 8000000000 | tf_op jit(solution)/shard_map/pallas_call | solution.py:445
  20.2 7.7 %all-to-all-start.1 = ((bf16[64,4,768]{2,1,0:T(4,128)(2,1)}), bf16[64,4,768]{2,1,0:T(4,128)(2,1)S(1)}, u32[]{:S(2)}, u32[]{:S(2)}) async-start(bf16[64,4,768]{2,1,0:T(4,128)(2,1)} %get-tuple-element.46), calls=%async_computation.1 | async-start | bytes 786432 | tf_op jit(solution)/shard_map/all_to_all | solution.py:373
  27.9 2.3 %collective-permute-done.rest_0_ = bf16[304,512]{1,0:T(8,128)(2,1)} collective-permute-done((bf16[304,512]{1,0:T(8,128)(2,1)S(1)}, bf16[304,512]{1,0:T(8,128)(2,1)}, u32[]{:S(2)}, u32[]{:S(2)}) %collective-permute-start) | collective-permute-done | bytes 311328 | tf_op jit(solution)/shard_map/ppermute | solution.py:454
  30.2 2.5 %shard_map.94 = (bf16[304,512]{1,0:T(8,128)(2,1)}, bf16[304,512]{1,0:T(8,128)(2,1)S(1)}) custom-call(bf16[304,512]{1,0:T(8,128)(2,1)S(1)} %get-tuple-element.60.heads_ref, bf16[304,512]{1,0:T(8,128)(2,1)} %collective-permute-done.rest_0_, bf16[512,4096]{1,0:T(8,128)(2,1)} %weight_ref.5), custom_call_target="tpu_custom_call" | custom-call | flops 20000000000 | tf_op jit(solution)/shard_map/pallas_call | solution.py:434
  32.7 2.7 %collective-permute-start.2 = (bf16[304,512]{1,0:T(8,128)(2,1)S(1)}, bf16[304,512]{1,0:T(8,128)(2,1)S(1)}, u32[]{:S(2)}, u32[]{:S(2)}) collective-permute-start(bf16[304,512]{1,0:T(8,128)(2,1)S(1)} %get-tuple-element.50), channel_id=1, source_target_pairs={{0,7},{1,0},{2,1},{3,2},{4,3},{5,4},{6,5},{7,6},{8,15},{9,8},{10,9... | collective-permute-start | bytes 933896 | tf_op jit(solution)/shard_map/ppermute | solution.py:428
  35.4 2.8 %all-to-all-done.1.asked_ref = bf16[64,4,768]{2,1,0:T(4,128)(2,1)S(1)} async-done(((bf16[64,4,768]{2,1,0:T(4,128)(2,1)}), bf16[64,4,768]{2,1,0:T(4,128)(2,1)S(1)}, u32[]{:S(2)}, u32[]{:S(2)}) %all-to-all-start.1) | async-done | bytes 393248 | tf_op jit(solution)/shard_map/all_to_all | solution.py:373
  38.2 2.2 %shard_map.95 = bf16[64,4,512]{2,1,0:T(4,128)(2,1)} custom-call(s32[8,128]{1,0:T(8,128)S(1)} %get-tuple-element.37.plan_src.plan_ref, bf16[64,4,768]{2,1,0:T(4,128)(2,1)S(1)} %all-to-all-done.1.asked_ref, bf16[26,128,128]{2,1,0:T(8,128)(2,1)S(1)} %get-tuple-element.52.keys_ref, bf16[26,128,128]{2,1,0:T(8,128)(2,1)S(1)} %get-tuple-element.53.values_ref), custom_call_target="tpu_custom_call" | custom-call | tf_op jit(solution)/shard_map/pallas_call | solution.py:459
  40.5 5.5 %all-to-all-start.2 = ((bf16[64,4,512]{2,1,0:T(4,128)(2,1)}), bf16[64,4,512]{2,1,0:T(4,128)(2,1)S(1)}, u32[]{:S(2)}, u32[]{:S(2)}) async-start(bf16[64,4,512]{2,1,0:T(4,128)(2,1)} %shard_map.95), calls=%async_computation.2 | async-start | bytes 524288 | tf_op jit(solution)/shard_map/all_to_all | solution.py:373
  46.0 1.9 %shard_map.96 = (bf16[304,512]{1,0:T(8,128)(2,1)S(1)}, bf16[304,512]{1,0:T(8,128)(2,1)S(1)}) custom-call(bf16[304,512]{1,0:T(8,128)(2,1)S(1)} %get-tuple-element.60.heads_ref, bf16[304,512]{1,0:T(8,128)(2,1)S(1)} %collective-permute-done.1.rest_0_, bf16[304,512]{1,0:T(8,128)(2,1)S(1)} %collective-permute-done.2.rest_1_, bf16[512,4096]{1,0:T(8,128)(2,1)} %weight_ref.5), custom_call_target="tpu_custom_call" | custom-call | flops 20000000000 | tf_op jit(solution)/shard_map/pallas_call | solution.py:434
  48.0 2.7 %collective-permute-start.4 = (bf16[304,512]{1,0:T(8,128)(2,1)S(1)}, bf16[304,512]{1,0:T(8,128)(2,1)S(1)}, u32[]{:S(2)}, u32[]{:S(2)}) collective-permute-start(bf16[304,512]{1,0:T(8,128)(2,1)S(1)} %get-tuple-element.57), channel_id=1, source_target_pairs={{0,7},{1,0},{2,1},{3,2},{4,3},{5,4},{6,5},{7,6},{8,15},{9,8},{10,9... | collective-permute-start | bytes 933896 | tf_op jit(solution)/shard_map/ppermute | solution.py:428
  50.7 4.3 %all-to-all-done.2.back_ref = bf16[64,4,512]{2,1,0:T(4,128)(2,1)S(1)} async-done(((bf16[64,4,512]{2,1,0:T(4,128)(2,1)}), bf16[64,4,512]{2,1,0:T(4,128)(2,1)S(1)}, u32[]{:S(2)}, u32[]{:S(2)}) %all-to-all-start.2) | async-done | bytes 262176 | tf_op jit(solution)/shard_map/all_to_all | solution.py:373
  55.0 3.7 %shard_map.97 = (bf16[8,104,512]{2,1,0:T(8,128)(2,1)}, bf16[512,512]{1,0:T(8,128)(2,1)S(1)}, bf16[512,512]{1,0:T(8,128)(2,1)S(1)}) custom-call(s32[8,128]{1,0:T(8,128)S(1)} %get-tuple-element.43.here_src, bf16[64,4,512]{2,1,0:T(4,128)(2,1)S(1)} %all-to-all-done.2.back_ref, bf16[512,4096]{1,0:T(8,128)(2,1)} %weight_ref.5), custom_call_target="tpu_custom_call" | custom-call | flops 8000000000 | tf_op jit(solution)/shard_map/pallas_call | solution.py:472
  58.7 1.0 %shard_map.98 = (bf16[304,512]{1,0:T(8,128)(2,1)S(1)}, bf16[304,512]{1,0:T(8,128)(2,1)S(1)}) custom-call(bf16[304,512]{1,0:T(8,128)(2,1)S(1)} %get-tuple-element.60.heads_ref, bf16[304,512]{1,0:T(8,128)(2,1)S(1)} %collective-permute-done.3.rest_0_, bf16[304,512]{1,0:T(8,128)(2,1)S(1)} %collective-permute-done.4.rest_1_, bf16[512,4096]{1,0:T(8,128)(2,1)} %weight_ref.5, ...), custom_call_target="tpu_custom_call" | custom-call | flops 20000000000 | tf_op jit(solution)/shard_map/pallas_call | solution.py:434
  59.6 1.1 %collective-permute-start.5 = (bf16[304,512]{1,0:T(8,128)(2,1)S(1)}, bf16[304,512]{1,0:T(8,128)(2,1)S(1)}, u32[]{:S(2)}, u32[]{:S(2)}) collective-permute-start(bf16[304,512]{1,0:T(8,128)(2,1)S(1)} %get-tuple-element.63), channel_id=1, source_target_pairs={{0,1},{1,2},{2,3},{3,4},{4,5},{5,6},{6,7},{7,0},{8,9},{9,10},{10,1... | collective-permute-start | bytes 933896 | tf_op jit(solution)/shard_map/ppermute | solution.py:428
  60.7 1.7 %collective-permute-start.6 = (bf16[304,512]{1,0:T(8,128)(2,1)S(1)}, bf16[304,512]{1,0:T(8,128)(2,1)S(1)}, u32[]{:S(2)}, u32[]{:S(2)}) collective-permute-start(bf16[304,512]{1,0:T(8,128)(2,1)S(1)} %get-tuple-element.64), channel_id=1, source_target_pairs={{0,7},{1,0},{2,1},{3,2},{4,3},{5,4},{6,5},{7,6},{8,15},{9,8},{10,9... | collective-permute-start | bytes 933896 | tf_op jit(solution)/shard_map/ppermute | solution.py:428
  62.4 5.3 %all-to-all-start.3 = ((bf16[8,104,512]{2,1,0:T(8,128)(2,1)}), bf16[8,104,512]{2,1,0:T(8,128)(2,1)S(1)}, u32[]{:S(2)}, u32[]{:S(2)}) async-start(bf16[8,104,512]{2,1,0:T(8,128)(2,1)} %get-tuple-element.66), calls=%async_computation.3 | async-start | bytes 1703936 | tf_op jit(solution)/shard_map/all_to_all | solution.py:373
  67.7 1.8 %collective-permute-done.5.up_ref = bf16[304,512]{1,0:T(8,128)(2,1)S(1)} collective-permute-done((bf16[304,512]{1,0:T(8,128)(2,1)S(1)}, bf16[304,512]{1,0:T(8,128)(2,1)S(1)}, u32[]{:S(2)}, u32[]{:S(2)}) %collective-permute-start.5) | collective-permute-done | bytes 311328 | tf_op jit(solution)/shard_map/ppermute | solution.py:428
  69.5 2.7 %shard_map.99.placed_ref = bf16[128,4,512]{2,1,0:T(4,128)(2,1)S(1)} custom-call(s32[8,128]{1,0:T(8,128)S(1)} %get-tuple-element.37.plan_src.plan_ref, bf16[304,512]{1,0:T(8,128)(2,1)S(1)} %get-tuple-element.60.heads_ref, bf16[304,512]{1,0:T(8,128)(2,1)S(1)} %collective-permute-done.5.up_ref, bf16[304,512]{1,0:T(8,128)(2,1)S(1)} %collective-permute-done.6.down_ref, ...), custom_call_target="tpu_custom_call" | custom-call | flops 40000000000 | tf_op jit(solution)/shard_map/pallas_call | solution.py:495
  72.3 18.4 %all-to-all-done.3.blocks_ref = bf16[8,104,512]{2,1,0:T(8,128)(2,1)S(1)} async-done(((bf16[8,104,512]{2,1,0:T(8,128)(2,1)}), bf16[8,104,512]{2,1,0:T(8,128)(2,1)S(1)}, u32[]{:S(2)}, u32[]{:S(2)}) %all-to-all-start.3) | async-done | bytes 852000 | tf_op jit(solution)/shard_map/all_to_all | solution.py:373
  90.7 1.4 %shard_map.100 = bf16[128,4,512]{2,1,0:T(4,128)(2,1)} custom-call(s32[8,128]{1,0:T(8,128)S(1)} %get-tuple-element.43.here_src, bf16[128,4,512]{2,1,0:T(4,128)(2,1)S(1)} %shard_map.99.placed_ref, bf16[8,104,512]{2,1,0:T(8,128)(2,1)S(1)} %all-to-all-done.3.blocks_ref), custom_call_target="tpu_custom_call" | custom-call | bytes 2097152 | tf_op jit(solution)/shard_map/pallas_call | solution.py:502
  (8 shorter events, 0.2 us)
Async XLA Ops:
  1.5 17.0 %all-to-all-start = ((s32[32,1,128]{2,1,0:T(1,128)}), s32[32,1,128]{2,1,0:T(1,128)S(1)}, u32[]{:S(2)}, u32[]{:S(2)}) async-start(s32[32,1,128]{2,1,0:T(1,128)} %bitcast.4), calls=%async_computation | async-start | bytes 32768 | tf_op jit(solution)/shard_map/all_to_all | solution.py:373
  16.8 13.3 %collective-permute-start = (bf16[304,512]{1,0:T(8,128)(2,1)S(1)}, bf16[304,512]{1,0:T(8,128)(2,1)}, u32[]{:S(2)}, u32[]{:S(2)}) collective-permute-start(bf16[304,512]{1,0:T(8,128)(2,1)S(1)} %get-tuple-element.48), channel_id=1, source_target_pairs={{0,1},{1,2},{2,3},{3,4},{4,5},{5,6},{6,7},{7,0},{8,9},{9,10},{10,1... | collective-permute-start | bytes 933896 | tf_op jit(solution)/shard_map/ppermute | solution.py:454
  20.2 18.0 %all-to-all-start.1 = ((bf16[64,4,768]{2,1,0:T(4,128)(2,1)}), bf16[64,4,768]{2,1,0:T(4,128)(2,1)S(1)}, u32[]{:S(2)}, u32[]{:S(2)}) async-start(bf16[64,4,768]{2,1,0:T(4,128)(2,1)} %get-tuple-element.46), calls=%async_computation.1 | async-start | bytes 786432 | tf_op jit(solution)/shard_map/all_to_all | solution.py:373
  32.6 13.3 %collective-permute-start.1 = (bf16[304,512]{1,0:T(8,128)(2,1)}, bf16[304,512]{1,0:T(8,128)(2,1)S(1)}, u32[]{:S(2)}, u32[]{:S(2)}) collective-permute-start(bf16[304,512]{1,0:T(8,128)(2,1)} %get-tuple-element.49), channel_id=1, source_target_pairs={{0,1},{1,2},{2,3},{3,4},{4,5},{5,6},{6,7},{7,0},{8,9},{9,10},{10,1... | collective-permute-start | bytes 933896 | tf_op jit(solution)/shard_map/ppermute | solution.py:428
  32.7 13.3 %collective-permute-start.2 = (bf16[304,512]{1,0:T(8,128)(2,1)S(1)}, bf16[304,512]{1,0:T(8,128)(2,1)S(1)}, u32[]{:S(2)}, u32[]{:S(2)}) collective-permute-start(bf16[304,512]{1,0:T(8,128)(2,1)S(1)} %get-tuple-element.50), channel_id=1, source_target_pairs={{0,7},{1,0},{2,1},{3,2},{4,3},{5,4},{6,5},{7,6},{8,15},{9,8},{10,9... | collective-permute-start | bytes 933896 | tf_op jit(solution)/shard_map/ppermute | solution.py:428
  40.5 14.5 %all-to-all-start.2 = ((bf16[64,4,512]{2,1,0:T(4,128)(2,1)}), bf16[64,4,512]{2,1,0:T(4,128)(2,1)S(1)}, u32[]{:S(2)}, u32[]{:S(2)}) async-start(bf16[64,4,512]{2,1,0:T(4,128)(2,1)} %shard_map.95), calls=%async_computation.2 | async-start | bytes 524288 | tf_op jit(solution)/shard_map/all_to_all | solution.py:373
  47.9 10.7 %collective-permute-start.3 = (bf16[304,512]{1,0:T(8,128)(2,1)S(1)}, bf16[304,512]{1,0:T(8,128)(2,1)S(1)}, u32[]{:S(2)}, u32[]{:S(2)}) collective-permute-start(bf16[304,512]{1,0:T(8,128)(2,1)S(1)} %get-tuple-element.56), channel_id=1, source_target_pairs={{0,1},{1,2},{2,3},{3,4},{4,5},{5,6},{6,7},{7,0},{8,9},{9,10},{10,1... | collective-permute-start | bytes 933896 | tf_op jit(solution)/shard_map/ppermute | solution.py:428
  48.0 10.6 %collective-permute-start.4 = (bf16[304,512]{1,0:T(8,128)(2,1)S(1)}, bf16[304,512]{1,0:T(8,128)(2,1)S(1)}, u32[]{:S(2)}, u32[]{:S(2)}) collective-permute-start(bf16[304,512]{1,0:T(8,128)(2,1)S(1)} %get-tuple-element.57), channel_id=1, source_target_pairs={{0,7},{1,0},{2,1},{3,2},{4,3},{5,4},{6,5},{7,6},{8,15},{9,8},{10,9... | collective-permute-start | bytes 933896 | tf_op jit(solution)/shard_map/ppermute | solution.py:428
  59.6 9.9 %collective-permute-start.5 = (bf16[304,512]{1,0:T(8,128)(2,1)S(1)}, bf16[304,512]{1,0:T(8,128)(2,1)S(1)}, u32[]{:S(2)}, u32[]{:S(2)}) collective-permute-start(bf16[304,512]{1,0:T(8,128)(2,1)S(1)} %get-tuple-element.63), channel_id=1, source_target_pairs={{0,1},{1,2},{2,3},{3,4},{4,5},{5,6},{6,7},{7,0},{8,9},{9,10},{10,1... | collective-permute-start | bytes 933896 | tf_op jit(solution)/shard_map/ppermute | solution.py:428
  60.7 8.8 %collective-permute-start.6 = (bf16[304,512]{1,0:T(8,128)(2,1)S(1)}, bf16[304,512]{1,0:T(8,128)(2,1)S(1)}, u32[]{:S(2)}, u32[]{:S(2)}) collective-permute-start(bf16[304,512]{1,0:T(8,128)(2,1)S(1)} %get-tuple-element.64), channel_id=1, source_target_pairs={{0,7},{1,0},{2,1},{3,2},{4,3},{5,4},{6,5},{7,6},{8,15},{9,8},{10,9... | collective-permute-start | bytes 933896 | tf_op jit(solution)/shard_map/ppermute | solution.py:428
  62.4 28.3 %all-to-all-start.3 = ((bf16[8,104,512]{2,1,0:T(8,128)(2,1)}), bf16[8,104,512]{2,1,0:T(8,128)(2,1)S(1)}, u32[]{:S(2)}, u32[]{:S(2)}) async-start(bf16[8,104,512]{2,1,0:T(8,128)(2,1)} %get-tuple-element.66), calls=%async_computation.3 | async-start | bytes 1703936 | tf_op jit(solution)/shard_map/all_to_all | solution.py:373

commit v10 on v9

--- a/solution.py
+++ b/solution.py
@@ -199,6 +199,13 @@
     def slot(i):
         return plan_ref[STAY_SLOT, i]
 
+    def await_values(b):
+        if b == 0:
+            for i in range(leave_keys_ref.shape[0]):
+                leave_keys_ref[i] = kbuf[plan_ref[LEAVE_SLOT, i], 0:cache, :]
+        for c in due[b]:
+            values[c].wait()
+
     for copy in [listed] + fresh:
         copy.wait()
     mixed = attend(
@@ -208,14 +215,13 @@
         lambda i: (fresh_ref[slot(i), :, wide : wide + head], fresh_ref[slot(i), :, wide + head : wide + 2 * head]),
         lambda i: plan_ref[STAY_LENGTH, i],
         lambda b: [keys[c].wait() for c in due[b]],
-        lambda b: [values[c].wait() for c in due[b]],
+        await_values,
     )
     for j in range(rows // 4):
         for h in range(wide // head):
             tile = jnp.concatenate([o[h * steps : (h + 1) * steps] for o in mixed[4 * j : 4 * j + 4]], axis=0)
             heads_ref[16 * j : 16 * j + 16, h * head : (h + 1) * head] = tile.astype(BF16)
     for i in range(leave_keys_ref.shape[0]):
-        leave_keys_ref[i] = kbuf[plan_ref[LEAVE_SLOT, i], 0:cache, :]
         leave_values_ref[i] = vbuf[plan_ref[LEAVE_SLOT, i], 0:cache, :]
     far.wait()
     up_ref[...] = jnp.dot(heads_ref[...], wbuf[...], preferred_element_type=F32).astype(BF16)

time: 92.5 us -> 92.6 us (level)
  no operation moved by 1% of the time
where the time goes in v10:
time: 92.6 us; the launch traced here: 92.1 us
  starting transfers between devices  37.1 us (40%)
  waiting for transfers between devices  29.6 us (32%)
  Pallas kernels  25.3 us (27%)
    all_to_all x4, starting transfers between devices, exchange(): return lax.all_to_all(x, axis, split_axis=0, concat_axis=0, tiled=True)  27.1 us
    all_to_all x4, waiting for transfers between devices, exchange(): return lax.all_to_all(x, axis, split_axis=0, concat_axis=0, tiled=True)  25.5 us
    ppermute x6, starting transfers between devices, hop(): return (lax.ppermute(u, 'tp', ahead), lax.ppermute(d, 'tp', astern))  8.25 us
    pallas_call x1, Pallas kernels, on_device(): call(staying_kernel, [shape((tokens, columns), BF16), shape((tokens, wide...  6.69 us
    pallas_call x3, Pallas kernels, add(): call(functools.partial(hop_kernel, blocks, len(sums), len(held)), [shape(...  5.33 us
    pallas_call x1, Pallas kernels, on_device(): call(functools.partial(arrived_kernel, order), [shape((ring, arrived, col...  3.64 us
    pallas_call x1, Pallas kernels, on_device(): call(place_kernel, shape((slots, steps, columns), BF16), [SMEM] + [VMEM]...  2.72 us
    ppermute x1, waiting for transfers between devices, on_device(): up = lax.ppermute(up, 'tp', ahead)  2.27 us
  transfers between devices with their start and end apart: 11, of which 5 were waited for; matrix products, arithmetic and copies ran while one was open for 0% of the time, Pallas kernels for 23%

profile of v10, /device:TPU:1, one launch (start us, length us, event | category | flops | bytes accessed | tf_op | source)
XLA Modules:
  0.0 92.1 jit_solution(10230648773087827578)
XLA Ops:
  0.0 1.5 %shard_map.91 = (s32[32,128]{1,0:T(8,128)}, s32[8,128]{1,0:T(8,128)S(1)}) custom-call(s32[3,26]{1,0:T(4,128)} %bitcast.9, s32[1,128]{1,0:T(1,128)} %bitcast.10, s32[1,128]{1,0:T(1,128)} %bitcast.11), custom_call_target="tpu_custom_call" | custom-call | bytes 65536 | tf_op jit(solution)/shard_map/pallas_call | solution.py:389
  1.5 8.6 %all-to-all-start = ((s32[32,1,128]{2,1,0:T(1,128)}), s32[32,1,128]{2,1,0:T(1,128)S(1)}, u32[]{:S(2)}, u32[]{:S(2)}) async-start(s32[32,1,128]{2,1,0:T(1,128)} %bitcast.4), calls=%async_computation | async-start | bytes 32768 | tf_op jit(solution)/shard_map/all_to_all | solution.py:379
  10.2 6.7 %shard_map.92 = (bf16[304,512]{1,0:T(8,128)(2,1)S(1)}, bf16[304,512]{1,0:T(8,128)(2,1)S(1)}, bf16[128,4,768]{2,1,0:T(4,128)(2,1)S(1)}, bf16[26,128,128]{2,1,0:T(8,128)(2,1)S(1)}, bf16[26,128,128]{2,1,0:T(8,128)(2,1)S(1)}) custom-call(s32[8,128]{1,0:T(8,128)S(1)} %get-tuple-element.37.plan_src.plan_ref, bf16[128,4,512]{2,1,0:T(4,128)(2,1)} %query_ref.1, ...), custom_call_target="tpu_custom_call" | custom-call | flops 159383552 | bytes 16777216 | tf_op jit(solution)/shard_map/pallas_call | solution.py:404
  16.8 1.7 %collective-permute-start = (bf16[304,512]{1,0:T(8,128)(2,1)S(1)}, bf16[304,512]{1,0:T(8,128)(2,1)}, u32[]{:S(2)}, u32[]{:S(2)}) collective-permute-start(bf16[304,512]{1,0:T(8,128)(2,1)S(1)} %get-tuple-element.48), channel_id=1, source_target_pairs={{0,1},{1,2},{2,3},{3,4},{4,5},{5,6},{6,7},{7,0},{8,9},{9,10},{10,1... | collective-permute-start | bytes 933896 | tf_op jit(solution)/shard_map/ppermute | solution.py:460
  18.6 1.7 %shard_map.93 = (bf16[64,4,768]{2,1,0:T(4,128)(2,1)}, s32[8,128]{1,0:T(8,128)S(1)}) custom-call(s32[32,128]{1,0:T(8,128)S(1)} %bitcast.7, s32[32,128]{1,0:T(8,128)S(1)} %bitcast.8, bf16[128,4,768]{2,1,0:T(4,128)(2,1)S(1)} %get-tuple-element.42.fresh_ref), custom_call_target="tpu_custom_call" | custom-call | flops 8000000000 | tf_op jit(solution)/shard_map/pallas_call | solution.py:451
  20.2 7.7 %all-to-all-start.1 = ((bf16[64,4,768]{2,1,0:T(4,128)(2,1)}), bf16[64,4,768]{2,1,0:T(4,128)(2,1)S(1)}, u32[]{:S(2)}, u32[]{:S(2)}) async-start(bf16[64,4,768]{2,1,0:T(4,128)(2,1)} %get-tuple-element.46), calls=%async_computation.1 | async-start | bytes 786432 | tf_op jit(solution)/shard_map/all_to_all | solution.py:379
  27.9 2.3 %collective-permute-done.rest_0_ = bf16[304,512]{1,0:T(8,128)(2,1)} collective-permute-done((bf16[304,512]{1,0:T(8,128)(2,1)S(1)}, bf16[304,512]{1,0:T(8,128)(2,1)}, u32[]{:S(2)}, u32[]{:S(2)}) %collective-permute-start) | collective-permute-done | bytes 311328 | tf_op jit(solution)/shard_map/ppermute | solution.py:460
  30.2 2.5 %shard_map.94 = (bf16[304,512]{1,0:T(8,128)(2,1)}, bf16[304,512]{1,0:T(8,128)(2,1)S(1)}) custom-call(bf16[304,512]{1,0:T(8,128)(2,1)S(1)} %get-tuple-element.60.heads_ref, bf16[304,512]{1,0:T(8,128)(2,1)} %collective-permute-done.rest_0_, bf16[512,4096]{1,0:T(8,128)(2,1)} %weight_ref.5), custom_call_target="tpu_custom_call" | custom-call | flops 20000000000 | tf_op jit(solution)/shard_map/pallas_call | solution.py:440
  32.7 2.7 %collective-permute-start.2 = (bf16[304,512]{1,0:T(8,128)(2,1)S(1)}, bf16[304,512]{1,0:T(8,128)(2,1)S(1)}, u32[]{:S(2)}, u32[]{:S(2)}) collective-permute-start(bf16[304,512]{1,0:T(8,128)(2,1)S(1)} %get-tuple-element.50), channel_id=1, source_target_pairs={{0,7},{1,0},{2,1},{3,2},{4,3},{5,4},{6,5},{7,6},{8,15},{9,8},{10,9... | collective-permute-start | bytes 933896 | tf_op jit(solution)/shard_map/ppermute | solution.py:434
  35.4 2.8 %all-to-all-done.1.asked_ref = bf16[64,4,768]{2,1,0:T(4,128)(2,1)S(1)} async-done(((bf16[64,4,768]{2,1,0:T(4,128)(2,1)}), bf16[64,4,768]{2,1,0:T(4,128)(2,1)S(1)}, u32[]{:S(2)}, u32[]{:S(2)}) %all-to-all-start.1) | async-done | bytes 393248 | tf_op jit(solution)/shard_map/all_to_all | solution.py:379
  38.2 2.2 %shard_map.95 = bf16[64,4,512]{2,1,0:T(4,128)(2,1)} custom-call(s32[8,128]{1,0:T(8,128)S(1)} %get-tuple-element.37.plan_src.plan_ref, bf16[64,4,768]{2,1,0:T(4,128)(2,1)S(1)} %all-to-all-done.1.asked_ref, bf16[26,128,128]{2,1,0:T(8,128)(2,1)S(1)} %get-tuple-element.52.keys_ref, bf16[26,128,128]{2,1,0:T(8,128)(2,1)S(1)} %get-tuple-element.53.values_ref), custom_call_target="tpu_custom_call" | custom-call | tf_op jit(solution)/shard_map/pallas_call | solution.py:465
  40.5 5.5 %all-to-all-start.2 = ((bf16[64,4,512]{2,1,0:T(4,128)(2,1)}), bf16[64,4,512]{2,1,0:T(4,128)(2,1)S(1)}, u32[]{:S(2)}, u32[]{:S(2)}) async-start(bf16[64,4,512]{2,1,0:T(4,128)(2,1)} %shard_map.95), calls=%async_computation.2 | async-start | bytes 524288 | tf_op jit(solution)/shard_map/all_to_all | solution.py:379
  46.0 1.9 %shard_map.96 = (bf16[304,512]{1,0:T(8,128)(2,1)S(1)}, bf16[304,512]{1,0:T(8,128)(2,1)S(1)}) custom-call(bf16[304,512]{1,0:T(8,128)(2,1)S(1)} %get-tuple-element.60.heads_ref, bf16[304,512]{1,0:T(8,128)(2,1)S(1)} %collective-permute-done.1.rest_0_, bf16[304,512]{1,0:T(8,128)(2,1)S(1)} %collective-permute-done.2.rest_1_, bf16[512,4096]{1,0:T(8,128)(2,1)} %weight_ref.5), custom_call_target="tpu_custom_call" | custom-call | flops 20000000000 | tf_op jit(solution)/shard_map/pallas_call | solution.py:440
  48.0 2.7 %collective-permute-start.4 = (bf16[304,512]{1,0:T(8,128)(2,1)S(1)}, bf16[304,512]{1,0:T(8,128)(2,1)S(1)}, u32[]{:S(2)}, u32[]{:S(2)}) collective-permute-start(bf16[304,512]{1,0:T(8,128)(2,1)S(1)} %get-tuple-element.57), channel_id=1, source_target_pairs={{0,7},{1,0},{2,1},{3,2},{4,3},{5,4},{6,5},{7,6},{8,15},{9,8},{10,9... | collective-permute-start | bytes 933896 | tf_op jit(solution)/shard_map/ppermute | solution.py:434
  50.7 4.3 %all-to-all-done.2.back_ref = bf16[64,4,512]{2,1,0:T(4,128)(2,1)S(1)} async-done(((bf16[64,4,512]{2,1,0:T(4,128)(2,1)}), bf16[64,4,512]{2,1,0:T(4,128)(2,1)S(1)}, u32[]{:S(2)}, u32[]{:S(2)}) %all-to-all-start.2) | async-done | bytes 262176 | tf_op jit(solution)/shard_map/all_to_all | solution.py:379
  55.0 3.6 %shard_map.97 = (bf16[8,104,512]{2,1,0:T(8,128)(2,1)}, bf16[512,512]{1,0:T(8,128)(2,1)S(1)}, bf16[512,512]{1,0:T(8,128)(2,1)S(1)}) custom-call(s32[8,128]{1,0:T(8,128)S(1)} %get-tuple-element.43.here_src, bf16[64,4,512]{2,1,0:T(4,128)(2,1)S(1)} %all-to-all-done.2.back_ref, bf16[512,4096]{1,0:T(8,128)(2,1)} %weight_ref.5), custom_call_target="tpu_custom_call" | custom-call | flops 8000000000 | tf_op jit(solution)/shard_map/pallas_call | solution.py:478
  58.6 1.0 %shard_map.98 = (bf16[304,512]{1,0:T(8,128)(2,1)S(1)}, bf16[304,512]{1,0:T(8,128)(2,1)S(1)}) custom-call(bf16[304,512]{1,0:T(8,128)(2,1)S(1)} %get-tuple-element.60.heads_ref, bf16[304,512]{1,0:T(8,128)(2,1)S(1)} %collective-permute-done.3.rest_0_, bf16[304,512]{1,0:T(8,128)(2,1)S(1)} %collective-permute-done.4.rest_1_, bf16[512,4096]{1,0:T(8,128)(2,1)} %weight_ref.5, ...), custom_call_target="tpu_custom_call" | custom-call | flops 20000000000 | tf_op jit(solution)/shard_map/pallas_call | solution.py:440
  59.6 1.1 %collective-permute-start.5 = (bf16[304,512]{1,0:T(8,128)(2,1)S(1)}, bf16[304,512]{1,0:T(8,128)(2,1)S(1)}, u32[]{:S(2)}, u32[]{:S(2)}) collective-permute-start(bf16[304,512]{1,0:T(8,128)(2,1)S(1)} %get-tuple-element.63), channel_id=1, source_target_pairs={{0,1},{1,2},{2,3},{3,4},{4,5},{5,6},{6,7},{7,0},{8,9},{9,10},{10,1... | collective-permute-start | bytes 933896 | tf_op jit(solution)/shard_map/ppermute | solution.py:434
  60.7 1.7 %collective-permute-start.6 = (bf16[304,512]{1,0:T(8,128)(2,1)S(1)}, bf16[304,512]{1,0:T(8,128)(2,1)S(1)}, u32[]{:S(2)}, u32[]{:S(2)}) collective-permute-start(bf16[304,512]{1,0:T(8,128)(2,1)S(1)} %get-tuple-element.64), channel_id=1, source_target_pairs={{0,7},{1,0},{2,1},{3,2},{4,3},{5,4},{6,5},{7,6},{8,15},{9,8},{10,9... | collective-permute-start | bytes 933896 | tf_op jit(solution)/shard_map/ppermute | solution.py:434
  62.4 5.4 %all-to-all-start.3 = ((bf16[8,104,512]{2,1,0:T(8,128)(2,1)}), bf16[8,104,512]{2,1,0:T(8,128)(2,1)S(1)}, u32[]{:S(2)}, u32[]{:S(2)}) async-start(bf16[8,104,512]{2,1,0:T(8,128)(2,1)} %get-tuple-element.66), calls=%async_computation.3 | async-start | bytes 1703936 | tf_op jit(solution)/shard_map/all_to_all | solution.py:379
  67.7 1.8 %collective-permute-done.5.up_ref = bf16[304,512]{1,0:T(8,128)(2,1)S(1)} collective-permute-done((bf16[304,512]{1,0:T(8,128)(2,1)S(1)}, bf16[304,512]{1,0:T(8,128)(2,1)S(1)}, u32[]{:S(2)}, u32[]{:S(2)}) %collective-permute-start.5) | collective-permute-done | bytes 311328 | tf_op jit(solution)/shard_map/ppermute | solution.py:434
  69.5 2.7 %shard_map.99.placed_ref = bf16[128,4,512]{2,1,0:T(4,128)(2,1)S(1)} custom-call(s32[8,128]{1,0:T(8,128)S(1)} %get-tuple-element.37.plan_src.plan_ref, bf16[304,512]{1,0:T(8,128)(2,1)S(1)} %get-tuple-element.60.heads_ref, bf16[304,512]{1,0:T(8,128)(2,1)S(1)} %collective-permute-done.5.up_ref, bf16[304,512]{1,0:T(8,128)(2,1)S(1)} %collective-permute-done.6.down_ref, ...), custom_call_target="tpu_custom_call" | custom-call | flops 40000000000 | tf_op jit(solution)/shard_map/pallas_call | solution.py:501
  72.3 18.4 %all-to-all-done.3.blocks_ref = bf16[8,104,512]{2,1,0:T(8,128)(2,1)S(1)} async-done(((bf16[8,104,512]{2,1,0:T(8,128)(2,1)}), bf16[8,104,512]{2,1,0:T(8,128)(2,1)S(1)}, u32[]{:S(2)}, u32[]{:S(2)}) %all-to-all-start.3) | async-done | bytes 852000 | tf_op jit(solution)/shard_map/all_to_all | solution.py:379
  90.7 1.4 %shard_map.100 = bf16[128,4,512]{2,1,0:T(4,128)(2,1)} custom-call(s32[8,128]{1,0:T(8,128)S(1)} %get-tuple-element.43.here_src, bf16[128,4,512]{2,1,0:T(4,128)(2,1)S(1)} %shard_map.99.placed_ref, bf16[8,104,512]{2,1,0:T(8,128)(2,1)S(1)} %all-to-all-done.3.blocks_ref), custom_call_target="tpu_custom_call" | custom-call | bytes 2097152 | tf_op jit(solution)/shard_map/pallas_call | solution.py:508
  (8 shorter events, 0.2 us)
Async XLA Ops:
  1.5 17.0 %all-to-all-start = ((s32[32,1,128]{2,1,0:T(1,128)}), s32[32,1,128]{2,1,0:T(1,128)S(1)}, u32[]{:S(2)}, u32[]{:S(2)}) async-start(s32[32,1,128]{2,1,0:T(1,128)} %bitcast.4), calls=%async_computation | async-start | bytes 32768 | tf_op jit(solution)/shard_map/all_to_all | solution.py:379
  16.8 13.3 %collective-permute-start = (bf16[304,512]{1,0:T(8,128)(2,1)S(1)}, bf16[304,512]{1,0:T(8,128)(2,1)}, u32[]{:S(2)}, u32[]{:S(2)}) collective-permute-start(bf16[304,512]{1,0:T(8,128)(2,1)S(1)} %get-tuple-element.48), channel_id=1, source_target_pairs={{0,1},{1,2},{2,3},{3,4},{4,5},{5,6},{6,7},{7,0},{8,9},{9,10},{10,1... | collective-permute-start | bytes 933896 | tf_op jit(solution)/shard_map/ppermute | solution.py:460
  20.2 18.0 %all-to-all-start.1 = ((bf16[64,4,768]{2,1,0:T(4,128)(2,1)}), bf16[64,4,768]{2,1,0:T(4,128)(2,1)S(1)}, u32[]{:S(2)}, u32[]{:S(2)}) async-start(bf16[64,4,768]{2,1,0:T(4,128)(2,1)} %get-tuple-element.46), calls=%async_computation.1 | async-start | bytes 786432 | tf_op jit(solution)/shard_map/all_to_all | solution.py:379
  32.7 13.3 %collective-permute-start.1 = (bf16[304,512]{1,0:T(8,128)(2,1)}, bf16[304,512]{1,0:T(8,128)(2,1)S(1)}, u32[]{:S(2)}, u32[]{:S(2)}) collective-permute-start(bf16[304,512]{1,0:T(8,128)(2,1)} %get-tuple-element.49), channel_id=1, source_target_pairs={{0,1},{1,2},{2,3},{3,4},{4,5},{5,6},{6,7},{7,0},{8,9},{9,10},{10,1... | collective-permute-start | bytes 933896 | tf_op jit(solution)/shard_map/ppermute | solution.py:434
  32.7 13.3 %collective-permute-start.2 = (bf16[304,512]{1,0:T(8,128)(2,1)S(1)}, bf16[304,512]{1,0:T(8,128)(2,1)S(1)}, u32[]{:S(2)}, u32[]{:S(2)}) collective-permute-start(bf16[304,512]{1,0:T(8,128)(2,1)S(1)} %get-tuple-element.50), channel_id=1, source_target_pairs={{0,7},{1,0},{2,1},{3,2},{4,3},{5,4},{6,5},{7,6},{8,15},{9,8},{10,9... | collective-permute-start | bytes 933896 | tf_op jit(solution)/shard_map/ppermute | solution.py:434
  40.5 14.5 %all-to-all-start.2 = ((bf16[64,4,512]{2,1,0:T(4,128)(2,1)}), bf16[64,4,512]{2,1,0:T(4,128)(2,1)S(1)}, u32[]{:S(2)}, u32[]{:S(2)}) async-start(bf16[64,4,512]{2,1,0:T(4,128)(2,1)} %shard_map.95), calls=%async_computation.2 | async-start | bytes 524288 | tf_op jit(solution)/shard_map/all_to_all | solution.py:379
  47.9 10.7 %collective-permute-start.3 = (bf16[304,512]{1,0:T(8,128)(2,1)S(1)}, bf16[304,512]{1,0:T(8,128)(2,1)S(1)}, u32[]{:S(2)}, u32[]{:S(2)}) collective-permute-start(bf16[304,512]{1,0:T(8,128)(2,1)S(1)} %get-tuple-element.56), channel_id=1, source_target_pairs={{0,1},{1,2},{2,3},{3,4},{4,5},{5,6},{6,7},{7,0},{8,9},{9,10},{10,1... | collective-permute-start | bytes 933896 | tf_op jit(solution)/shard_map/ppermute | solution.py:434
  48.0 10.6 %collective-permute-start.4 = (bf16[304,512]{1,0:T(8,128)(2,1)S(1)}, bf16[304,512]{1,0:T(8,128)(2,1)S(1)}, u32[]{:S(2)}, u32[]{:S(2)}) collective-permute-start(bf16[304,512]{1,0:T(8,128)(2,1)S(1)} %get-tuple-element.57), channel_id=1, source_target_pairs={{0,7},{1,0},{2,1},{3,2},{4,3},{5,4},{6,5},{7,6},{8,15},{9,8},{10,9... | collective-permute-start | bytes 933896 | tf_op jit(solution)/shard_map/ppermute | solution.py:434
  59.6 9.9 %collective-permute-start.5 = (bf16[304,512]{1,0:T(8,128)(2,1)S(1)}, bf16[304,512]{1,0:T(8,128)(2,1)S(1)}, u32[]{:S(2)}, u32[]{:S(2)}) collective-permute-start(bf16[304,512]{1,0:T(8,128)(2,1)S(1)} %get-tuple-element.63), channel_id=1, source_target_pairs={{0,1},{1,2},{2,3},{3,4},{4,5},{5,6},{6,7},{7,0},{8,9},{9,10},{10,1... | collective-permute-start | bytes 933896 | tf_op jit(solution)/shard_map/ppermute | solution.py:434
  60.7 8.8 %collective-permute-start.6 = (bf16[304,512]{1,0:T(8,128)(2,1)S(1)}, bf16[304,512]{1,0:T(8,128)(2,1)S(1)}, u32[]{:S(2)}, u32[]{:S(2)}) collective-permute-start(bf16[304,512]{1,0:T(8,128)(2,1)S(1)} %get-tuple-element.64), channel_id=1, source_target_pairs={{0,7},{1,0},{2,1},{3,2},{4,3},{5,4},{6,5},{7,6},{8,15},{9,8},{10,9... | collective-permute-start | bytes 933896 | tf_op jit(solution)/shard_map/ppermute | solution.py:434
  62.4 28.3 %all-to-all-start.3 = ((bf16[8,104,512]{2,1,0:T(8,128)(2,1)}), bf16[8,104,512]{2,1,0:T(8,128)(2,1)S(1)}, u32[]{:S(2)}, u32[]{:S(2)}) async-start(bf16[8,104,512]{2,1,0:T(8,128)(2,1)} %get-tuple-element.66), calls=%async_computation.3 | async-start | bytes 1703936 | tf_op jit(solution)/shard_map/all_to_all | solution.py:379
